TPU v7x, 32 devices: a whole 2x2x4 slice. The times are simulated.
32 devices in a mesh: groups: 2 (over y), space: 4 (over z), chan: 4 (over x, core).
Axes of the slice: x: 2, y: 2, z: 4, core: 2. Of those that a mesh axis runs over, the one named last changes fastest.
Arguments:
- inputs: bfloat16 [2, 128, 8, 1024], P('groups', 'chan', 'space'), parts along dimension 0, may hold values from -6 to 6
- pre_act: bfloat16 [2, 128, 8, 1024], P('groups', 'chan', 'space'), parts along dimension 0, may hold values from -6 to 6
- out_grad: bfloat16 [2, 256, 4, 256], P('groups', 'chan', 'space'), parts along dimension 0, may hold values from -12 to 12
- weight_one: bfloat16 [3, 3, 3, 128, 128], P(None, None, None, 'chan'), may hold values from -0.109375 to 0.109375
- weight_two: bfloat16 [3, 3, 3, 128, 256], P(None, None, None, 'chan'), may hold values from -0.109375 to 0.109375
Outputs:
- in_grad: bfloat16 [2, 128, 8, 1024], P('groups', 'chan', 'space'), parts along dimension 0
- filter_one_grad: float32 [6, 3, 3, 128, 128], P('groups', None, None, 'chan'), parts along dimension 0
- filter_two_grad: float32 [6, 3, 3, 128, 256], P('groups', None, None, 'chan'), parts along dimension 0
There are 2 independent parts, one for each index of `groups`. A program takes and returns all parts, laid end to end along the dimension named above; an argument that names none is the same for every part. Nothing has to cross between parts.
All inputs are finite; a program needn't handle non-finite values.
Results may differ from a plain program's by a relative error of at most 0.0049.
Values may be sent and summed in bfloat16 or wider, within the bound.
No kernel may reach another device: no remote copies, remote signals or barrier semaphores. Data moves between devices by JAX's collectives and lax.ppermute only.
A program may use at most 64 MiB of HBM per device.

v0:
```python
import math

import jax
import jax.numpy as jnp
import numpy as np
from jax import lax
from jax.experimental import pallas as pl
from jax.experimental.pallas import tpu as pltpu
from jax.sharding import PartitionSpec as P

leak_slope = 0.3
F32 = jnp.float32
BF16 = jnp.bfloat16
CONTRACT_LAST = (((1,), (1,)), ((), ()))


def moved(value, rows, cols, og):
    if rows == 0 and cols == 0:
        return value
    width = og * og
    value = value.astype(F32)
    lane = lax.broadcasted_iota(jnp.int32, value.shape, 1)
    rolled = pltpu.roll(value, (-(rows * og + cols)) % width, 1)
    keep = None
    for step, place in ((rows, lane // og), (cols, lane % og)):
        if step:
            good = place < og - 1 if step > 0 else place > 0
            keep = good if keep is None else keep & good
    return jnp.where(keep, rolled, 0.0)


def neighbour(parity, step):
    place = parity + step
    return place % 2, place // 2


def leaky(value, gate):
    return jnp.where(gate > 0, value, leak_slope * value)


def split_matrix(og):
    width = og * og
    grid = 2 * og
    cell = np.arange(width)
    row, col = cell // grid, cell % grid
    place = ((row % 2) * 2 + col % 2) * (width // 4) + (row // 2) * og + col // 2
    return (place[:, None] == np.arange(width)[None, :]).astype(np.float32)


def split_kernel(og, planes, chans, x_ref, h_ref, e_ref, xp_ref, hp_ref):
    width = og * og
    part = width // 4
    matrix = e_ref[...]
    for source, target in ((x_ref, xp_ref), (h_ref, hp_ref)):
        value = source[...]
        stacked = jnp.concatenate([value[:, i * width : (i + 1) * width] for i in range(4 * planes)], axis=0)
        sorted_cells = jnp.dot(stacked, matrix, preferred_element_type=F32)
        for plane in range(planes):
            for parity in range(4):
                pieces = [
                    sorted_cells[(plane * 4 + i) * chans : (plane * 4 + i + 1) * chans, parity * part : (parity + 1) * part]
                    for i in range(4)
                ]
                at = (plane * 4 + parity) * chans
                target[at : at + chans, :] = jnp.concatenate(pieces, axis=1).astype(BF16)


def transposed_taps(taps, chans, og):
    def tap(row, col):
        at = (row * 3 + col) * chans
        return taps[at : at + chans]

    return [
        tap(1, 1),
        tap(1, 2) + moved(tap(1, 0), 0, 1, og),
        tap(2, 1) + moved(tap(0, 1), 1, 0, og),
        tap(2, 2) + moved(tap(0, 2), 1, 0, og) + moved(tap(2, 0), 0, 1, og) + moved(tap(0, 0), 1, 1, og),
    ]


def plane_grad(w_ref, near, after, gates, chans, og, out_ref, at, live):
    block = 9 * chans
    if after is None:
        taps = jnp.dot(w_ref[block : 2 * block, :], near, preferred_element_type=F32)
    else:
        taps = jnp.dot(w_ref[2 * block : 3 * block, :], near, preferred_element_type=F32)
        taps = taps + jnp.dot(w_ref[0:block, :], after, preferred_element_type=F32)
    for parity, value in enumerate(transposed_taps(taps, chans, og)):
        gate = gates[parity * chans : (parity + 1) * chans].astype(F32)
        value = leaky(value, gate)
        if live is not None:
            value = jnp.where(live, value, 0.0)
        out_ref[at + parity * chans : at + (parity + 1) * chans, :] = value.astype(BF16)


def own_grad_kernel(og, chans, count, w_ref, g_ref, gn_ref, hp_ref, p_ref):
    s = lax.axis_index("space")
    half = 4 * chans
    here = g_ref[...]
    after = jnp.where(s < count - 1, gn_ref[...].astype(F32), 0.0).astype(BF16)
    plane_grad(w_ref, here, None, hp_ref[0:half, :], chans, og, p_ref, 0, None)
    plane_grad(w_ref, here, after, hp_ref[half : 2 * half, :], chans, og, p_ref, half, None)


def rim_grad_kernel(og, chans, count, w_ref, gp_ref, g_ref, gn_ref, hp_prev_ref, hp_next_ref, p_ref):
    s = lax.axis_index("space")
    half = 4 * chans
    plane_grad(w_ref, gp_ref[...], g_ref[...], hp_prev_ref[half : 2 * half, :], chans, og, p_ref, 0, s > 0)
    plane_grad(w_ref, gn_ref[...], None, hp_next_ref[0:half, :], chans, og, p_ref, half, s < count - 1)


def window_rows(blocks, parity, og):
    rows = []
    for row_tap in range(3):
        row_parity, row_move = neighbour(parity // 2, row_tap - 1)
        for col_tap in range(3):
            col_parity, col_move = neighbour(parity % 2, col_tap - 1)
            rows.append(blocks[(row_parity * 2 + col_parity, row_move, col_move)])
    return jnp.concatenate(rows, axis=0)


def moved_blocks(plane, chans, og):
    result = {}
    for parity in range(4):
        value = plane[parity * chans : (parity + 1) * chans]
        for row_move in (0, -1 if parity // 2 else 1):
            for col_move in (0, -1 if parity % 2 else 1):
                result[parity, row_move, col_move] = moved(value, row_move, col_move, og).astype(BF16)
    return result


def filter_one_kernel(og, chans, count, rows, a_ref, xprev_ref, xp_ref, xnext_ref, own_ref, *rest):
    outs, (p_scr, x_scr, f_scr) = rest[: count - 1], rest[count - 1 :]
    s = lax.axis_index("space")
    width = og * og
    shards = a_ref.shape[0]
    all_chans = shards * chans
    half = 4 * chans
    block = 9 * chans
    for plane in range(2):
        for parity in range(4):
            for j in range(shards):
                at = plane * all_chans + j * chans
                p_scr[at : at + chans, parity * width : (parity + 1) * width] = a_ref[
                    j, (plane * 4 + parity) * chans : (plane * 4 + parity + 1) * chans, :
                ]
    planes = (xprev_ref[...], xp_ref[0:half, :], xp_ref[half : 2 * half, :], xnext_ref[...])
    ends = ((0, all_chans), (0, 2 * all_chans), (0, 2 * all_chans), (all_chans, 2 * all_chans))
    products = []
    for index, plane in enumerate(planes):
        blocks = moved_blocks(plane, chans, og)
        for parity in range(4):
            x_scr[index, :, parity * width : (parity + 1) * width] = window_rows(blocks, parity, og)
        first, last = ends[index]
        products.append(
            lax.dot_general(x_scr[index], p_scr[first:last, :], CONTRACT_LAST, preferred_element_type=F32)
        )
    before, even, odd, after = products
    f_scr[0:block, :] = before + even[:, all_chans:]
    f_scr[block : 2 * block, :] = even[:, :all_chans] + odd[:, all_chans:]
    f_scr[2 * block : 3 * block, :] = odd[:, :all_chans] + after
    if count * rows > 3 * block:
        f_scr[3 * block :, :] = jnp.zeros((count * rows - 3 * block, all_chans), F32)

    def piece(step):
        at = pl.multiple_of(lax.rem(s + step, count) * rows, 16)
        return f_scr[pl.ds(at, rows), :]

    own_ref[...] = piece(0)
    for step, out in enumerate(outs):
        out[...] = piece(step + 1).astype(BF16)


def in_grad_kernel(og, chans, w_ref, a_ref, r_ref, e_ref, out_ref, p_scr):
    width = og * og
    part = width // 4
    shards = a_ref.shape[0]
    all_chans = shards * chans
    block = 9 * chans
    for index in range(4):
        source, first = (r_ref, index // 3) if index in (0, 3) else (a_ref, index - 1)
        for parity in range(4):
            for j in range(shards):
                at = index * all_chans + j * chans
                p_scr[at : at + chans, parity * width : (parity + 1) * width] = source[
                    j, (first * 4 + parity) * chans : (first * 4 + parity + 1) * chans, :
                ]
    weights = jnp.concatenate([w_ref[depth * block : (depth + 1) * block, :] for depth in (2, 1, 0)], axis=1)
    stacked = []
    for plane in range(2):
        taps = jnp.dot(
            weights, p_scr[plane * all_chans : (plane + 3) * all_chans, :], preferred_element_type=F32
        )
        sums = []
        for parity in range(4):
            terms = {}
            for row_tap in range(3):
                row_parity, row_move = neighbour(parity // 2, 1 - row_tap)
                for col_tap in range(3):
                    col_parity, col_move = neighbour(parity % 2, 1 - col_tap)
                    at = (row_tap * 3 + col_tap) * chans
                    lane = (row_parity * 2 + col_parity) * width
                    term = taps[at : at + chans, lane : lane + width]
                    key = (row_move, col_move)
                    terms[key] = term if key not in terms else terms[key] + term
            total = None
            for (row_move, col_move), term in terms.items():
                term = moved(term, row_move, col_move, og)
                total = term if total is None else total + term
            sums.append(total)
        for i in range(4):
            stacked.append(
                jnp.concatenate([value[:, i * part : (i + 1) * part] for value in sums], axis=1).astype(BF16)
            )
    joined = lax.dot_general(jnp.concatenate(stacked, axis=0), e_ref[...], CONTRACT_LAST, preferred_element_type=F32)
    for i in range(8):
        out_ref[:, i * width : (i + 1) * width] = joined[i * chans : (i + 1) * chans].astype(BF16)


def filter_two_kernel(og, chans, count, scale, *refs):
    grads, gates, out_ref = refs[:count], refs[count : 2 * count], refs[2 * count]
    g_scr, even_scr, odd_scr = refs[2 * count + 1 :]
    s = lax.axis_index("space")
    half = 4 * chans
    block = 9 * chans
    for step in range(count):
        at = lax.rem(s + count - step, count)
        g_scr[at] = grads[step][...]
        value = gates[step][...].astype(F32)
        act = leaky(value, value).astype(BF16)
        for plane, target in enumerate((even_scr, odd_scr)):
            blocks = moved_blocks(act[plane * half : (plane + 1) * half], chans, og)
            target[at] = window_rows(blocks, 0, og)
    totals = [jnp.zeros((block, g_scr.shape[1]), F32) for _ in range(3)]
    for at in range(count):
        sources = (odd_scr.at[at - 1] if at else None, even_scr.at[at], odd_scr.at[at])
        for depth, source in enumerate(sources):
            if source is not None:
                totals[depth] = totals[depth] + lax.dot_general(
                    source[...], g_scr[at], CONTRACT_LAST, preferred_element_type=F32
                )
    for depth in range(3):
        out_ref[depth * block : (depth + 1) * block, :] = totals[depth] * scale


def place_kernel(count, rows, *refs):
    pieces, out_ref, scr = refs[:count], refs[count], refs[count + 1]
    s = lax.axis_index("space")
    for step, piece in enumerate(pieces):
        at = pl.multiple_of(lax.rem(s + count - step, count) * rows, 16)
        scr[pl.ds(at, rows), :] = piece[...].astype(F32)
    out_ref[...] = scr[0 : out_ref.shape[0], :]


def local_call(kernel, out_shape, scratch, flops, *operands):
    total = sum(value.size * value.dtype.itemsize for value in operands)
    total += sum(math.prod(o.shape) * o.dtype.itemsize for o in jax.tree.leaves(out_shape))
    return pl.pallas_call(
        kernel,
        out_shape=out_shape,
        in_specs=[pl.BlockSpec(memory_space=pltpu.VMEM)] * len(operands),
        out_specs=jax.tree.map(lambda _: pl.BlockSpec(memory_space=pltpu.VMEM), out_shape),
        scratch_shapes=scratch,
        cost_estimate=pl.CostEstimate(flops=flops, bytes_accessed=total, transcendentals=0),
        compiler_params=pltpu.CompilerParams(vmem_limit_bytes=50 * 1024 * 1024),
    )(*operands)


def ring(value, step):
    count = lax.axis_size("space")
    return lax.ppermute(value, "space", [(i, (i + step) % count) for i in range(count)])


def shards(inputs, pre_act, out_grad, weight_one, weight_two):
    samples, chans, planes, cells = inputs.shape
    count = lax.axis_size("space")
    og = math.isqrt(out_grad.shape[3])
    width = og * og
    half = 4 * chans
    block = 9 * chans
    all_chans = weight_one.shape[4]
    all_out = weight_two.shape[4]
    w1 = weight_one.reshape(3 * block, all_chans)
    w2 = weight_two.reshape(3 * block, all_out)
    matrix = jnp.asarray(split_matrix(og), BF16)
    shape = jax.ShapeDtypeStruct

    grads = lax.all_gather(out_grad.reshape(-1, width), "chan", axis=0, tiled=True)
    xp, hp = local_call(
        lambda *r: split_kernel(og, planes, chans, *r),
        [shape((planes * half, width), BF16)] * 2,
        [],
        2 * 2 * planes * half * width * width,
        inputs.reshape(chans, planes * cells),
        pre_act.reshape(chans, planes * cells),
        matrix,
    )
    grads_next = ring(grads, count - 1)
    up = [(i, i + 1) for i in range(count - 1)]
    down = [(i + 1, i) for i in range(count - 1)]
    x_prev = lax.ppermute(xp[half:], "space", up)
    x_next = lax.ppermute(xp[:half], "space", down)

    p_own = local_call(
        lambda *r: own_grad_kernel(og, chans, count, *r),
        shape((2 * half, width), BF16),
        [],
        2 * 3 * block * all_out * width,
        w2,
        grads,
        grads_next,
        hp,
    )
    a_own = lax.all_gather(p_own, "chan", axis=0)

    all_grads = [grads] + [ring(grads, step) for step in range(1, count - 1)] + [grads_next]
    all_hp = [hp] + [ring(hp, step) for step in range(1, count)]

    rows = -(-3 * block // (16 * count)) * 16
    pieces = local_call(
        lambda *r: filter_one_kernel(og, chans, count, rows, *r),
        [shape((rows, all_chans), F32)] + [shape((rows, all_chans), BF16)] * (count - 1),
        [
            pltpu.VMEM((2 * all_chans, 4 * width), BF16),
            pltpu.VMEM((4, block, 4 * width), BF16),
            pltpu.VMEM((count * rows, all_chans), F32),
        ],
        2 * 6 * block * all_chans * cells,
        a_own,
        x_prev,
        xp,
        x_next,
    )
    total = pieces[0]
    for step in range(1, count):
        total = total + ring(pieces[step], step).astype(F32)
    scale_one = 1.0 / math.sqrt(samples * planes * count * cells)
    scale_two = 1.0 / math.sqrt(samples * out_grad.shape[2] * count * width)
    total = (total * scale_one).astype(BF16)

    p_rim = local_call(
        lambda *r: rim_grad_kernel(og, chans, count, *r),
        shape((2 * half, width), BF16),
        [],
        2 * 3 * block * all_out * width,
        w2,
        all_grads[1],
        grads,
        grads_next,
        all_hp[1],
        all_hp[count - 1],
    )
    a_rim = lax.all_gather(p_rim, "chan", axis=0)
    in_grad = local_call(
        lambda *r: in_grad_kernel(og, chans, *r),
        shape((chans, planes * cells), BF16),
        [pltpu.VMEM((4 * all_chans, 4 * width), BF16)],
        2 * 6 * block * all_chans * cells,
        w1,
        a_own,
        a_rim,
        matrix,
    )
    filter_two = local_call(
        lambda *r: filter_two_kernel(og, chans, count, scale_two, *r),
        shape((3 * block, all_out), F32),
        [
            pltpu.VMEM((count, all_out, width), BF16),
            pltpu.VMEM((count, block, width), BF16),
            pltpu.VMEM((count, block, width), BF16),
        ],
        2 * 3 * count * block * all_out * width,
        *all_grads,
        *all_hp,
    )
    filter_one = local_call(
        lambda *r: place_kernel(count, rows, *r),
        shape((3 * block, all_chans), F32),
        [pltpu.VMEM((count * rows, all_chans), F32)],
        0,
        total,
        *[ring(total, step) for step in range(1, count)],
    )
    return (
        in_grad.reshape(samples, chans, planes, cells),
        filter_one.reshape(3, 3, 3, chans, all_chans),
        filter_two.reshape(3, 3, 3, chans, all_out),
    )


def solution(mesh):
    in_specs = (
        P("groups", "chan", "space", None),
        P("groups", "chan", "space", None),
        P("groups", "chan", "space", None),
        P(None, None, None, "chan", None),
        P(None, None, None, "chan", None),
    )
    out_specs = (
        P("groups", "chan", "space", None),
        P("groups", None, None, "chan", None),
        P("groups", None, None, "chan", None),
    )
    return jax.shard_map(shards, mesh=mesh, in_specs=in_specs, out_specs=out_specs, check_vma=False)
```

profile of v0, /device:TPU:0, one launch (start us, length us, event | category | flops | bytes accessed | tf_op | source)
XLA Modules:
  0.0 57.4 jit_solution(16990804306196411218)
XLA Ops:
  0.6 6.8 %all-gather = bf16[1,256,1,256]{3,1,2,0:T(8,128)(2,1)S(1)} all-gather(bf16[1,64,1,256]{3,1,2,0:T(8,128)(2,1)} %param.8), channel_id=2, replica_groups=mesh['groups'=2,'space'=4,'chan'=4] {'chan'}, dimensions={1}, use_global_device_ids=true | all-gather | bytes 163840 | tf_op jit(solution)/shard_map/all_gather | solution.py:288
  7.5 2.0 %collective-permute-start.1 = (bf16[256,256]{1,0:T(8,128)(2,1)S(1)}, bf16[256,256]{1,0:T(8,128)(2,1)S(1)}, u32[]{:S(2)}, u32[]{:S(2)}) collective-permute-start(bf16[256,256]{1,0:T(8,128)(2,1)S(1)} %bitcast.13), channel_id=1, source_target_pairs={{0,4},{4,8},{8,12},{12,0},{1,5},{5,9},{9,13},{13,1},{2,6},{6,10},{... | collective-permute-start | bytes 393224 | tf_op jit(solution)/shard_map/ppermute | solution.py:271
  9.4 2.0 %collective-permute-start = (bf16[256,256]{1,0:T(8,128)(2,1)S(1)}, bf16[256,256]{1,0:T(8,128)(2,1)S(1)}, u32[]{:S(2)}, u32[]{:S(2)}) collective-permute-start(bf16[256,256]{1,0:T(8,128)(2,1)S(1)} %bitcast.14), channel_id=1, source_target_pairs={{0,12},{4,0},{8,4},{12,8},{1,13},{5,1},{9,5},{13,9},{2,14},{6,2},{... | collective-permute-start | bytes 393224 | tf_op jit(solution)/shard_map/ppermute | solution.py:271
  11.5 0.9 %copy-done.4 = bf16[1,32,2,1024]{3,2,1,0:T(2,128)(2,1)S(1)} copy-done((bf16[1,32,2,1024]{3,2,1,0:T(2,128)(2,1)S(1)}, bf16[1,32,2,1024]{3,2,1,0:T(2,128)(2,1)}, u32[]{:S(2)}) %copy-start.4) | copy-done | bytes 131096
  12.7 2.1 %collective-permute-start.3 = (bf16[256,256]{1,0:T(8,128)(2,1)S(1)}, bf16[256,256]{1,0:T(8,128)(2,1)S(1)}, u32[]{:S(2)}, u32[]{:S(2)}) collective-permute-start(bf16[256,256]{1,0:T(8,128)(2,1)S(1)} %get-tuple-element.9.r_3_.r_4_), channel_id=1, source_target_pairs={{0,12},{4,0},{8,4},{12,8},{1,13},{5,1},{9,5},{13,9},{2,14},{6,2},{... | collective-permute-start | bytes 393224 | tf_op jit(solution)/shard_map/ppermute | solution.py:271
  14.8 1.3 %collective-permute-start.5 = (bf16[128,256]{1,0:T(8,128)(2,1)S(1)}, bf16[128,256]{1,0:T(8,128)(2,1)S(1)}, u32[]{:S(2)}, u32[]{:S(2)}) collective-permute-start(bf16[128,256]{1,0:T(8,128)(2,1)S(1)} %get-tuple-element.15), channel_id=1, source_target_pairs={{4,0},{8,4},{12,8},{5,1},{9,5},{13,9},{6,2},{10,6},{14,10},{7,3},{... | collective-permute-start | bytes 196616 | tf_op jit(solution)/shard_map/ppermute | solution.py:302
  16.1 2.2 %collective-permute-done.r_2_.r_3_ = bf16[256,256]{1,0:T(8,128)(2,1)S(1)} collective-permute-done((bf16[256,256]{1,0:T(8,128)(2,1)S(1)}, bf16[256,256]{1,0:T(8,128)(2,1)S(1)}, u32[]{:S(2)}, u32[]{:S(2)}) %collective-permute-start) | collective-permute-done | bytes 131104 | tf_op jit(solution)/shard_map/ppermute | solution.py:271
  18.4 2.5 %collective-permute-start.4 = (bf16[128,256]{1,0:T(8,128)(2,1)S(1)}, bf16[128,256]{1,0:T(8,128)(2,1)S(1)}, u32[]{:S(2)}, u32[]{:S(2)}) collective-permute-start(bf16[128,256]{1,0:T(8,128)(2,1)S(1)} %get-tuple-element.16), channel_id=1, source_target_pairs={{0,4},{4,8},{8,12},{1,5},{5,9},{9,13},{2,6},{6,10},{10,14},{3,7},{... | collective-permute-start | bytes 196616 | tf_op jit(solution)/shard_map/ppermute | solution.py:301
  21.2 7.3 %all-gather.1 = bf16[1024,256]{1,0:T(8,128)(2,1)S(1)} all-gather(bf16[256,256]{1,0:T(8,128)(2,1)S(1)} %shard_map.86), channel_id=3, replica_groups=mesh['groups'=2,'space'=4,'chan'=4] {'chan'}, dimensions={0}, use_global_device_ids=true | all-gather | bytes 655360 | tf_op jit(solution)/shard_map/all_gather | solution.py:314
  28.5 2.1 %collective-permute-start.12 = (bf16[256,256]{1,0:T(8,128)(2,1)S(1)}, bf16[256,256]{1,0:T(8,128)(2,1)S(1)}, u32[]{:S(2)}, u32[]{:S(2)}) collective-permute-start(bf16[256,256]{1,0:T(8,128)(2,1)S(1)} %bitcast.16), channel_id=1, source_target_pairs={{0,8},{4,12},{8,0},{12,4},{1,9},{5,13},{9,1},{13,5},{2,10},{6,14},... | collective-permute-start | bytes 393224 | tf_op jit(solution)/shard_map/ppermute | solution.py:271
  30.5 0.9 %collective-permute-start.13 = (bf16[256,256]{1,0:T(8,128)(2,1)S(1)}, bf16[256,256]{1,0:T(8,128)(2,1)S(1)}, u32[]{:S(2)}, u32[]{:S(2)}) collective-permute-start(bf16[256,256]{1,0:T(8,128)(2,1)S(1)} %get-tuple-element.9.r_3_.r_4_), channel_id=1, source_target_pairs={{0,8},{4,12},{8,0},{12,4},{1,9},{5,13},{9,1},{13,5},{2,10},{6,14},... | collective-permute-start | bytes 393224 | tf_op jit(solution)/shard_map/ppermute | solution.py:271
  31.4 0.9 %shard_map.89 = (f32[224,128]{1,0:T(8,128)S(1)}, bf16[224,128]{1,0:T(8,128)(2,1)S(1)}, bf16[224,128]{1,0:T(8,128)(2,1)S(1)}, bf16[224,128]{1,0:T(8,128)(2,1)S(1)}) custom-call(bf16[4,256,256]{2,1,0:T(8,128)(2,1)S(1)} %bitcast.21, bf16[128,256]{1,0:T(8,128)(2,1)S(1)} %collective-permute-done.4.r_1_, bf16[256,256]{1,0:T(8,128)(2,1)S(1)} %get-tuple-element.10.r_2_, ...), custom_call_target="tpu_custom_call" | custom-call | flops 452984832 | bytes 1073152 | tf_op jit(solution)/shard_map/pallas_call | solution.py:258
  32.3 1.0 %collective-permute-start.6 = (bf16[224,128]{1,0:T(8,128)(2,1)S(1)}, bf16[224,128]{1,0:T(8,128)(2,1)S(1)}, u32[]{:S(2)}, u32[]{:S(2)}) collective-permute-start(bf16[224,128]{1,0:T(8,128)(2,1)S(1)} %get-tuple-element.12), channel_id=1, source_target_pairs={{0,4},{4,8},{8,12},{12,0},{1,5},{5,9},{9,13},{13,1},{2,6},{6,10},{... | collective-permute-start | bytes 172040 | tf_op jit(solution)/shard_map/ppermute | solution.py:271
  33.3 1.2 %collective-permute-start.7 = (bf16[224,128]{1,0:T(8,128)(2,1)S(1)}, bf16[224,128]{1,0:T(8,128)(2,1)S(1)}, u32[]{:S(2)}, u32[]{:S(2)}) collective-permute-start(bf16[224,128]{1,0:T(8,128)(2,1)S(1)} %get-tuple-element.13), channel_id=1, source_target_pairs={{0,8},{4,12},{8,0},{12,4},{1,9},{5,13},{9,1},{13,5},{2,10},{6,14},... | collective-permute-start | bytes 172040 | tf_op jit(solution)/shard_map/ppermute | solution.py:271
  34.5 2.8 %collective-permute-start.8 = (bf16[224,128]{1,0:T(8,128)(2,1)S(1)}, bf16[224,128]{1,0:T(8,128)(2,1)S(1)}, u32[]{:S(2)}, u32[]{:S(2)}) collective-permute-start(bf16[224,128]{1,0:T(8,128)(2,1)S(1)} %get-tuple-element.14), channel_id=1, source_target_pairs={{0,12},{4,0},{8,4},{12,8},{1,13},{5,1},{9,5},{13,9},{2,14},{6,2},{... | collective-permute-start | bytes 172040 | tf_op jit(solution)/shard_map/ppermute | solution.py:271
  37.7 6.5 %all-gather.2 = bf16[1024,256]{1,0:T(8,128)(2,1)S(1)} all-gather(bf16[256,256]{1,0:T(8,128)(2,1)S(1)} %shard_map.87), channel_id=4, replica_groups=mesh['groups'=2,'space'=4,'chan'=4] {'chan'}, dimensions={0}, use_global_device_ids=true | all-gather | bytes 655360 | tf_op jit(solution)/shard_map/all_gather | solution.py:353
  44.2 3.4 %collective-permute-done.7 = bf16[224,128]{1,0:T(8,128)(2,1)S(1)} collective-permute-done((bf16[224,128]{1,0:T(8,128)(2,1)S(1)}, bf16[224,128]{1,0:T(8,128)(2,1)S(1)}, u32[]{:S(2)}, u32[]{:S(2)}) %collective-permute-start.7) | collective-permute-done | bytes 57376 | tf_op jit(solution)/shard_map/ppermute | solution.py:271
  47.7 1.8 %collective-permute-start.11 = (bf16[224,128]{1,0:T(8,128)(2,1)S(1)}, bf16[224,128]{1,0:T(8,128)(2,1)S(1)}, u32[]{:S(2)}, u32[]{:S(2)}) collective-permute-start(bf16[224,128]{1,0:T(8,128)(2,1)S(1)} %multiply_convert_fusion.r_0_), channel_id=1, source_target_pairs={{0,12},{4,0},{8,4},{12,8},{1,13},{5,1},{9,5},{13,9},{2,14},{6,2},{... | collective-permute-start | bytes 172040 | tf_op jit(solution)/shard_map/ppermute | solution.py:271
  49.4 1.1 %collective-permute-start.10 = (bf16[224,128]{1,0:T(8,128)(2,1)S(1)}, bf16[224,128]{1,0:T(8,128)(2,1)S(1)}, u32[]{:S(2)}, u32[]{:S(2)}) collective-permute-start(bf16[224,128]{1,0:T(8,128)(2,1)S(1)} %multiply_convert_fusion.r_0_), channel_id=1, source_target_pairs={{0,8},{4,12},{8,0},{12,4},{1,9},{5,13},{9,1},{13,5},{2,10},{6,14},... | collective-permute-start | bytes 172040 | tf_op jit(solution)/shard_map/ppermute | solution.py:271
  50.6 1.1 %shard_map.88 = bf16[32,2048]{1,0:T(8,128)(2,1)S(1)} custom-call(bf16[864,128]{1,0:T(8,128)(2,1)S(1)} %bitcast.26, bf16[4,256,256]{2,1,0:T(8,128)(2,1)S(1)} %bitcast.22, bf16[4,256,256]{2,1,0:T(8,128)(2,1)S(1)} %bitcast.23, bf16[256,256]{1,0:T(8,128)(2,1)S(1)} %copy-done.1), custom_call_target="tpu_custom_call" | custom-call | flops 452984832 | bytes 1531904 | tf_op jit(solution)/shard_map/pallas_call | solution.py:258
  52.4 1.8 %shard_map.91 = f32[864,256]{1,0:T(8,128)} custom-call(bf16[256,256]{1,0:T(8,128)(2,1)S(1)} %bitcast.18, bf16[256,256]{1,0:T(8,128)(2,1)S(1)} %collective-permute-done.1.r_1_, bf16[256,256]{1,0:T(8,128)(2,1)S(1)} %collective-permute-done.12.r_2_, bf16[256,256]{1,0:T(8,128)(2,1)S(1)} %collective-permute-done.r_2_.r_3_, ...), custom_call_target="tpu_custom_call" | custom-call | flops 452984832 | bytes 1933312 | tf_op jit(solution)/shard_map/pallas_call | solution.py:258
  54.2 1.3 %collective-permute-done.10.r_2_ = bf16[224,128]{1,0:T(8,128)(2,1)S(1)} collective-permute-done((bf16[224,128]{1,0:T(8,128)(2,1)S(1)}, bf16[224,128]{1,0:T(8,128)(2,1)S(1)}, u32[]{:S(2)}, u32[]{:S(2)}) %collective-permute-start.10) | collective-permute-done | bytes 57376 | tf_op jit(solution)/shard_map/ppermute | solution.py:271
  55.5 1.0 %collective-permute-done.9.r_1_ = bf16[224,128]{1,0:T(8,128)(2,1)S(1)} collective-permute-done((bf16[224,128]{1,0:T(8,128)(2,1)S(1)}, bf16[224,128]{1,0:T(8,128)(2,1)S(1)}, u32[]{:S(2)}, u32[]{:S(2)}) %collective-permute-start.9) | collective-permute-done | bytes 57376 | tf_op jit(solution)/shard_map/ppermute | solution.py:271
  56.6 0.8 %shard_map.90 = f32[864,128]{1,0:T(8,128)} custom-call(bf16[224,128]{1,0:T(8,128)(2,1)S(1)} %multiply_convert_fusion.r_0_, bf16[224,128]{1,0:T(8,128)(2,1)S(1)} %collective-permute-done.9.r_1_, bf16[224,128]{1,0:T(8,128)(2,1)S(1)} %collective-permute-done.10.r_2_, bf16[224,128]{1,0:T(8,128)(2,1)S(1)} %collective-permute-done.11.r_3_), custom_call_target="tpu_custom_call" | custom-call | bytes 671744 | tf_op jit(solution)/shard_map/pallas_call | solution.py:258
  (29 shorter events, 1.9 us)
Async XLA Ops:
  0.6 10.8 %copy-start.3 = (bf16[1,32,2,1024]{3,2,1,0:T(2,128)(2,1)S(1)}, bf16[1,32,2,1024]{3,2,1,0:T(2,128)(2,1)}, u32[]{:S(2)}) copy-start(bf16[1,32,2,1024]{3,2,1,0:T(2,128)(2,1)} %param.6) | copy-start | bytes 393220
  7.5 24.8 %collective-permute-start.1 = (bf16[256,256]{1,0:T(8,128)(2,1)S(1)}, bf16[256,256]{1,0:T(8,128)(2,1)S(1)}, u32[]{:S(2)}, u32[]{:S(2)}) collective-permute-start(bf16[256,256]{1,0:T(8,128)(2,1)S(1)} %bitcast.13), channel_id=1, source_target_pairs={{0,4},{4,8},{8,12},{12,0},{1,5},{5,9},{9,13},{13,1},{2,6},{6,10},{... | collective-permute-start | bytes 393224 | tf_op jit(solution)/shard_map/ppermute | solution.py:271
  9.4 8.9 %collective-permute-start = (bf16[256,256]{1,0:T(8,128)(2,1)S(1)}, bf16[256,256]{1,0:T(8,128)(2,1)S(1)}, u32[]{:S(2)}, u32[]{:S(2)}) collective-permute-start(bf16[256,256]{1,0:T(8,128)(2,1)S(1)} %bitcast.14), channel_id=1, source_target_pairs={{0,12},{4,0},{8,4},{12,8},{1,13},{5,1},{9,5},{13,9},{2,14},{6,2},{... | collective-permute-start | bytes 393224 | tf_op jit(solution)/shard_map/ppermute | solution.py:271
  11.5 0.9 %copy-start.4 = (bf16[1,32,2,1024]{3,2,1,0:T(2,128)(2,1)S(1)}, bf16[1,32,2,1024]{3,2,1,0:T(2,128)(2,1)}, u32[]{:S(2)}) copy-start(bf16[1,32,2,1024]{3,2,1,0:T(2,128)(2,1)} %param.7) | copy-start | bytes 393220
  11.5 1.0 %copy-start.1 = (bf16[256,256]{1,0:T(8,128)(2,1)S(1)}, bf16[256,256]{1,0:T(8,128)(2,1)}, u32[]{:S(2)}) copy-start(bf16[256,256]{1,0:T(8,128)(2,1)} %constant.4.clone.r_2_.r_3_) | copy-start | bytes 393220
  12.4 8.5 %copy-start = (bf16[3,3,3,32,256]{4,3,2,1,0:T(8,128)(2,1)S(1)}, bf16[3,3,3,32,256]{4,3,2,1,0:T(8,128)(2,1)}, u32[]{:S(2)}) copy-start(bf16[3,3,3,32,256]{4,3,2,1,0:T(8,128)(2,1)} %param.10) | copy-start | bytes 1327108
  12.7 20.5 %collective-permute-start.3 = (bf16[256,256]{1,0:T(8,128)(2,1)S(1)}, bf16[256,256]{1,0:T(8,128)(2,1)S(1)}, u32[]{:S(2)}, u32[]{:S(2)}) collective-permute-start(bf16[256,256]{1,0:T(8,128)(2,1)S(1)} %get-tuple-element.9.r_3_.r_4_), channel_id=1, source_target_pairs={{0,12},{4,0},{8,4},{12,8},{1,13},{5,1},{9,5},{13,9},{2,14},{6,2},{... | collective-permute-start | bytes 393224 | tf_op jit(solution)/shard_map/ppermute | solution.py:271
  14.8 19.7 %collective-permute-start.2 = (bf16[256,256]{1,0:T(8,128)(2,1)S(1)}, bf16[256,256]{1,0:T(8,128)(2,1)S(1)}, u32[]{:S(2)}, u32[]{:S(2)}) collective-permute-start(bf16[256,256]{1,0:T(8,128)(2,1)S(1)} %get-tuple-element.9.r_3_.r_4_), channel_id=1, source_target_pairs={{0,4},{4,8},{8,12},{12,0},{1,5},{5,9},{9,13},{13,1},{2,6},{6,10},{... | collective-permute-start | bytes 393224 | tf_op jit(solution)/shard_map/ppermute | solution.py:271
  14.8 13.6 %collective-permute-start.5 = (bf16[128,256]{1,0:T(8,128)(2,1)S(1)}, bf16[128,256]{1,0:T(8,128)(2,1)S(1)}, u32[]{:S(2)}, u32[]{:S(2)}) collective-permute-start(bf16[128,256]{1,0:T(8,128)(2,1)S(1)} %get-tuple-element.15), channel_id=1, source_target_pairs={{4,0},{8,4},{12,8},{5,1},{9,5},{13,9},{6,2},{10,6},{14,10},{7,3},{... | collective-permute-start | bytes 196616 | tf_op jit(solution)/shard_map/ppermute | solution.py:302
  18.4 12.2 %collective-permute-start.4 = (bf16[128,256]{1,0:T(8,128)(2,1)S(1)}, bf16[128,256]{1,0:T(8,128)(2,1)S(1)}, u32[]{:S(2)}, u32[]{:S(2)}) collective-permute-start(bf16[128,256]{1,0:T(8,128)(2,1)S(1)} %get-tuple-element.16), channel_id=1, source_target_pairs={{0,4},{4,8},{8,12},{1,5},{5,9},{9,13},{2,6},{6,10},{10,14},{3,7},{... | collective-permute-start | bytes 196616 | tf_op jit(solution)/shard_map/ppermute | solution.py:301
  28.5 23.9 %collective-permute-start.12 = (bf16[256,256]{1,0:T(8,128)(2,1)S(1)}, bf16[256,256]{1,0:T(8,128)(2,1)S(1)}, u32[]{:S(2)}, u32[]{:S(2)}) collective-permute-start(bf16[256,256]{1,0:T(8,128)(2,1)S(1)} %bitcast.16), channel_id=1, source_target_pairs={{0,8},{4,12},{8,0},{12,4},{1,9},{5,13},{9,1},{13,5},{2,10},{6,14},... | collective-permute-start | bytes 393224 | tf_op jit(solution)/shard_map/ppermute | solution.py:271
  30.5 21.9 %collective-permute-start.13 = (bf16[256,256]{1,0:T(8,128)(2,1)S(1)}, bf16[256,256]{1,0:T(8,128)(2,1)S(1)}, u32[]{:S(2)}, u32[]{:S(2)}) collective-permute-start(bf16[256,256]{1,0:T(8,128)(2,1)S(1)} %get-tuple-element.9.r_3_.r_4_), channel_id=1, source_target_pairs={{0,8},{4,12},{8,0},{12,4},{1,9},{5,13},{9,1},{13,5},{2,10},{6,14},... | collective-permute-start | bytes 393224 | tf_op jit(solution)/shard_map/ppermute | solution.py:271
  32.3 11.9 %collective-permute-start.6 = (bf16[224,128]{1,0:T(8,128)(2,1)S(1)}, bf16[224,128]{1,0:T(8,128)(2,1)S(1)}, u32[]{:S(2)}, u32[]{:S(2)}) collective-permute-start(bf16[224,128]{1,0:T(8,128)(2,1)S(1)} %get-tuple-element.12), channel_id=1, source_target_pairs={{0,4},{4,8},{8,12},{12,0},{1,5},{5,9},{9,13},{13,1},{2,6},{6,10},{... | collective-permute-start | bytes 172040 | tf_op jit(solution)/shard_map/ppermute | solution.py:271
  33.3 14.4 %collective-permute-start.7 = (bf16[224,128]{1,0:T(8,128)(2,1)S(1)}, bf16[224,128]{1,0:T(8,128)(2,1)S(1)}, u32[]{:S(2)}, u32[]{:S(2)}) collective-permute-start(bf16[224,128]{1,0:T(8,128)(2,1)S(1)} %get-tuple-element.13), channel_id=1, source_target_pairs={{0,8},{4,12},{8,0},{12,4},{1,9},{5,13},{9,1},{13,5},{2,10},{6,14},... | collective-permute-start | bytes 172040 | tf_op jit(solution)/shard_map/ppermute | solution.py:271
  34.5 13.1 %collective-permute-start.8 = (bf16[224,128]{1,0:T(8,128)(2,1)S(1)}, bf16[224,128]{1,0:T(8,128)(2,1)S(1)}, u32[]{:S(2)}, u32[]{:S(2)}) collective-permute-start(bf16[224,128]{1,0:T(8,128)(2,1)S(1)} %get-tuple-element.14), channel_id=1, source_target_pairs={{0,12},{4,0},{8,4},{12,8},{1,13},{5,1},{9,5},{13,9},{2,14},{6,2},{... | collective-permute-start | bytes 172040 | tf_op jit(solution)/shard_map/ppermute | solution.py:271
  44.2 6.4 %copy-start.2 = (bf16[3,3,3,32,128]{4,3,2,1,0:T(8,128)(2,1)S(1)}, bf16[3,3,3,32,128]{4,3,2,1,0:T(8,128)(2,1)}, u32[]{:S(2)}) copy-start(bf16[3,3,3,32,128]{4,3,2,1,0:T(8,128)(2,1)} %param.9) | copy-start | bytes 663556
  47.7 6.5 %collective-permute-start.11 = (bf16[224,128]{1,0:T(8,128)(2,1)S(1)}, bf16[224,128]{1,0:T(8,128)(2,1)S(1)}, u32[]{:S(2)}, u32[]{:S(2)}) collective-permute-start(bf16[224,128]{1,0:T(8,128)(2,1)S(1)} %multiply_convert_fusion.r_0_), channel_id=1, source_target_pairs={{0,12},{4,0},{8,4},{12,8},{1,13},{5,1},{9,5},{13,9},{2,14},{6,2},{... | collective-permute-start | bytes 172040 | tf_op jit(solution)/shard_map/ppermute | solution.py:271
  49.4 6.1 %collective-permute-start.10 = (bf16[224,128]{1,0:T(8,128)(2,1)S(1)}, bf16[224,128]{1,0:T(8,128)(2,1)S(1)}, u32[]{:S(2)}, u32[]{:S(2)}) collective-permute-start(bf16[224,128]{1,0:T(8,128)(2,1)S(1)} %multiply_convert_fusion.r_0_), channel_id=1, source_target_pairs={{0,8},{4,12},{8,0},{12,4},{1,9},{5,13},{9,1},{13,5},{2,10},{6,14},... | collective-permute-start | bytes 172040 | tf_op jit(solution)/shard_map/ppermute | solution.py:271
  50.6 6.0 %collective-permute-start.9 = (bf16[224,128]{1,0:T(8,128)(2,1)S(1)}, bf16[224,128]{1,0:T(8,128)(2,1)S(1)}, u32[]{:S(2)}, u32[]{:S(2)}) collective-permute-start(bf16[224,128]{1,0:T(8,128)(2,1)S(1)} %multiply_convert_fusion.r_0_), channel_id=1, source_target_pairs={{0,4},{4,8},{8,12},{12,0},{1,5},{5,9},{9,13},{13,1},{2,6},{6,10},{... | collective-permute-start | bytes 172040 | tf_op jit(solution)/shard_map/ppermute | solution.py:271
where the time goes:
time: 57.6 us; the launch traced here: 57.4 us
  starting transfers between devices  20.7 us (36%)
  blocking collectives  20.6 us (36%)
  waiting for transfers between devices  7.98 us (14%)
  Pallas kernels  5.61 us (10%)
  local copies, waits for them, and re-layouts  1.71 us (3%)
  between operations  0.74 us (1%)
    ppermute x12, starting transfers between devices, ring(): lax.ppermute(value, 'space', [(i, (i + step) % count) for i in range(coun...  16.9 us
    ppermute x12, waiting for transfers between devices, ring(): lax.ppermute(value, 'space', [(i, (i + step) % count) for i in range(coun...  7.97 us
    all_gather x1, blocking collectives, shards(): a_own = lax.all_gather(p_own, 'chan', axis=0)  7.27 us
    all_gather x1, blocking collectives, shards(): lax.all_gather(out_grad.reshape(-1, width), 'chan', axis=0, tiled=True)  6.82 us
    all_gather x1, blocking collectives, shards(): a_rim = lax.all_gather(p_rim, 'chan', axis=0)  6.51 us
    pallas_call x7, Pallas kernels, local_call(): pl.pallas_call(kernel, out_shape=out_shape, in_specs=[pl.BlockSpec(memory...  5.61 us
    ppermute x1, starting transfers between devices, shards(): x_prev = lax.ppermute(xp[half:], 'space', up)  2.46 us
    ppermute x1, starting transfers between devices, shards(): x_next = lax.ppermute(xp[:half], 'space', down)  1.29 us
  transfers between devices with their start and end apart: 14, of which 4 were waited for; matrix products, arithmetic and copies ran while one was open for 1% of the time, Pallas kernels for 8%

commit v1 on v0

--- a/solution.py
+++ b/solution.py
@@ -173,10 +173,8 @@
 
 def in_grad_kernel(og, chans, w_ref, a_ref, r_ref, e_ref, out_ref, p_scr):
     width = og * og
-    part = width // 4
     shards = a_ref.shape[0]
     all_chans = shards * chans
-    block = 9 * chans
     for index in range(4):
         source, first = (r_ref, index // 3) if index in (0, 3) else (a_ref, index - 1)
         for parity in range(4):
@@ -185,6 +183,13 @@
                 p_scr[at : at + chans, parity * width : (parity + 1) * width] = source[
                     j, (first * 4 + parity) * chans : (first * 4 + parity + 1) * chans, :
                 ]
+    in_grad_planes(og, chans, all_chans, w_ref, e_ref, out_ref, p_scr)
+
+
+def in_grad_planes(og, chans, all_chans, w_ref, e_ref, out_ref, p_scr):
+    width = og * og
+    part = width // 4
+    block = 9 * chans
     weights = jnp.concatenate([w_ref[depth * block : (depth + 1) * block, :] for depth in (2, 1, 0)], axis=1)
     stacked = []
     for plane in range(2):
@@ -217,15 +222,21 @@
         out_ref[:, i * width : (i + 1) * width] = joined[i * chans : (i + 1) * chans].astype(BF16)
 
 
-def filter_two_kernel(og, chans, count, scale, *refs):
-    grads, gates, out_ref = refs[:count], refs[count : 2 * count], refs[2 * count]
-    g_scr, even_scr, odd_scr = refs[2 * count + 1 :]
+def filter_two_kernel(og, chans, count, scale, gathered, *refs):
+    number = 1 if gathered else count
+    grads, gates, out_ref = refs[:number], refs[number : number + count], refs[number + count]
+    g_scr, even_scr, odd_scr = refs[number + count + 1 :]
     s = lax.axis_index("space")
     half = 4 * chans
     block = 9 * chans
     for step in range(count):
         at = lax.rem(s + count - step, count)
-        g_scr[at] = grads[step][...]
+        if gathered:
+            part = grads[0].shape[1] // count
+            for j in range(grads[0].shape[0]):
+                g_scr[at, j * part : (j + 1) * part, :] = grads[0][j, step * part : (step + 1) * part, :]
+        else:
+            g_scr[at] = grads[step][...]
         value = gates[step][...].astype(F32)
         act = leaky(value, value).astype(BF16)
         for plane, target in enumerate((even_scr, odd_scr)):
@@ -252,6 +263,107 @@
     out_ref[...] = scr[0 : out_ref.shape[0], :]
 
 
+def all_grad_kernel(og, chans, count, w_ref, g_ref, *refs):
+    gates, (all_ref, local_ref, g_scr, h_scr, p_scr) = refs[:count], refs[count:]
+    s = lax.axis_index("space")
+    half = 4 * chans
+    part = g_ref.shape[1] // count
+    for step in range(count):
+        at = lax.rem(s + count - step, count)
+        for j in range(g_ref.shape[0]):
+            g_scr[at, j * part : (j + 1) * part, :] = g_ref[j, step * part : (step + 1) * part, :]
+        h_scr[at] = gates[step][...]
+    empty = jnp.zeros((half, og * og), BF16)
+    p_scr[0] = empty
+    p_scr[2 * count + 1] = empty
+    for q in range(count):
+        here = g_scr[q]
+        plane_grad(w_ref, here, None, h_scr[q, 0:half, :], chans, og, p_scr.at[2 * q + 1], 0, None)
+        after = g_scr[q + 1] if q < count - 1 else jnp.zeros_like(here)
+        plane_grad(w_ref, here, after, h_scr[q, half : 2 * half, :], chans, og, p_scr.at[2 * q + 2], 0, None)
+    all_ref[...] = p_scr[1 : 2 * count + 1]
+    local_ref[...] = p_scr[pl.ds(2 * s, 4)]
+
+
+def block_rows(chans):
+    return -(-27 * chans // 64) * 16
+
+
+def filter_block_kernel(og, chans, count, scale, p_ref, x_ref, out_ref, p_scr, x_scr):
+    width = og * og
+    half = 4 * chans
+    block = 9 * chans
+    lanes = 4 * chans
+    planes = 2 * count
+    empty = jnp.zeros((chans, 4 * width), BF16)
+    for index in (0, planes + 1, planes + 2):
+        p_scr[index * chans : (index + 1) * chans, :] = empty
+    for plane in range(planes):
+        at = (plane + 1) * chans
+        for parity in range(4):
+            p_scr[at : at + chans, parity * width : (parity + 1) * width] = p_ref[
+                plane, parity * chans : (parity + 1) * chans, :
+            ]
+    total = jnp.zeros((block, lanes), F32)
+    for plane in range(planes):
+        first = (plane % 2) * half
+        blocks = moved_blocks(x_ref[plane // 2, first : first + half, :], chans, og)
+        for parity in range(4):
+            x_scr[plane % 2, :, parity * width : (parity + 1) * width] = window_rows(blocks, parity, og)
+        total = total + lax.dot_general(
+            x_scr[plane % 2], p_scr[plane * chans : plane * chans + lanes, :], CONTRACT_LAST, preferred_element_type=F32
+        )
+    total = total * scale
+    rows = block_rows(chans)
+    tail = total[rows:]
+    moved_tail = [pltpu.roll(tail, lanes - (i + 1) * chans, 1) for i in range(3)]
+    spare = rows - 3 * (block - rows)
+    if spare:
+        moved_tail.append(jnp.zeros((spare, lanes), F32))
+    lane = lax.broadcasted_iota(jnp.int32, (rows, lanes), 1)
+    out_ref[...] = jnp.where(lane < 3 * chans, total[:rows], jnp.concatenate(moved_tail, axis=0)).astype(BF16)
+
+
+def join_kernel(chans, count, *refs):
+    pieces, out_ref, scr = refs[:count], refs[count], refs[count + 1]
+    s = lax.axis_index("space")
+    lanes = 4 * chans
+    block = 9 * chans
+    rows = block_rows(chans)
+    rest = block - rows
+    for step, piece in enumerate(pieces):
+        scr[step] = piece[...].astype(F32)
+    group = lax.broadcasted_iota(jnp.int32, (block, lanes), 1) // chans
+    sums = [jnp.zeros((block, lanes), F32) for _ in range(3)]
+    for j in range(count):
+        value = scr[lax.rem(s + count - j, count)]
+        tail = [pltpu.roll(value[i * rest : (i + 1) * rest], (i + 1) * chans, 1) for i in range(3)]
+        tail = jnp.where(group[:rest] == 0, tail[0], jnp.where(group[:rest] == 1, tail[1], tail[2]))
+        whole = jnp.concatenate([value, tail], axis=0)
+        for depth in range(3):
+            shift = (j - (2 - depth)) * chans % lanes
+            placed = pltpu.roll(whole, shift, 1) if shift else whole
+            sums[depth] = jnp.where(group == j, placed, sums[depth])
+    for depth in range(3):
+        out_ref[depth * block : (depth + 1) * block, :] = sums[depth]
+
+
+def in_grad_square_kernel(og, chans, count, w_ref, e_ref, *refs):
+    sources, out_ref, p_scr = refs[:count], refs[count], refs[count + 1]
+    i = lax.axis_index("chan")
+    width = og * og
+    all_chans = count * chans
+    for mask, source in enumerate(sources):
+        j = lax.bitwise_xor(i, mask)
+        for index in range(4):
+            at = pl.multiple_of(index * all_chans + j * chans, chans)
+            for parity in range(4):
+                p_scr[pl.ds(at, chans), parity * width : (parity + 1) * width] = source[
+                    index, parity * chans : (parity + 1) * chans, :
+                ]
+    in_grad_planes(og, chans, all_chans, w_ref, e_ref, out_ref, p_scr)
+
+
 def local_call(kernel, out_shape, scratch, flops, *operands):
     total = sum(value.size * value.dtype.itemsize for value in operands)
     total += sum(math.prod(o.shape) * o.dtype.itemsize for o in jax.tree.leaves(out_shape))
@@ -271,7 +383,7 @@
     return lax.ppermute(value, "space", [(i, (i + step) % count) for i in range(count)])
 
 
-def shards(inputs, pre_act, out_grad, weight_one, weight_two):
+def ring_shards(inputs, pre_act, out_grad, weight_one, weight_two):
     samples, chans, planes, cells = inputs.shape
     count = lax.axis_size("space")
     og = math.isqrt(out_grad.shape[3])
@@ -362,7 +474,7 @@
         matrix,
     )
     filter_two = local_call(
-        lambda *r: filter_two_kernel(og, chans, count, scale_two, *r),
+        lambda *r: filter_two_kernel(og, chans, count, scale_two, False, *r),
         shape((3 * block, all_out), F32),
         [
             pltpu.VMEM((count, all_out, width), BF16),
@@ -388,6 +500,118 @@
     )
 
 
+def square_shards(inputs, pre_act, out_grad, weight_one, weight_two):
+    samples, chans, planes, cells = inputs.shape
+    count = lax.axis_size("space")
+    og = math.isqrt(out_grad.shape[3])
+    width = og * og
+    half = 4 * chans
+    block = 9 * chans
+    all_chans = weight_one.shape[4]
+    all_out = weight_two.shape[4]
+    w1 = weight_one.reshape(3 * block, all_chans)
+    w2 = weight_two.reshape(3 * block, all_out)
+    matrix = jnp.asarray(split_matrix(og), BF16)
+    shape = jax.ShapeDtypeStruct
+    both = ("space", "chan")
+    scale_one = 1.0 / math.sqrt(samples * planes * count * cells)
+    scale_two = 1.0 / math.sqrt(samples * out_grad.shape[2] * count * width)
+
+    near = out_grad.reshape(-1, width)
+    near = jnp.concatenate([near] + [ring(near, step) for step in range(1, count)], axis=0)
+    xp, hp = local_call(
+        lambda *r: split_kernel(og, planes, chans, *r),
+        [shape((planes * half, width), BF16)] * 2,
+        [],
+        2 * 2 * planes * half * width * width,
+        inputs.reshape(chans, planes * cells),
+        pre_act.reshape(chans, planes * cells),
+        matrix,
+    )
+    turn = [(a * count + b, b * count + a) for a in range(count) for b in range(count)]
+    x_turned = lax.ppermute(xp, both, turn)
+    all_hp = [hp] + [ring(hp, step) for step in range(1, count)]
+    grads = lax.all_gather(near, "chan", axis=0)
+    p_all, p_local = local_call(
+        lambda *r: all_grad_kernel(og, chans, count, *r),
+        [shape((planes * count, half, width), BF16), shape((4, half, width), BF16)],
+        [
+            pltpu.VMEM((count, all_out, width), BF16),
+            pltpu.VMEM((count, planes * half, width), BF16),
+            pltpu.VMEM((planes * count + 2, half, width), BF16),
+        ],
+        2 * 3 * count * block * all_out * width,
+        w2,
+        grads,
+        *all_hp,
+    )
+    near_p = [p_local]
+    bit = count // 2
+    found = {0: p_local}
+    while bit:
+        pairs = [(i, i ^ bit) for i in range(count)]
+        found.update({mask ^ bit: lax.ppermute(value, "chan", pairs) for mask, value in found.items()})
+        bit //= 2
+    near_p = [found[mask] for mask in range(count)]
+
+    x_all = lax.all_gather(x_turned, "chan", axis=0)
+    rows = block_rows(chans)
+    piece = local_call(
+        lambda *r: filter_block_kernel(og, chans, count, scale_one, *r),
+        shape((rows, all_chans), BF16),
+        [
+            pltpu.VMEM(((planes * count + 3) * chans, 4 * width), BF16),
+            pltpu.VMEM((2, block, 4 * width), BF16),
+        ],
+        2 * 3 * count * block * all_chans * cells,
+        p_all,
+        x_all,
+    )
+    pieces = []
+    for step in range(count):
+        pairs = [(a * count + b, (b + step) % count * count + a) for a in range(count) for b in range(count)]
+        pieces.append(lax.ppermute(piece, both, pairs))
+    filter_two = local_call(
+        lambda *r: filter_two_kernel(og, chans, count, scale_two, True, *r),
+        shape((3 * block, all_out), F32),
+        [
+            pltpu.VMEM((count, all_out, width), BF16),
+            pltpu.VMEM((count, block, width), BF16),
+            pltpu.VMEM((count, block, width), BF16),
+        ],
+        2 * 3 * count * block * all_out * width,
+        grads,
+        *all_hp,
+    )
+    in_grad = local_call(
+        lambda *r: in_grad_square_kernel(og, chans, count, *r),
+        shape((chans, planes * cells), BF16),
+        [pltpu.VMEM((4 * all_chans, 4 * width), BF16)],
+        2 * 6 * block * all_chans * cells,
+        w1,
+        matrix,
+        *near_p,
+    )
+    filter_one = local_call(
+        lambda *r: join_kernel(chans, count, *r),
+        shape((3 * block, all_chans), F32),
+        [pltpu.VMEM((count, rows, all_chans), F32)],
+        0,
+        *pieces,
+    )
+    return (
+        in_grad.reshape(samples, chans, planes, cells),
+        filter_one.reshape(3, 3, 3, chans, all_chans),
+        filter_two.reshape(3, 3, 3, chans, all_out),
+    )
+
+
+def shards(*arguments):
+    count = lax.axis_size("space")
+    square = count == lax.axis_size("chan") and 4 * arguments[0].shape[1] == arguments[3].shape[4]
+    return (square_shards if square else ring_shards)(*arguments)
+
+
 def solution(mesh):
     in_specs = (
         P("groups", "chan", "space", None),

time: 57.6 us -> 60.5 us (1.050)
  the two profiles are of different devices: /device:TPU:0 before, /device:TPU:3 now
where the time goes in v1:
time: 60.5 us; the launch traced here: 60.3 us
  starting transfers between devices  22.2 us (37%)
  blocking collectives  18.7 us (31%)
  waiting for transfers between devices  9.08 us (15%)
  Pallas kernels  6.93 us (11%)
  local copies, waits for them, and re-layouts  2.61 us (4%)
  between operations  0.77 us (1%)
    all_gather x1, blocking collectives, square_shards(): x_all = lax.all_gather(x_turned, 'chan', axis=0)  10.2 us
    all_gather x1, blocking collectives, square_shards(): grads = lax.all_gather(near, 'chan', axis=0)  8.43 us
    ppermute x6, starting transfers between devices, ring(): lax.ppermute(value, 'space', [(i, (i + step) % count) for i in range(coun...  8.05 us
    pallas_call x6, Pallas kernels, local_call(): pl.pallas_call(kernel, out_shape=out_shape, in_specs=[pl.BlockSpec(memory...  6.93 us
    ppermute x4, waiting for transfers between devices, square_shards(): pieces.append(lax.ppermute(piece, both, pairs))  6.8 us
    ppermute x1, starting transfers between devices, square_shards(): x_turned = lax.ppermute(xp, both, turn)  6.46 us
    ppermute x4, starting transfers between devices, square_shards(): pieces.append(lax.ppermute(piece, both, pairs))  5.41 us
    ppermute x3, starting transfers between devices, square_shards(): lax.ppermute(value, 'chan', pairs)  2.3 us
  transfers between devices with their start and end apart: 14, of which 4 were waited for; matrix products, arithmetic and copies ran while one was open for 2% of the time, Pallas kernels for 8%

profile of v1, /device:TPU:3, one launch (start us, length us, event | category | flops | bytes accessed | tf_op | source)
XLA Modules:
  0.0 60.3 jit_solution(124772928477213767)
XLA Ops:
  0.6 1.3 %collective-permute-start = (bf16[64,256]{1,0:T(8,128)(2,1)}, bf16[64,256]{1,0:T(8,128)(2,1)S(1)}, u32[]{:S(2)}, u32[]{:S(2)}) collective-permute-start(bf16[64,256]{1,0:T(8,128)(2,1)} %bitcast.24), channel_id=1, source_target_pairs={{0,4},{4,8},{8,12},{12,0},{1,5},{5,9},{9,13},{13,1},{2,6},{6,10},{... | collective-permute-start | bytes 98312 | tf_op jit(solution)/shard_map/ppermute | solution.py:383
  2.0 2.3 %collective-permute-start.1 = (bf16[64,256]{1,0:T(8,128)(2,1)}, bf16[64,256]{1,0:T(8,128)(2,1)S(1)}, u32[]{:S(2)}, u32[]{:S(2)}) collective-permute-start(bf16[64,256]{1,0:T(8,128)(2,1)} %bitcast.25), channel_id=1, source_target_pairs={{0,8},{4,12},{8,0},{12,4},{1,9},{5,13},{9,1},{13,5},{2,10},{6,14},... | collective-permute-start | bytes 98312 | tf_op jit(solution)/shard_map/ppermute | solution.py:383
  4.3 1.1 %collective-permute-start.2 = (bf16[64,256]{1,0:T(8,128)(2,1)}, bf16[64,256]{1,0:T(8,128)(2,1)S(1)}, u32[]{:S(2)}, u32[]{:S(2)}) collective-permute-start(bf16[64,256]{1,0:T(8,128)(2,1)} %bitcast.26), channel_id=1, source_target_pairs={{0,12},{4,0},{8,4},{12,8},{1,13},{5,1},{9,5},{13,9},{2,14},{6,2},{... | collective-permute-start | bytes 98312 | tf_op jit(solution)/shard_map/ppermute | solution.py:383
  5.4 1.0 %copy.10 = bf16[4,8,2,1024]{3,1,2,0:T(8,128)(2,1)S(1)} copy(bf16[4,8,2,1024]{3,2,1,0:T(2,128)(2,1)} %bitcast.22) | data formatting | bytes 262144
  6.4 0.9 %copy-done = bf16[256,256]{1,0:T(8,128)(2,1)S(1)} copy-done((bf16[256,256]{1,0:T(8,128)(2,1)S(1)}, bf16[256,256]{1,0:T(8,128)(2,1)}, u32[]{:S(2)}) %copy-start) | copy-done | bytes 131096
  7.6 0.4 collective-permute-start.3
  8.1 2.8 %collective-permute-start.5 = (bf16[256,256]{1,0:T(8,128)(2,1)S(1)}, bf16[256,256]{1,0:T(8,128)(2,1)S(1)}, u32[]{:S(2)}, u32[]{:S(2)}) collective-permute-start(bf16[256,256]{1,0:T(8,128)(2,1)S(1)} %get-tuple-element.7.r_2_.r_1_), channel_id=1, source_target_pairs={{0,12},{4,0},{8,4},{12,8},{1,13},{5,1},{9,5},{13,9},{2,14},{6,2},{... | collective-permute-start | bytes 393224 | tf_op jit(solution)/shard_map/ppermute | solution.py:383
  10.9 8.4 %all-gather = bf16[1024,256]{1,0:T(8,128)(2,1)S(1)} all-gather(bf16[256,256]{1,0:T(8,128)(2,1)S(1)} %pad_maximum_fusion), channel_id=2, replica_groups=mesh['groups'=2,'space'=4,'chan'=4] {'chan'}, dimensions={0}, use_global_device_ids=true | all-gather | bytes 655360 | tf_op jit(solution)/shard_map/all_gather | solution.py:534
  19.4 0.8 %shard_map.86 = (bf16[8,128,256]{2,1,0:T(8,128)(2,1)S(1)}, bf16[4,128,256]{2,1,0:T(8,128)(2,1)S(1)}) custom-call(bf16[864,256]{1,0:T(8,128)(2,1)S(1)} %bitcast.18, bf16[4,256,256]{2,1,0:T(8,128)(2,1)S(1)} %bitcast.13, bf16[256,256]{1,0:T(8,128)(2,1)S(1)} %get-tuple-element.7.r_2_.r_1_, bf16[256,256]{1,0:T(8,128)(2,1)S(1)} %collective-permute-done.3.r_3_.r_2_, ...), custom_call_target="tpu_custom_call" | custom-call | flops 452984832 | bytes 2277376 | tf_op jit(solution)/shard_map/pallas_call | solution.py:370
  20.2 0.9 %collective-permute-start.7 = (bf16[4,128,256]{2,1,0:T(8,128)(2,1)S(1)}, bf16[4,128,256]{2,1,0:T(8,128)(2,1)S(1)}, u32[]{:S(2)}, u32[]{:S(2)}) collective-permute-start(bf16[4,128,256]{2,1,0:T(8,128)(2,1)S(1)} %get-tuple-element.8.r_2_), channel_id=1, source_target_pairs={{0,2},{1,3},{2,0},{3,1},{4,6},{5,7},{6,4},{7,5},{8,10},{9,11},{10,... | collective-permute-start | bytes 786440 | tf_op jit(solution)/shard_map/ppermute | solution.py:553
  21.2 6.5 %collective-permute-start.9 = (bf16[256,256]{1,0:T(8,128)(2,1)S(1)}, bf16[256,256]{1,0:T(8,128)(2,1)S(1)}, u32[]{:S(2)}, u32[]{:S(2)}) collective-permute-start(bf16[256,256]{1,0:T(8,128)(2,1)S(1)} %get-tuple-element.10), channel_id=1, source_target_pairs={{0,0},{1,4},{2,8},{3,12},{4,1},{5,5},{6,9},{7,13},{8,2},{9,6},{10,... | collective-permute-start | bytes 393224 | tf_op jit(solution)/shard_map/ppermute | solution.py:532
  27.7 1.3 %collective-permute-start.8 = (bf16[4,128,256]{2,1,0:T(8,128)(2,1)S(1)}, bf16[4,128,256]{2,1,0:T(8,128)(2,1)S(1)}, u32[]{:S(2)}, u32[]{:S(2)}) collective-permute-start(bf16[4,128,256]{2,1,0:T(8,128)(2,1)S(1)} %collective-permute-done.7.r_4_), channel_id=1, source_target_pairs={{0,1},{1,0},{2,3},{3,2},{4,5},{5,4},{6,7},{7,6},{8,9},{9,8},{10,11... | collective-permute-start | bytes 786440 | tf_op jit(solution)/shard_map/ppermute | solution.py:553
  29.0 2.2 %collective-permute-done.9 = bf16[256,256]{1,0:T(8,128)(2,1)S(1)} collective-permute-done((bf16[256,256]{1,0:T(8,128)(2,1)S(1)}, bf16[256,256]{1,0:T(8,128)(2,1)S(1)}, u32[]{:S(2)}, u32[]{:S(2)}) %collective-permute-start.9) | collective-permute-done | bytes 131104 | tf_op jit(solution)/shard_map/ppermute | solution.py:532
  31.2 10.2 %all-gather.1 = bf16[1024,256]{1,0:T(8,128)(2,1)S(1)} all-gather(bf16[256,256]{1,0:T(8,128)(2,1)S(1)} %collective-permute-done.9), channel_id=3, replica_groups=mesh['groups'=2,'space'=4,'chan'=4] {'chan'}, dimensions={0}, use_global_device_ids=true | all-gather | bytes 655360 | tf_op jit(solution)/shard_map/all_gather | solution.py:557
  41.5 1.5 %shard_map.88 = bf16[224,128]{1,0:T(8,128)(2,1)S(1)} custom-call(bf16[8,128,256]{2,1,0:T(8,128)(2,1)S(1)} %get-tuple-element.9.r_0_, bf16[4,256,256]{2,1,0:T(8,128)(2,1)S(1)} %bitcast.15), custom_call_target="tpu_custom_call" | custom-call | flops 905969664 | bytes 1105920 | tf_op jit(solution)/shard_map/pallas_call | solution.py:370
  43.0 3.8 %collective-permute-start.10 = (bf16[224,128]{1,0:T(8,128)(2,1)S(1)}, bf16[224,128]{1,0:T(8,128)(2,1)S(1)}, u32[]{:S(2)}, u32[]{:S(2)}) collective-permute-start(bf16[224,128]{1,0:T(8,128)(2,1)S(1)} %shard_map.88), channel_id=1, source_target_pairs={{0,0},{1,4},{2,8},{3,12},{4,1},{5,5},{6,9},{7,13},{8,2},{9,6},{10,... | collective-permute-start | bytes 172040 | tf_op jit(solution)/shard_map/ppermute | solution.py:573
  46.9 0.5 collective-permute-start.12
  47.4 3.9 %collective-permute-done.10.r_0_ = bf16[224,128]{1,0:T(8,128)(2,1)S(1)} collective-permute-done((bf16[224,128]{1,0:T(8,128)(2,1)S(1)}, bf16[224,128]{1,0:T(8,128)(2,1)S(1)}, u32[]{:S(2)}, u32[]{:S(2)}) %collective-permute-start.10) | collective-permute-done | bytes 57376 | tf_op jit(solution)/shard_map/ppermute | solution.py:573
  51.3 1.0 %collective-permute-start.13 = (bf16[224,128]{1,0:T(8,128)(2,1)S(1)}, bf16[224,128]{1,0:T(8,128)(2,1)S(1)}, u32[]{:S(2)}, u32[]{:S(2)}) collective-permute-start(bf16[224,128]{1,0:T(8,128)(2,1)S(1)} %shard_map.88), channel_id=1, source_target_pairs={{0,12},{1,0},{2,4},{3,8},{4,13},{5,1},{6,5},{7,9},{8,14},{9,2},{10... | collective-permute-start | bytes 172040 | tf_op jit(solution)/shard_map/ppermute | solution.py:573
  52.3 1.8 %shard_map.90 = f32[864,256]{1,0:T(8,128)} custom-call(bf16[4,256,256]{2,1,0:T(8,128)(2,1)S(1)} %bitcast.14, bf16[256,256]{1,0:T(8,128)(2,1)S(1)} %get-tuple-element.7.r_2_.r_1_, bf16[256,256]{1,0:T(8,128)(2,1)S(1)} %collective-permute-done.3.r_3_.r_2_, bf16[256,256]{1,0:T(8,128)(2,1)S(1)} %collective-permute-done.4.r_4_.r_3_, ...), custom_call_target="tpu_custom_call" | custom-call | flops 452984832 | bytes 1933312 | tf_op jit(solution)/shard_map/pallas_call | solution.py:370
  54.1 2.9 %collective-permute-done.13.r_3_ = bf16[224,128]{1,0:T(8,128)(2,1)S(1)} collective-permute-done((bf16[224,128]{1,0:T(8,128)(2,1)S(1)}, bf16[224,128]{1,0:T(8,128)(2,1)S(1)}, u32[]{:S(2)}, u32[]{:S(2)}) %collective-permute-start.13) | collective-permute-done | bytes 57376 | tf_op jit(solution)/shard_map/ppermute | solution.py:573
  57.0 1.4 %shard_map.89 = f32[864,128]{1,0:T(8,128)} custom-call(bf16[224,128]{1,0:T(8,128)(2,1)S(1)} %collective-permute-done.10.r_0_, bf16[224,128]{1,0:T(8,128)(2,1)S(1)} %collective-permute-done.11.r_1_, bf16[224,128]{1,0:T(8,128)(2,1)S(1)} %collective-permute-done.12.r_2_, bf16[224,128]{1,0:T(8,128)(2,1)S(1)} %collective-permute-done.13.r_3_), custom_call_target="tpu_custom_call" | custom-call | bytes 671744 | tf_op jit(solution)/shard_map/pallas_call | solution.py:370
  58.4 1.2 %shard_map.87 = bf16[32,2048]{1,0:T(8,128)(2,1)S(1)} custom-call(bf16[864,128]{1,0:T(8,128)(2,1)S(1)} %bitcast.19, bf16[256,256]{1,0:T(8,128)(2,1)S(1)} %copy-done, bf16[4,128,256]{2,1,0:T(8,128)(2,1)S(1)} %get-tuple-element.8.r_2_, bf16[4,128,256]{2,1,0:T(8,128)(2,1)S(1)} %collective-permute-done.6.r_3_, ...), custom_call_target="tpu_custom_call" | custom-call | flops 452984832 | bytes 1531904 | tf_op jit(solution)/shard_map/pallas_call | solution.py:370
  59.5 0.7 %reshape.35 = bf16[1,32,2,1024]{3,2,1,0:T(2,128)(2,1)} reshape(bf16[32,2048]{1,0:T(8,128)(2,1)S(1)} %shard_map.87) | data formatting | bytes 262144 | tf_op jit(solution)/shard_map/reshape | solution.py:603
  (26 shorter events, 0.6 us)
Async XLA Ops:
  0.6 7.4 %collective-permute-start = (bf16[64,256]{1,0:T(8,128)(2,1)}, bf16[64,256]{1,0:T(8,128)(2,1)S(1)}, u32[]{:S(2)}, u32[]{:S(2)}) collective-permute-start(bf16[64,256]{1,0:T(8,128)(2,1)} %bitcast.24), channel_id=1, source_target_pairs={{0,4},{4,8},{8,12},{12,0},{1,5},{5,9},{9,13},{13,1},{2,6},{6,10},{... | collective-permute-start | bytes 98312 | tf_op jit(solution)/shard_map/ppermute | solution.py:383
  2.0 8.9 %collective-permute-start.1 = (bf16[64,256]{1,0:T(8,128)(2,1)}, bf16[64,256]{1,0:T(8,128)(2,1)S(1)}, u32[]{:S(2)}, u32[]{:S(2)}) collective-permute-start(bf16[64,256]{1,0:T(8,128)(2,1)} %bitcast.25), channel_id=1, source_target_pairs={{0,8},{4,12},{8,0},{12,4},{1,9},{5,13},{9,1},{13,5},{2,10},{6,14},... | collective-permute-start | bytes 98312 | tf_op jit(solution)/shard_map/ppermute | solution.py:383
  4.3 6.6 %collective-permute-start.2 = (bf16[64,256]{1,0:T(8,128)(2,1)}, bf16[64,256]{1,0:T(8,128)(2,1)S(1)}, u32[]{:S(2)}, u32[]{:S(2)}) collective-permute-start(bf16[64,256]{1,0:T(8,128)(2,1)} %bitcast.26), channel_id=1, source_target_pairs={{0,12},{4,0},{8,4},{12,8},{1,13},{5,1},{9,5},{13,9},{2,14},{6,2},{... | collective-permute-start | bytes 98312 | tf_op jit(solution)/shard_map/ppermute | solution.py:383
  5.4 1.0 %copy-start.3 = (bf16[1,32,2,1024]{3,2,1,0:T(2,128)(2,1)S(1)}, bf16[1,32,2,1024]{3,2,1,0:T(2,128)(2,1)}, u32[]{:S(2)}) copy-start(bf16[1,32,2,1024]{3,2,1,0:T(2,128)(2,1)} %param.6) | copy-start | bytes 393220
  6.3 0.9 %copy-start = (bf16[256,256]{1,0:T(8,128)(2,1)S(1)}, bf16[256,256]{1,0:T(8,128)(2,1)}, u32[]{:S(2)}) copy-start(bf16[256,256]{1,0:T(8,128)(2,1)} %constant.2.clone.r_2_.r_1_) | copy-start | bytes 393220
  7.2 3.7 %copy-start.4 = (bf16[1,64,1,256]{3,1,2,0:T(8,128)(2,1)S(1)}, bf16[1,64,1,256]{3,1,2,0:T(8,128)(2,1)}, u32[]{:S(2)}) copy-start(bf16[1,64,1,256]{3,1,2,0:T(8,128)(2,1)} %param.8) | copy-start | bytes 98308
  7.6 11.9 %copy-start.1 = (bf16[3,3,3,32,256]{4,3,2,1,0:T(8,128)(2,1)S(1)}, bf16[3,3,3,32,256]{4,3,2,1,0:T(8,128)(2,1)}, u32[]{:S(2)}) copy-start(bf16[3,3,3,32,256]{4,3,2,1,0:T(8,128)(2,1)} %param.10) | copy-start | bytes 1327108
  7.6 11.8 %collective-permute-start.3 = (bf16[256,256]{1,0:T(8,128)(2,1)S(1)}, bf16[256,256]{1,0:T(8,128)(2,1)S(1)}, u32[]{:S(2)}, u32[]{:S(2)}) collective-permute-start(bf16[256,256]{1,0:T(8,128)(2,1)S(1)} %get-tuple-element.7.r_2_.r_1_), channel_id=1, source_target_pairs={{0,4},{4,8},{8,12},{12,0},{1,5},{5,9},{9,13},{13,1},{2,6},{6,10},{... | collective-permute-start | bytes 393224 | tf_op jit(solution)/shard_map/ppermute | solution.py:383
  8.0 11.4 %collective-permute-start.4 = (bf16[256,256]{1,0:T(8,128)(2,1)S(1)}, bf16[256,256]{1,0:T(8,128)(2,1)S(1)}, u32[]{:S(2)}, u32[]{:S(2)}) collective-permute-start(bf16[256,256]{1,0:T(8,128)(2,1)S(1)} %get-tuple-element.7.r_2_.r_1_), channel_id=1, source_target_pairs={{0,8},{4,12},{8,0},{12,4},{1,9},{5,13},{9,1},{13,5},{2,10},{6,14},... | collective-permute-start | bytes 393224 | tf_op jit(solution)/shard_map/ppermute | solution.py:383
  8.1 11.3 %collective-permute-start.5 = (bf16[256,256]{1,0:T(8,128)(2,1)S(1)}, bf16[256,256]{1,0:T(8,128)(2,1)S(1)}, u32[]{:S(2)}, u32[]{:S(2)}) collective-permute-start(bf16[256,256]{1,0:T(8,128)(2,1)S(1)} %get-tuple-element.7.r_2_.r_1_), channel_id=1, source_target_pairs={{0,12},{4,0},{8,4},{12,8},{1,13},{5,1},{9,5},{13,9},{2,14},{6,2},{... | collective-permute-start | bytes 393224 | tf_op jit(solution)/shard_map/ppermute | solution.py:383
  20.2 7.5 %collective-permute-start.7 = (bf16[4,128,256]{2,1,0:T(8,128)(2,1)S(1)}, bf16[4,128,256]{2,1,0:T(8,128)(2,1)S(1)}, u32[]{:S(2)}, u32[]{:S(2)}) collective-permute-start(bf16[4,128,256]{2,1,0:T(8,128)(2,1)S(1)} %get-tuple-element.8.r_2_), channel_id=1, source_target_pairs={{0,2},{1,3},{2,0},{3,1},{4,6},{5,7},{6,4},{7,5},{8,10},{9,11},{10,... | collective-permute-start | bytes 786440 | tf_op jit(solution)/shard_map/ppermute | solution.py:553
  21.2 10.1 %collective-permute-start.9 = (bf16[256,256]{1,0:T(8,128)(2,1)S(1)}, bf16[256,256]{1,0:T(8,128)(2,1)S(1)}, u32[]{:S(2)}, u32[]{:S(2)}) collective-permute-start(bf16[256,256]{1,0:T(8,128)(2,1)S(1)} %get-tuple-element.10), channel_id=1, source_target_pairs={{0,0},{1,4},{2,8},{3,12},{4,1},{5,5},{6,9},{7,13},{8,2},{9,6},{10,... | collective-permute-start | bytes 393224 | tf_op jit(solution)/shard_map/ppermute | solution.py:532
  27.7 30.7 %collective-permute-start.6 = (bf16[4,128,256]{2,1,0:T(8,128)(2,1)S(1)}, bf16[4,128,256]{2,1,0:T(8,128)(2,1)S(1)}, u32[]{:S(2)}, u32[]{:S(2)}) collective-permute-start(bf16[4,128,256]{2,1,0:T(8,128)(2,1)S(1)} %get-tuple-element.8.r_2_), channel_id=1, source_target_pairs={{0,1},{1,0},{2,3},{3,2},{4,5},{5,4},{6,7},{7,6},{8,9},{9,8},{10,11... | collective-permute-start | bytes 786440 | tf_op jit(solution)/shard_map/ppermute | solution.py:553
  27.7 30.6 %collective-permute-start.8 = (bf16[4,128,256]{2,1,0:T(8,128)(2,1)S(1)}, bf16[4,128,256]{2,1,0:T(8,128)(2,1)S(1)}, u32[]{:S(2)}, u32[]{:S(2)}) collective-permute-start(bf16[4,128,256]{2,1,0:T(8,128)(2,1)S(1)} %collective-permute-done.7.r_4_), channel_id=1, source_target_pairs={{0,1},{1,0},{2,3},{3,2},{4,5},{5,4},{6,7},{7,6},{8,9},{9,8},{10,11... | collective-permute-start | bytes 786440 | tf_op jit(solution)/shard_map/ppermute | solution.py:553
  43.0 8.3 %collective-permute-start.10 = (bf16[224,128]{1,0:T(8,128)(2,1)S(1)}, bf16[224,128]{1,0:T(8,128)(2,1)S(1)}, u32[]{:S(2)}, u32[]{:S(2)}) collective-permute-start(bf16[224,128]{1,0:T(8,128)(2,1)S(1)} %shard_map.88), channel_id=1, source_target_pairs={{0,0},{1,4},{2,8},{3,12},{4,1},{5,5},{6,9},{7,13},{8,2},{9,6},{10,... | collective-permute-start | bytes 172040 | tf_op jit(solution)/shard_map/ppermute | solution.py:573
  46.8 7.3 %collective-permute-start.11 = (bf16[224,128]{1,0:T(8,128)(2,1)S(1)}, bf16[224,128]{1,0:T(8,128)(2,1)S(1)}, u32[]{:S(2)}, u32[]{:S(2)}) collective-permute-start(bf16[224,128]{1,0:T(8,128)(2,1)S(1)} %shard_map.88), channel_id=1, source_target_pairs={{0,4},{1,8},{2,12},{3,0},{4,5},{5,9},{6,13},{7,1},{8,6},{9,10},{10... | collective-permute-start | bytes 172040 | tf_op jit(solution)/shard_map/ppermute | solution.py:573
  46.9 7.2 %collective-permute-start.12 = (bf16[224,128]{1,0:T(8,128)(2,1)S(1)}, bf16[224,128]{1,0:T(8,128)(2,1)S(1)}, u32[]{:S(2)}, u32[]{:S(2)}) collective-permute-start(bf16[224,128]{1,0:T(8,128)(2,1)S(1)} %shard_map.88), channel_id=1, source_target_pairs={{0,8},{1,12},{2,0},{3,4},{4,9},{5,13},{6,1},{7,5},{8,10},{9,14},{1... | collective-permute-start | bytes 172040 | tf_op jit(solution)/shard_map/ppermute | solution.py:573
  51.3 5.7 %collective-permute-start.13 = (bf16[224,128]{1,0:T(8,128)(2,1)S(1)}, bf16[224,128]{1,0:T(8,128)(2,1)S(1)}, u32[]{:S(2)}, u32[]{:S(2)}) collective-permute-start(bf16[224,128]{1,0:T(8,128)(2,1)S(1)} %shard_map.88), channel_id=1, source_target_pairs={{0,12},{1,0},{2,4},{3,8},{4,13},{5,1},{6,5},{7,9},{8,14},{9,2},{10... | collective-permute-start | bytes 172040 | tf_op jit(solution)/shard_map/ppermute | solution.py:573
  54.1 4.3 %copy-start.2 = (bf16[3,3,3,32,128]{4,3,2,1,0:T(8,128)(2,1)S(1)}, bf16[3,3,3,32,128]{4,3,2,1,0:T(8,128)(2,1)}, u32[]{:S(2)}) copy-start(bf16[3,3,3,32,128]{4,3,2,1,0:T(8,128)(2,1)} %param.9) | copy-start | bytes 663556

commit v2 on v1

--- a/solution.py
+++ b/solution.py
@@ -183,10 +183,12 @@
                 p_scr[at : at + chans, parity * width : (parity + 1) * width] = source[
                     j, (first * 4 + parity) * chans : (first * 4 + parity + 1) * chans, :
                 ]
-    in_grad_planes(og, chans, all_chans, w_ref, e_ref, out_ref, p_scr)
-
-
-def in_grad_planes(og, chans, all_chans, w_ref, e_ref, out_ref, p_scr):
+    joined = in_grad_planes(og, chans, all_chans, w_ref, e_ref, p_scr)
+    for i in range(8):
+        out_ref[:, i * width : (i + 1) * width] = joined[i * chans : (i + 1) * chans].astype(BF16)
+
+
+def in_grad_planes(og, chans, all_chans, w_ref, e_ref, p_scr):
     width = og * og
     part = width // 4
     block = 9 * chans
@@ -217,31 +219,36 @@
             stacked.append(
                 jnp.concatenate([value[:, i * part : (i + 1) * part] for value in sums], axis=1).astype(BF16)
             )
-    joined = lax.dot_general(jnp.concatenate(stacked, axis=0), e_ref[...], CONTRACT_LAST, preferred_element_type=F32)
-    for i in range(8):
-        out_ref[:, i * width : (i + 1) * width] = joined[i * chans : (i + 1) * chans].astype(BF16)
-
-
-def filter_two_kernel(og, chans, count, scale, gathered, *refs):
-    number = 1 if gathered else count
-    grads, gates, out_ref = refs[:number], refs[number : number + count], refs[number + count]
-    g_scr, even_scr, odd_scr = refs[number + count + 1 :]
+    return lax.dot_general(jnp.concatenate(stacked, axis=0), e_ref[...], CONTRACT_LAST, preferred_element_type=F32)
+
+
+def filter_two_kernel(og, chans, count, scale, *refs):
+    grads, gates, out_ref = refs[:count], refs[count : 2 * count], refs[2 * count]
+    g_scr, even_scr, odd_scr = refs[2 * count + 1 :]
     s = lax.axis_index("space")
     half = 4 * chans
     block = 9 * chans
     for step in range(count):
         at = lax.rem(s + count - step, count)
-        if gathered:
-            part = grads[0].shape[1] // count
-            for j in range(grads[0].shape[0]):
-                g_scr[at, j * part : (j + 1) * part, :] = grads[0][j, step * part : (step + 1) * part, :]
-        else:
-            g_scr[at] = grads[step][...]
+        g_scr[at] = grads[step][...]
         value = gates[step][...].astype(F32)
         act = leaky(value, value).astype(BF16)
         for plane, target in enumerate((even_scr, odd_scr)):
             blocks = moved_blocks(act[plane * half : (plane + 1) * half], chans, og)
             target[at] = window_rows(blocks, 0, og)
+    filter_two_sums(count, block, scale, g_scr, even_scr, odd_scr, out_ref)
+
+
+def filter_two_square_kernel(og, chans, count, scale, g_ref, act_ref, out_ref, even_scr, odd_scr):
+    half = 4 * chans
+    for at in range(count):
+        for plane, target in enumerate((even_scr, odd_scr)):
+            blocks = moved_blocks(act_ref[at, plane * half : (plane + 1) * half, :], chans, og)
+            target[at] = window_rows(blocks, 0, og)
+    filter_two_sums(count, 9 * chans, scale, g_ref, even_scr, odd_scr, out_ref)
+
+
+def filter_two_sums(count, block, scale, g_scr, even_scr, odd_scr, out_ref):
     totals = [jnp.zeros((block, g_scr.shape[1]), F32) for _ in range(3)]
     for at in range(count):
         sources = (odd_scr.at[at - 1] if at else None, even_scr.at[at], odd_scr.at[at])
@@ -263,38 +270,80 @@
     out_ref[...] = scr[0 : out_ref.shape[0], :]
 
 
-def all_grad_kernel(og, chans, count, w_ref, g_ref, *refs):
-    gates, (all_ref, local_ref, g_scr, h_scr, p_scr) = refs[:count], refs[count:]
+def plane_matrix(chans, planes):
+    row = np.arange(chans * planes)
+    place = (row % planes) * chans + row // planes
+    return (place[None, :] == np.arange(chans * planes)[:, None]).astype(np.float32)
+
+
+def split_planes(value, order, matrix, chans, planes, og):
+    width = og * og
+    part = width // 4
+    value = value.reshape(chans * planes, 4 * width)
+    value = jnp.dot(order, value, preferred_element_type=F32).astype(BF16)
+    stacked = jnp.concatenate([value[:, i * width : (i + 1) * width] for i in range(4)], axis=0)
+    cells = jnp.dot(stacked, matrix, preferred_element_type=F32)
+    rows = chans * planes
+    result = []
+    for plane in range(planes):
+        for parity in range(4):
+            pieces = [
+                cells[i * rows + plane * chans : i * rows + (plane + 1) * chans, parity * part : (parity + 1) * part]
+                for i in range(4)
+            ]
+            result.append(jnp.concatenate(pieces, axis=1))
+    return jnp.concatenate(result, axis=0)
+
+
+def pack_kernel(*refs):
+    sources, out_ref = refs[:-1], refs[-1]
+    rows = sources[0].shape[0]
+    for step, source in enumerate(sources):
+        out_ref[step * rows : (step + 1) * rows, :] = source[...]
+
+
+def all_grad_kernel(og, chans, count, scale, w_ref, e_ref, order_ref, *refs):
+    grads, gates, x_all, refs = refs[0], refs[1 : count + 1], refs[count + 1], refs[count + 2 :]
+    local_ref, g_ref, act_ref, piece_ref, h_scr, p_scr, *block_refs = refs
     s = lax.axis_index("space")
     half = 4 * chans
-    part = g_ref.shape[1] // count
+    part = grads.shape[1] // count
     for step in range(count):
         at = lax.rem(s + count - step, count)
-        for j in range(g_ref.shape[0]):
-            g_scr[at, j * part : (j + 1) * part, :] = g_ref[j, step * part : (step + 1) * part, :]
-        h_scr[at] = gates[step][...]
+        for j in range(count):
+            g_ref[at, j * part : (j + 1) * part, :] = grads[j, step * part : (step + 1) * part, :]
+        value = split_planes(gates[step][...], order_ref[...], e_ref[...], chans, 2, og)
+        h_scr[at] = value.astype(BF16)
+        act_ref[at] = leaky(value, value).astype(BF16)
     empty = jnp.zeros((half, og * og), BF16)
     p_scr[0] = empty
     p_scr[2 * count + 1] = empty
     for q in range(count):
-        here = g_scr[q]
+        here = g_ref[q]
         plane_grad(w_ref, here, None, h_scr[q, 0:half, :], chans, og, p_scr.at[2 * q + 1], 0, None)
-        after = g_scr[q + 1] if q < count - 1 else jnp.zeros_like(here)
+        after = g_ref[q + 1] if q < count - 1 else jnp.zeros_like(here)
         plane_grad(w_ref, here, after, h_scr[q, half : 2 * half, :], chans, og, p_scr.at[2 * q + 2], 0, None)
-    all_ref[...] = p_scr[1 : 2 * count + 1]
     local_ref[...] = p_scr[pl.ds(2 * s, 4)]
+    filter_block(og, chans, count, scale, p_scr, e_ref, order_ref, x_all, piece_ref, *block_refs)
+
+
+def mixed(index, count):
+    return index % 2 * (count // 2) + index // 2
 
 
 def block_rows(chans):
     return -(-27 * chans // 64) * 16
 
 
-def filter_block_kernel(og, chans, count, scale, p_ref, x_ref, out_ref, p_scr, x_scr):
+def filter_block(og, chans, count, scale, p_ref, e_ref, order_ref, source, out_ref, x_ref, p_scr, x_scr):
     width = og * og
     half = 4 * chans
     block = 9 * chans
     lanes = 4 * chans
     planes = 2 * count
+    for j in range(count):
+        value = split_planes(source[j], order_ref[...], e_ref[...], chans, 2, og)
+        x_ref[mixed(j, count)] = value.astype(BF16)
     empty = jnp.zeros((chans, 4 * width), BF16)
     for index in (0, planes + 1, planes + 2):
         p_scr[index * chans : (index + 1) * chans, :] = empty
@@ -302,7 +351,7 @@
         at = (plane + 1) * chans
         for parity in range(4):
             p_scr[at : at + chans, parity * width : (parity + 1) * width] = p_ref[
-                plane, parity * chans : (parity + 1) * chans, :
+                plane + 1, parity * chans : (parity + 1) * chans, :
             ]
     total = jnp.zeros((block, lanes), F32)
     for plane in range(planes):
@@ -348,7 +397,7 @@
         out_ref[depth * block : (depth + 1) * block, :] = sums[depth]
 
 
-def in_grad_square_kernel(og, chans, count, w_ref, e_ref, *refs):
+def in_grad_square_kernel(og, chans, count, w_ref, e_ref, order_ref, *refs):
     sources, out_ref, p_scr = refs[:count], refs[count], refs[count + 1]
     i = lax.axis_index("chan")
     width = og * og
@@ -361,7 +410,14 @@
                 p_scr[pl.ds(at, chans), parity * width : (parity + 1) * width] = source[
                     index, parity * chans : (parity + 1) * chans, :
                 ]
-    in_grad_planes(og, chans, all_chans, w_ref, e_ref, out_ref, p_scr)
+    joined = in_grad_planes(og, chans, all_chans, w_ref, e_ref, p_scr)
+    rows = [
+        jnp.concatenate([joined[(plane * 4 + k) * chans : (plane * 4 + k + 1) * chans] for k in range(4)], axis=1)
+        for plane in range(2)
+    ]
+    value = jnp.concatenate(rows, axis=0).astype(BF16)
+    value = lax.dot_general(order_ref[...], value, (((0,), (0,)), ((), ())), preferred_element_type=F32)
+    out_ref[...] = value.astype(BF16).reshape(out_ref.shape)
 
 
 def local_call(kernel, out_shape, scratch, flops, *operands):
@@ -474,7 +530,7 @@
         matrix,
     )
     filter_two = local_call(
-        lambda *r: filter_two_kernel(og, chans, count, scale_two, False, *r),
+        lambda *r: filter_two_kernel(og, chans, count, scale_two, *r),
         shape((3 * block, all_out), F32),
         [
             pltpu.VMEM((count, all_out, width), BF16),
@@ -500,6 +556,21 @@
     )
 
 
+def spread(value, before_last=()):
+    count = lax.axis_size("chan")
+    found = {0: value}
+    bit = count // 2
+    while bit:
+        pairs = [(i, i ^ bit) for i in range(count)]
+        if bit == 1 and before_last:
+            for mask in found:
+                if mask:
+                    found[mask] = lax.optimization_barrier((found[mask], *before_last))[0]
+        found.update({mask ^ bit: lax.ppermute(item, "chan", pairs) for mask, item in found.items()})
+        bit //= 2
+    return [found[mask] for mask in range(count)]
+
+
 def square_shards(inputs, pre_act, out_grad, weight_one, weight_two):
     samples, chans, planes, cells = inputs.shape
     count = lax.axis_size("space")
@@ -517,79 +588,65 @@
     scale_one = 1.0 / math.sqrt(samples * planes * count * cells)
     scale_two = 1.0 / math.sqrt(samples * out_grad.shape[2] * count * width)
 
+    order = jnp.asarray(plane_matrix(chans, planes), BF16)
     near = out_grad.reshape(-1, width)
-    near = jnp.concatenate([near] + [ring(near, step) for step in range(1, count)], axis=0)
-    xp, hp = local_call(
-        lambda *r: split_kernel(og, planes, chans, *r),
-        [shape((planes * half, width), BF16)] * 2,
-        [],
-        2 * 2 * planes * half * width * width,
-        inputs.reshape(chans, planes * cells),
-        pre_act.reshape(chans, planes * cells),
-        matrix,
-    )
-    turn = [(a * count + b, b * count + a) for a in range(count) for b in range(count)]
-    x_turned = lax.ppermute(xp, both, turn)
-    all_hp = [hp] + [ring(hp, step) for step in range(1, count)]
-    grads = lax.all_gather(near, "chan", axis=0)
-    p_all, p_local = local_call(
-        lambda *r: all_grad_kernel(og, chans, count, *r),
-        [shape((planes * count, half, width), BF16), shape((4, half, width), BF16)],
+    around = [near] + [ring(near, step) for step in range(1, count)]
+    turn = [(mixed(j, count) * count + mixed(a, count), a * count + j) for a in range(count) for j in range(count)]
+    x_turned = lax.ppermute(inputs.reshape(chans, planes, cells), both, turn)
+    packed = local_call(pack_kernel, shape((count * near.shape[0], width), BF16), [], 0, *around)
+    gate = pre_act.reshape(chans, planes, cells)
+    gate, packed = lax.optimization_barrier((gate, packed))
+    gates = [gate] + [ring(gate, step) for step in range(1, count)]
+    grads = lax.all_gather(packed, "chan", axis=0)
+    x_all = lax.all_gather(x_turned, "chan", axis=0)
+    rows = block_rows(chans)
+    p_local, grads, act, piece = local_call(
+        lambda *r: all_grad_kernel(og, chans, count, scale_one, *r),
         [
-            pltpu.VMEM((count, all_out, width), BF16),
+            shape((4, half, width), BF16),
+            shape((count, all_out, width), BF16),
+            shape((count, planes * half, width), BF16),
+            shape((rows, all_chans), BF16),
+        ],
+        [
             pltpu.VMEM((count, planes * half, width), BF16),
             pltpu.VMEM((planes * count + 2, half, width), BF16),
-        ],
-        2 * 3 * count * block * all_out * width,
-        w2,
-        grads,
-        *all_hp,
-    )
-    near_p = [p_local]
-    bit = count // 2
-    found = {0: p_local}
-    while bit:
-        pairs = [(i, i ^ bit) for i in range(count)]
-        found.update({mask ^ bit: lax.ppermute(value, "chan", pairs) for mask, value in found.items()})
-        bit //= 2
-    near_p = [found[mask] for mask in range(count)]
-
-    x_all = lax.all_gather(x_turned, "chan", axis=0)
-    rows = block_rows(chans)
-    piece = local_call(
-        lambda *r: filter_block_kernel(og, chans, count, scale_one, *r),
-        shape((rows, all_chans), BF16),
-        [
+            pltpu.VMEM((count, planes * half, width), BF16),
             pltpu.VMEM(((planes * count + 3) * chans, 4 * width), BF16),
             pltpu.VMEM((2, block, 4 * width), BF16),
         ],
-        2 * 3 * count * block * all_chans * cells,
-        p_all,
+        2 * 3 * count * block * (all_out * width + all_chans * cells),
+        w2,
+        matrix,
+        order,
+        grads,
+        *gates,
         x_all,
     )
     pieces = []
     for step in range(count):
-        pairs = [(a * count + b, (b + step) % count * count + a) for a in range(count) for b in range(count)]
+        pairs = [(a * count + j, (j + step) % count * count + mixed(a, count)) for a in range(count) for j in range(count)]
         pieces.append(lax.ppermute(piece, both, pairs))
+    near_p = spread(p_local, pieces)
     filter_two = local_call(
-        lambda *r: filter_two_kernel(og, chans, count, scale_two, True, *r),
+        lambda *r: filter_two_square_kernel(og, chans, count, scale_two, *r),
         shape((3 * block, all_out), F32),
         [
-            pltpu.VMEM((count, all_out, width), BF16),
             pltpu.VMEM((count, block, width), BF16),
             pltpu.VMEM((count, block, width), BF16),
         ],
         2 * 3 * count * block * all_out * width,
         grads,
-        *all_hp,
+        act,
     )
     in_grad = local_call(
         lambda *r: in_grad_square_kernel(og, chans, count, *r),
-        shape((chans, planes * cells), BF16),
+        shape((chans, planes, cells), BF16),
         [pltpu.VMEM((4 * all_chans, 4 * width), BF16)],
         2 * 6 * block * all_chans * cells,
         w1,
         matrix,
+        order,
         *near_p,
     )
     filter_one = local_call(

time: 60.5 us -> 55.5 us (0.917)
  waiting for transfers between devices: 9.08 us -> 3.92 us
  blocking collectives: 18.7 us -> 16 us
  Pallas kernels: 6.93 us -> 8.91 us
  starting transfers between devices: 22.2 us -> 24 us
  local copies, waits for them, and re-layouts: 2.61 us -> 1.66 us
    ppermute x4, starting transfers between devices: 5.41 us -> 11.2 us  [square_shards(): pieces.append(lax.ppermute(piece, both, pairs))]
    ppermute x4, waiting for transfers between devices: 6.8 us -> 3.89 us  [square_shards(): pieces.append(lax.ppermute(piece, both, pairs))]
    all_gather x1, blocking collectives: 10.2 us -> 7.42 us  [square_shards(): x_all = lax.all_gather(x_turned, 'chan', axis=0)]
    ppermute x6, starting transfers between devices: 8.05 us -> 5.32 us  [ring(): lax.ppermute(value, 'space', [(i, (i + step) % count) for i in range(coun...]
    ppermute x4, waiting for transfers between devices: 2.21 us -> 0.01 us  [the longest x3 0.01 us: spread(): lax.ppermute(item, 'chan', pairs)]
    pallas_call x6 -> x5, Pallas kernels: 6.93 us -> 8.91 us  [local_call(): pl.pallas_call(kernel, out_shape=out_shape, in_specs=[pl.BlockSpec(memory...]
    ppermute x4, starting transfers between devices: 8.76 us -> 7.49 us  [the longest x1 5.8 us: square_shards(): x_turned = lax.ppermute(inputs.reshape(chans, planes, cells), both, turn)]
    reshape x1 -> x0, local copies, waits for them, and re-layouts: 0.74 us -> none  [square_shards(): in_grad.reshape(samples, chans, planes, cells)]
  transfers between devices with their start and end apart: 14 -> 14, of which waited for: 4 -> 2; matrix products, arithmetic and copies ran while one was open for 2% -> 0% of each run, Pallas kernels for 8% -> 5%
where the time goes in v2:
time: 55.5 us; the launch traced here: 55.2 us
  starting transfers between devices  24 us (43%)
  blocking collectives  16 us (29%)
  Pallas kernels  8.91 us (16%)
  waiting for transfers between devices  3.92 us (7%)
  local copies, waits for them, and re-layouts  1.66 us (3%)
  between operations  0.76 us (1%)
    ppermute x4, starting transfers between devices, square_shards(): pieces.append(lax.ppermute(piece, both, pairs))  11.2 us
    pallas_call x5, Pallas kernels, local_call(): pl.pallas_call(kernel, out_shape=out_shape, in_specs=[pl.BlockSpec(memory...  8.91 us
    all_gather x1, blocking collectives, square_shards(): grads = lax.all_gather(packed, 'chan', axis=0)  8.57 us
    all_gather x1, blocking collectives, square_shards(): x_all = lax.all_gather(x_turned, 'chan', axis=0)  7.42 us
    ppermute x1, starting transfers between devices, square_shards(): x_turned = lax.ppermute(inputs.reshape(chans, planes, cells), both, turn)  5.8 us
    ppermute x6, starting transfers between devices, ring(): lax.ppermute(value, 'space', [(i, (i + step) % count) for i in range(coun...  5.32 us
    ppermute x4, waiting for transfers between devices, square_shards(): pieces.append(lax.ppermute(piece, both, pairs))  3.89 us
    ppermute x3, starting transfers between devices, spread(): lax.ppermute(item, 'chan', pairs)  1.69 us
  transfers between devices with their start and end apart: 14, of which 2 were waited for; matrix products, arithmetic and copies ran while one was open for 0% of the time, Pallas kernels for 5%

profile of v2, /device:TPU:3, one launch (start us, length us, event | category | flops | bytes accessed | tf_op | source)
XLA Modules:
  0.0 55.2 jit_solution(12294534273343337936)
XLA Ops:
  0.6 3.4 %collective-permute-start.2 = (bf16[64,256]{1,0:T(8,128)(2,1)}, bf16[64,256]{1,0:T(8,128)(2,1)S(1)}, u32[]{:S(2)}, u32[]{:S(2)}) collective-permute-start(bf16[64,256]{1,0:T(8,128)(2,1)} %bitcast.12), channel_id=1, source_target_pairs={{0,12},{4,0},{8,4},{12,8},{1,13},{5,1},{9,5},{13,9},{2,14},{6,2},{... | collective-permute-start | bytes 98312 | tf_op jit(solution)/shard_map/ppermute | solution.py:439
  4.0 0.0 collective-permute-start.1
  4.0 0.5 collective-permute-start
  4.5 5.8 %collective-permute-start.6 = (bf16[32,2,1024]{2,1,0:T(2,128)(2,1)}, bf16[32,2,1024]{2,1,0:T(2,128)(2,1)S(1)}, u32[]{:S(2)}, u32[]{:S(2)}) collective-permute-start(bf16[32,2,1024]{2,1,0:T(2,128)(2,1)} %bitcast.24), channel_id=1, source_target_pairs={{0,0},{8,1},{4,2},{12,3},{2,4},{10,5},{6,6},{14,7},{1,8},{9,9},{5,... | collective-permute-start | bytes 393224 | tf_op jit(solution)/shard_map/ppermute | solution.py:595
  10.3 0.0 collective-permute-done.2.refs_3_
  10.3 0.0 collective-permute-done.1.refs_2_
  10.3 0.7 %copy-done = bf16[1,64,1,256]{3,1,2,0:T(8,128)(2,1)S(1)} copy-done((bf16[1,64,1,256]{3,1,2,0:T(8,128)(2,1)S(1)}, bf16[1,64,1,256]{3,1,2,0:T(8,128)(2,1)}, u32[]{:S(2)}) %copy-start) | copy-done | bytes 32792
  11.1 0.9 %copy-done.3 = bf16[1,32,2,1024]{3,2,1,0:T(2,128)(2,1)S(1)} copy-done((bf16[1,32,2,1024]{3,2,1,0:T(2,128)(2,1)S(1)}, bf16[1,32,2,1024]{3,2,1,0:T(2,128)(2,1)}, u32[]{:S(2)}) %copy-start.3) | copy-done | bytes 131096
  12.0 0.0 collective-permute-start.5
  12.0 1.5 %collective-permute-start.4 = (bf16[32,2,1024]{2,1,0:T(2,128)(2,1)S(1)}, bf16[32,2,1024]{2,1,0:T(2,128)(2,1)S(1)}, u32[]{:S(2)}, u32[]{:S(2)}) collective-permute-start(bf16[32,2,1024]{2,1,0:T(2,128)(2,1)S(1)} %bitcast.19), channel_id=1, source_target_pairs={{0,8},{4,12},{8,0},{12,4},{1,9},{5,13},{9,1},{13,5},{2,10},{6,14},... | collective-permute-start | bytes 393224 | tf_op jit(solution)/shard_map/ppermute | solution.py:439
  13.5 8.6 %all-gather = bf16[1024,256]{1,0:T(8,128)(2,1)S(1)} all-gather(bf16[256,256]{1,0:T(8,128)(2,1)S(1)} %shard_map.94), channel_id=2, replica_groups=mesh['groups'=2,'space'=4,'chan'=4] {'chan'}, dimensions={0}, use_global_device_ids=true | all-gather | bytes 655360 | tf_op jit(solution)/shard_map/all_gather | solution.py:600
  22.0 7.4 %all-gather.1 = bf16[128,2,1024]{2,1,0:T(2,128)(2,1)S(1)} all-gather(bf16[32,2,1024]{2,1,0:T(2,128)(2,1)S(1)} %collective-permute-done.6), channel_id=3, replica_groups=mesh['groups'=2,'space'=4,'chan'=4] {'chan'}, dimensions={0}, use_global_device_ids=true | all-gather | bytes 655360 | tf_op jit(solution)/shard_map/all_gather | solution.py:601
  29.5 3.9 %shard_map.95 = (bf16[4,128,256]{2,1,0:T(8,128)(2,1)S(1)}, bf16[4,256,256]{2,1,0:T(8,128)(2,1)S(1)}, bf16[4,256,256]{2,1,0:T(8,128)(2,1)S(1)}, bf16[224,128]{1,0:T(8,128)(2,1)S(1)}) custom-call(bf16[864,256]{1,0:T(8,128)(2,1)S(1)} %bitcast.16, bf16[256,256]{1,0:T(8,128)(2,1)S(1)} %copy-done.4, bf16[64,64]{1,0:T(8,128)(2,1)S(1)} %copy-done.5, ...), custom_call_target="tpu_custom_call" | custom-call | flops 1358954496 | bytes 3522560 | tf_op jit(solution)/shard_map/pallas_call | solution.py:426
  33.4 1.0 %collective-permute-start.8 = (bf16[4,128,256]{2,1,0:T(8,128)(2,1)S(1)}, bf16[4,128,256]{2,1,0:T(8,128)(2,1)S(1)}, u32[]{:S(2)}, u32[]{:S(2)}) collective-permute-start(bf16[4,128,256]{2,1,0:T(8,128)(2,1)S(1)} %get-tuple-element.12.r_3_), channel_id=1, source_target_pairs={{0,2},{1,3},{2,0},{3,1},{4,6},{5,7},{6,4},{7,5},{8,10},{9,11},{10,... | collective-permute-start | bytes 786440 | tf_op jit(solution)/shard_map/ppermute | solution.py:569
  34.4 4.0 %collective-permute-start.12 = (bf16[224,128]{1,0:T(8,128)(2,1)S(1)}, bf16[224,128]{1,0:T(8,128)(2,1)S(1)}, u32[]{:S(2)}, u32[]{:S(2)}) collective-permute-start(bf16[224,128]{1,0:T(8,128)(2,1)S(1)} %get-tuple-element.13), channel_id=1, source_target_pairs={{0,12},{1,0},{2,4},{3,8},{4,14},{5,2},{6,6},{7,10},{8,13},{9,1},{1... | collective-permute-start | bytes 172040 | tf_op jit(solution)/shard_map/ppermute | solution.py:629
  38.4 1.3 %collective-permute-start.11 = (bf16[224,128]{1,0:T(8,128)(2,1)S(1)}, bf16[224,128]{1,0:T(8,128)(2,1)S(1)}, u32[]{:S(2)}, u32[]{:S(2)}) collective-permute-start(bf16[224,128]{1,0:T(8,128)(2,1)S(1)} %get-tuple-element.13), channel_id=1, source_target_pairs={{0,8},{1,12},{2,0},{3,4},{4,10},{5,14},{6,2},{7,6},{8,9},{9,13},{1... | collective-permute-start | bytes 172040 | tf_op jit(solution)/shard_map/ppermute | solution.py:629
  39.7 1.9 %collective-permute-start.10 = (bf16[224,128]{1,0:T(8,128)(2,1)S(1)}, bf16[224,128]{1,0:T(8,128)(2,1)S(1)}, u32[]{:S(2)}, u32[]{:S(2)}) collective-permute-start(bf16[224,128]{1,0:T(8,128)(2,1)S(1)} %get-tuple-element.13), channel_id=1, source_target_pairs={{0,4},{1,8},{2,12},{3,0},{4,6},{5,10},{6,14},{7,2},{8,5},{9,9},{10... | collective-permute-start | bytes 172040 | tf_op jit(solution)/shard_map/ppermute | solution.py:629
  41.7 3.9 %collective-permute-start.9 = (bf16[224,128]{1,0:T(8,128)(2,1)S(1)}, bf16[224,128]{1,0:T(8,128)(2,1)S(1)}, u32[]{:S(2)}, u32[]{:S(2)}) collective-permute-start(bf16[224,128]{1,0:T(8,128)(2,1)S(1)} %get-tuple-element.13), channel_id=1, source_target_pairs={{0,0},{1,4},{2,8},{3,12},{4,2},{5,6},{6,10},{7,14},{8,1},{9,5},{10... | collective-permute-start | bytes 172040 | tf_op jit(solution)/shard_map/ppermute | solution.py:629
  45.6 0.7 %collective-permute-start.7 = (bf16[4,128,256]{2,1,0:T(8,128)(2,1)S(1)}, bf16[4,128,256]{2,1,0:T(8,128)(2,1)S(1)}, u32[]{:S(2)}, u32[]{:S(2)}) collective-permute-start(bf16[4,128,256]{2,1,0:T(8,128)(2,1)S(1)} %get-tuple-element.12.r_3_), channel_id=1, source_target_pairs={{0,1},{1,0},{2,3},{3,2},{4,5},{5,4},{6,7},{7,6},{8,9},{9,8},{10,11... | collective-permute-start | bytes 786440 | tf_op jit(solution)/shard_map/ppermute | solution.py:569
  46.3 0.1 collective-permute-done.10.r_1_
  46.4 3.8 %collective-permute-done.9.r_0_ = bf16[224,128]{1,0:T(8,128)(2,1)S(1)} collective-permute-done((bf16[224,128]{1,0:T(8,128)(2,1)S(1)}, bf16[224,128]{1,0:T(8,128)(2,1)S(1)}, u32[]{:S(2)}, u32[]{:S(2)}) %collective-permute-start.9) | collective-permute-done | bytes 57376 | tf_op jit(solution)/shard_map/ppermute | solution.py:629
  50.2 1.6 %shard_map.98 = f32[864,256]{1,0:T(8,128)} custom-call(bf16[4,256,256]{2,1,0:T(8,128)(2,1)S(1)} %get-tuple-element.15.r_0_, bf16[4,256,256]{2,1,0:T(8,128)(2,1)S(1)} %get-tuple-element.16.r_1_), custom_call_target="tpu_custom_call" | custom-call | flops 452984832 | bytes 1933312 | tf_op jit(solution)/shard_map/pallas_call | solution.py:426
  51.8 1.4 %shard_map.97 = f32[864,128]{1,0:T(8,128)} custom-call(bf16[224,128]{1,0:T(8,128)(2,1)S(1)} %collective-permute-done.9.r_0_, bf16[224,128]{1,0:T(8,128)(2,1)S(1)} %collective-permute-done.10.r_1_, bf16[224,128]{1,0:T(8,128)(2,1)S(1)} %collective-permute-done.11.r_2_, bf16[224,128]{1,0:T(8,128)(2,1)S(1)} %collective-permute-done.12.r_3_), custom_call_target="tpu_custom_call" | custom-call | bytes 671744 | tf_op jit(solution)/shard_map/pallas_call | solution.py:426
  53.2 2.0 %shard_map.96 = bf16[32,2,1024]{2,1,0:T(2,128)(2,1)} custom-call(bf16[864,128]{1,0:T(8,128)(2,1)S(1)} %bitcast.17, bf16[256,256]{1,0:T(8,128)(2,1)S(1)} %copy-done.4, bf16[64,64]{1,0:T(8,128)(2,1)S(1)} %copy-done.5, bf16[4,128,256]{2,1,0:T(8,128)(2,1)S(1)} %get-tuple-element.12.r_3_, bf16[4,128,256]{2,1,0:T(8,128)(2,1)S(1)} %collective-permute-done.7.r_4_, ...), custom_call_target="tpu_custom_call" | custom-call | flops 452984832 | bytes 1540096 | tf_op jit(solution)/shard_map/pallas_call | solution.py:426
  (23 shorter events, 0.1 us)
Async XLA Ops:
  0.6 9.6 %collective-permute-start.2 = (bf16[64,256]{1,0:T(8,128)(2,1)}, bf16[64,256]{1,0:T(8,128)(2,1)S(1)}, u32[]{:S(2)}, u32[]{:S(2)}) collective-permute-start(bf16[64,256]{1,0:T(8,128)(2,1)} %bitcast.12), channel_id=1, source_target_pairs={{0,12},{4,0},{8,4},{12,8},{1,13},{5,1},{9,5},{13,9},{2,14},{6,2},{... | collective-permute-start | bytes 98312 | tf_op jit(solution)/shard_map/ppermute | solution.py:439
  4.0 6.3 %collective-permute-start.1 = (bf16[64,256]{1,0:T(8,128)(2,1)}, bf16[64,256]{1,0:T(8,128)(2,1)S(1)}, u32[]{:S(2)}, u32[]{:S(2)}) collective-permute-start(bf16[64,256]{1,0:T(8,128)(2,1)} %bitcast.13), channel_id=1, source_target_pairs={{0,8},{4,12},{8,0},{12,4},{1,9},{5,13},{9,1},{13,5},{2,10},{6,14},... | collective-permute-start | bytes 98312 | tf_op jit(solution)/shard_map/ppermute | solution.py:439
  4.0 6.3 %collective-permute-start = (bf16[64,256]{1,0:T(8,128)(2,1)}, bf16[64,256]{1,0:T(8,128)(2,1)S(1)}, u32[]{:S(2)}, u32[]{:S(2)}) collective-permute-start(bf16[64,256]{1,0:T(8,128)(2,1)} %bitcast.14), channel_id=1, source_target_pairs={{0,4},{4,8},{8,12},{12,0},{1,5},{5,9},{9,13},{13,1},{2,6},{6,10},{... | collective-permute-start | bytes 98312 | tf_op jit(solution)/shard_map/ppermute | solution.py:439
  4.5 17.6 %collective-permute-start.6 = (bf16[32,2,1024]{2,1,0:T(2,128)(2,1)}, bf16[32,2,1024]{2,1,0:T(2,128)(2,1)S(1)}, u32[]{:S(2)}, u32[]{:S(2)}) collective-permute-start(bf16[32,2,1024]{2,1,0:T(2,128)(2,1)} %bitcast.24), channel_id=1, source_target_pairs={{0,0},{8,1},{4,2},{12,3},{2,4},{10,5},{6,6},{14,7},{1,8},{9,9},{5,... | collective-permute-start | bytes 393224 | tf_op jit(solution)/shard_map/ppermute | solution.py:595
  10.3 0.8 %copy-start = (bf16[1,64,1,256]{3,1,2,0:T(8,128)(2,1)S(1)}, bf16[1,64,1,256]{3,1,2,0:T(8,128)(2,1)}, u32[]{:S(2)}) copy-start(bf16[1,64,1,256]{3,1,2,0:T(8,128)(2,1)} %param.9) | copy-start | bytes 98308
  11.1 0.9 %copy-start.3 = (bf16[1,32,2,1024]{3,2,1,0:T(2,128)(2,1)S(1)}, bf16[1,32,2,1024]{3,2,1,0:T(2,128)(2,1)}, u32[]{:S(2)}) copy-start(bf16[1,32,2,1024]{3,2,1,0:T(2,128)(2,1)} %param.8) | copy-start | bytes 393220
  12.0 17.5 %collective-permute-start.5 = (bf16[32,2,1024]{2,1,0:T(2,128)(2,1)S(1)}, bf16[32,2,1024]{2,1,0:T(2,128)(2,1)S(1)}, u32[]{:S(2)}, u32[]{:S(2)}) collective-permute-start(bf16[32,2,1024]{2,1,0:T(2,128)(2,1)S(1)} %bitcast.18), channel_id=1, source_target_pairs={{0,12},{4,0},{8,4},{12,8},{1,13},{5,1},{9,5},{13,9},{2,14},{6,2},{... | collective-permute-start | bytes 393224 | tf_op jit(solution)/shard_map/ppermute | solution.py:439
  12.0 17.5 %collective-permute-start.4 = (bf16[32,2,1024]{2,1,0:T(2,128)(2,1)S(1)}, bf16[32,2,1024]{2,1,0:T(2,128)(2,1)S(1)}, u32[]{:S(2)}, u32[]{:S(2)}) collective-permute-start(bf16[32,2,1024]{2,1,0:T(2,128)(2,1)S(1)} %bitcast.19), channel_id=1, source_target_pairs={{0,8},{4,12},{8,0},{12,4},{1,9},{5,13},{9,1},{13,5},{2,10},{6,14},... | collective-permute-start | bytes 393224 | tf_op jit(solution)/shard_map/ppermute | solution.py:439
  13.5 16.0 %collective-permute-start.3 = (bf16[32,2,1024]{2,1,0:T(2,128)(2,1)S(1)}, bf16[32,2,1024]{2,1,0:T(2,128)(2,1)S(1)}, u32[]{:S(2)}, u32[]{:S(2)}) collective-permute-start(bf16[32,2,1024]{2,1,0:T(2,128)(2,1)S(1)} %bitcast.20), channel_id=1, source_target_pairs={{0,4},{4,8},{8,12},{12,0},{1,5},{5,9},{9,13},{13,1},{2,6},{6,10},{... | collective-permute-start | bytes 393224 | tf_op jit(solution)/shard_map/ppermute | solution.py:439
  22.0 7.5 %copy-start.1 = (bf16[3,3,3,32,256]{4,3,2,1,0:T(8,128)(2,1)S(1)}, bf16[3,3,3,32,256]{4,3,2,1,0:T(8,128)(2,1)}, u32[]{:S(2)}) copy-start(bf16[3,3,3,32,256]{4,3,2,1,0:T(8,128)(2,1)} %param.11) | copy-start | bytes 1327108
  22.0 7.5 %copy-start.4 = (bf16[256,256]{1,0:T(8,128)(2,1)S(1)}, bf16[256,256]{1,0:T(8,128)(2,1)}, u32[]{:S(2)}) copy-start(bf16[256,256]{1,0:T(8,128)(2,1)} %constant.4.clone.r_1_) | copy-start | bytes 393220
  22.0 7.5 %copy-start.5 = (bf16[64,64]{1,0:T(8,128)(2,1)S(1)}, bf16[64,64]{1,0:T(8,128)(2,1)}, u32[]{:S(2)}) copy-start(bf16[64,64]{1,0:T(8,128)(2,1)} %constant.5.clone.r_2_) | copy-start | bytes 24580
  33.4 16.8 %collective-permute-start.8 = (bf16[4,128,256]{2,1,0:T(8,128)(2,1)S(1)}, bf16[4,128,256]{2,1,0:T(8,128)(2,1)S(1)}, u32[]{:S(2)}, u32[]{:S(2)}) collective-permute-start(bf16[4,128,256]{2,1,0:T(8,128)(2,1)S(1)} %get-tuple-element.12.r_3_), channel_id=1, source_target_pairs={{0,2},{1,3},{2,0},{3,1},{4,6},{5,7},{6,4},{7,5},{8,10},{9,11},{10,... | collective-permute-start | bytes 786440 | tf_op jit(solution)/shard_map/ppermute | solution.py:569
  34.4 11.2 %collective-permute-start.12 = (bf16[224,128]{1,0:T(8,128)(2,1)S(1)}, bf16[224,128]{1,0:T(8,128)(2,1)S(1)}, u32[]{:S(2)}, u32[]{:S(2)}) collective-permute-start(bf16[224,128]{1,0:T(8,128)(2,1)S(1)} %get-tuple-element.13), channel_id=1, source_target_pairs={{0,12},{1,0},{2,4},{3,8},{4,14},{5,2},{6,6},{7,10},{8,13},{9,1},{1... | collective-permute-start | bytes 172040 | tf_op jit(solution)/shard_map/ppermute | solution.py:629
  38.4 7.9 %collective-permute-start.11 = (bf16[224,128]{1,0:T(8,128)(2,1)S(1)}, bf16[224,128]{1,0:T(8,128)(2,1)S(1)}, u32[]{:S(2)}, u32[]{:S(2)}) collective-permute-start(bf16[224,128]{1,0:T(8,128)(2,1)S(1)} %get-tuple-element.13), channel_id=1, source_target_pairs={{0,8},{1,12},{2,0},{3,4},{4,10},{5,14},{6,2},{7,6},{8,9},{9,13},{1... | collective-permute-start | bytes 172040 | tf_op jit(solution)/shard_map/ppermute | solution.py:629
  39.7 6.7 %collective-permute-start.10 = (bf16[224,128]{1,0:T(8,128)(2,1)S(1)}, bf16[224,128]{1,0:T(8,128)(2,1)S(1)}, u32[]{:S(2)}, u32[]{:S(2)}) collective-permute-start(bf16[224,128]{1,0:T(8,128)(2,1)S(1)} %get-tuple-element.13), channel_id=1, source_target_pairs={{0,4},{1,8},{2,12},{3,0},{4,6},{5,10},{6,14},{7,2},{8,5},{9,9},{10... | collective-permute-start | bytes 172040 | tf_op jit(solution)/shard_map/ppermute | solution.py:629
  41.7 8.6 %collective-permute-start.9 = (bf16[224,128]{1,0:T(8,128)(2,1)S(1)}, bf16[224,128]{1,0:T(8,128)(2,1)S(1)}, u32[]{:S(2)}, u32[]{:S(2)}) collective-permute-start(bf16[224,128]{1,0:T(8,128)(2,1)S(1)} %get-tuple-element.13), channel_id=1, source_target_pairs={{0,0},{1,4},{2,8},{3,12},{4,2},{5,6},{6,10},{7,14},{8,1},{9,5},{10... | collective-permute-start | bytes 172040 | tf_op jit(solution)/shard_map/ppermute | solution.py:629
  45.6 7.5 %collective-permute-start.7 = (bf16[4,128,256]{2,1,0:T(8,128)(2,1)S(1)}, bf16[4,128,256]{2,1,0:T(8,128)(2,1)S(1)}, u32[]{:S(2)}, u32[]{:S(2)}) collective-permute-start(bf16[4,128,256]{2,1,0:T(8,128)(2,1)S(1)} %get-tuple-element.12.r_3_), channel_id=1, source_target_pairs={{0,1},{1,0},{2,3},{3,2},{4,5},{5,4},{6,7},{7,6},{8,9},{9,8},{10,11... | collective-permute-start | bytes 786440 | tf_op jit(solution)/shard_map/ppermute | solution.py:569
  50.2 3.0 %collective-permute-start.13 = (bf16[4,128,256]{2,1,0:T(8,128)(2,1)S(1)}, bf16[4,128,256]{2,1,0:T(8,128)(2,1)S(1)}, u32[]{:S(2)}, u32[]{:S(2)}) collective-permute-start(bf16[4,128,256]{2,1,0:T(8,128)(2,1)S(1)} %collective-permute-done.8.r_5_), channel_id=1, source_target_pairs={{0,1},{1,0},{2,3},{3,2},{4,5},{5,4},{6,7},{7,6},{8,9},{9,8},{10,11... | collective-permute-start | bytes 786440 | tf_op jit(solution)/shard_map/ppermute | solution.py:569
  51.8 1.4 %copy-start.2 = (bf16[3,3,3,32,128]{4,3,2,1,0:T(8,128)(2,1)S(1)}, bf16[3,3,3,32,128]{4,3,2,1,0:T(8,128)(2,1)}, u32[]{:S(2)}) copy-start(bf16[3,3,3,32,128]{4,3,2,1,0:T(8,128)(2,1)} %param.10) | copy-start | bytes 663556

commit v3 on v2

--- a/solution.py
+++ b/solution.py
@@ -36,6 +36,22 @@
 
 def leaky(value, gate):
     return jnp.where(gate > 0, value, leak_slope * value)
+
+
+def lane_matrix(og):
+    width = og * og
+    cell = lax.broadcasted_iota(jnp.int32, (width, width), 0)
+    place = lax.broadcasted_iota(jnp.int32, (width, width), 1)
+    row, col = cell // (2 * og), cell % (2 * og)
+    target = (row % 2 * 2 + col % 2) * (width // 4) + row // 2 * og + col // 2
+    return jnp.where(place == target, 1.0, 0.0).astype(BF16)
+
+
+def order_matrix(chans, planes):
+    rows = chans * planes
+    place = lax.broadcasted_iota(jnp.int32, (rows, rows), 0)
+    row = lax.broadcasted_iota(jnp.int32, (rows, rows), 1)
+    return jnp.where(place == row % planes * chans + row // planes, 1.0, 0.0).astype(BF16)
 
 
 def split_matrix(og):
@@ -183,12 +199,12 @@
                 p_scr[at : at + chans, parity * width : (parity + 1) * width] = source[
                     j, (first * 4 + parity) * chans : (first * 4 + parity + 1) * chans, :
                 ]
-    joined = in_grad_planes(og, chans, all_chans, w_ref, e_ref, p_scr)
+    joined = in_grad_planes(og, chans, all_chans, w_ref, e_ref[...], p_scr)
     for i in range(8):
         out_ref[:, i * width : (i + 1) * width] = joined[i * chans : (i + 1) * chans].astype(BF16)
 
 
-def in_grad_planes(og, chans, all_chans, w_ref, e_ref, p_scr):
+def in_grad_planes(og, chans, all_chans, w_ref, matrix, p_scr):
     width = og * og
     part = width // 4
     block = 9 * chans
@@ -219,7 +235,7 @@
             stacked.append(
                 jnp.concatenate([value[:, i * part : (i + 1) * part] for value in sums], axis=1).astype(BF16)
             )
-    return lax.dot_general(jnp.concatenate(stacked, axis=0), e_ref[...], CONTRACT_LAST, preferred_element_type=F32)
+    return lax.dot_general(jnp.concatenate(stacked, axis=0), matrix, CONTRACT_LAST, preferred_element_type=F32)
 
 
 def filter_two_kernel(og, chans, count, scale, *refs):
@@ -268,12 +284,6 @@
         at = pl.multiple_of(lax.rem(s + count - step, count) * rows, 16)
         scr[pl.ds(at, rows), :] = piece[...].astype(F32)
     out_ref[...] = scr[0 : out_ref.shape[0], :]
-
-
-def plane_matrix(chans, planes):
-    row = np.arange(chans * planes)
-    place = (row % planes) * chans + row // planes
-    return (place[None, :] == np.arange(chans * planes)[:, None]).astype(np.float32)
 
 
 def split_planes(value, order, matrix, chans, planes, og):
@@ -302,18 +312,25 @@
         out_ref[step * rows : (step + 1) * rows, :] = source[...]
 
 
-def all_grad_kernel(og, chans, count, scale, w_ref, e_ref, order_ref, *refs):
-    grads, gates, x_all, refs = refs[0], refs[1 : count + 1], refs[count + 1], refs[count + 2 :]
+def gate_kernel(og, chans, h_ref, out_ref):
+    value = split_planes(h_ref[...], order_matrix(chans, 2), lane_matrix(og), chans, 2, og)
+    out_ref[...] = value.astype(BF16)
+
+
+def all_grad_kernel(og, chans, count, scale, w_ref, *refs):
+    grads, gates, sources, refs = refs[0], refs[1 : count + 1], refs[count + 1 : 2 * count + 1], refs[2 * count + 1 :]
     local_ref, g_ref, act_ref, piece_ref, h_scr, p_scr, *block_refs = refs
+    matrix, order = lane_matrix(og), order_matrix(chans, 2)
     s = lax.axis_index("space")
     half = 4 * chans
     part = grads.shape[1] // count
     for step in range(count):
-        at = lax.rem(s + count - step, count)
+        at = lax.bitwise_xor(s, step)
         for j in range(count):
             g_ref[at, j * part : (j + 1) * part, :] = grads[j, step * part : (step + 1) * part, :]
-        value = split_planes(gates[step][...], order_ref[...], e_ref[...], chans, 2, og)
-        h_scr[at] = value.astype(BF16)
+        value = gates[step][...]
+        h_scr[at] = value
+        value = value.astype(F32)
         act_ref[at] = leaky(value, value).astype(BF16)
     empty = jnp.zeros((half, og * og), BF16)
     p_scr[0] = empty
@@ -324,7 +341,7 @@
         after = g_ref[q + 1] if q < count - 1 else jnp.zeros_like(here)
         plane_grad(w_ref, here, after, h_scr[q, half : 2 * half, :], chans, og, p_scr.at[2 * q + 2], 0, None)
     local_ref[...] = p_scr[pl.ds(2 * s, 4)]
-    filter_block(og, chans, count, scale, p_scr, e_ref, order_ref, x_all, piece_ref, *block_refs)
+    filter_block(og, chans, count, scale, p_scr, matrix, order, sources, piece_ref, *block_refs)
 
 
 def mixed(index, count):
@@ -335,15 +352,16 @@
     return -(-27 * chans // 64) * 16
 
 
-def filter_block(og, chans, count, scale, p_ref, e_ref, order_ref, source, out_ref, x_ref, p_scr, x_scr):
+def filter_block(og, chans, count, scale, p_ref, matrix, order, sources, out_ref, x_ref, p_scr, x_scr):
+    i = lax.axis_index("chan")
     width = og * og
     half = 4 * chans
     block = 9 * chans
     lanes = 4 * chans
     planes = 2 * count
-    for j in range(count):
-        value = split_planes(source[j], order_ref[...], e_ref[...], chans, 2, og)
-        x_ref[mixed(j, count)] = value.astype(BF16)
+    for mask, source in enumerate(sources):
+        value = split_planes(source[...], order, matrix, chans, 2, og)
+        x_ref[mixed(lax.bitwise_xor(i, mask), count)] = value.astype(BF16)
     empty = jnp.zeros((chans, 4 * width), BF16)
     for index in (0, planes + 1, planes + 2):
         p_scr[index * chans : (index + 1) * chans, :] = empty
@@ -373,7 +391,18 @@
     out_ref[...] = jnp.where(lane < 3 * chans, total[:rows], jnp.concatenate(moved_tail, axis=0)).astype(BF16)
 
 
-def join_kernel(chans, count, *refs):
+def join_matrix(chans, count):
+    lanes = 4 * chans
+    result = np.zeros((count * lanes, 4 * lanes), np.float32)
+    for j in range(count):
+        for group in range(4):
+            target = 2 - group if group < 3 else 3
+            for c in range(chans):
+                result[j * lanes + group * chans + c, target * lanes + j * chans + c] = 1
+    return result
+
+
+def join_kernel(chans, count, m_ref, *refs):
     pieces, out_ref, scr = refs[:count], refs[count], refs[count + 1]
     s = lax.axis_index("space")
     lanes = 4 * chans
@@ -381,23 +410,16 @@
     rows = block_rows(chans)
     rest = block - rows
     for step, piece in enumerate(pieces):
-        scr[step] = piece[...].astype(F32)
-    group = lax.broadcasted_iota(jnp.int32, (block, lanes), 1) // chans
-    sums = [jnp.zeros((block, lanes), F32) for _ in range(3)]
-    for j in range(count):
-        value = scr[lax.rem(s + count - j, count)]
-        tail = [pltpu.roll(value[i * rest : (i + 1) * rest], (i + 1) * chans, 1) for i in range(3)]
-        tail = jnp.where(group[:rest] == 0, tail[0], jnp.where(group[:rest] == 1, tail[1], tail[2]))
-        whole = jnp.concatenate([value, tail], axis=0)
-        for depth in range(3):
-            shift = (j - (2 - depth)) * chans % lanes
-            placed = pltpu.roll(whole, shift, 1) if shift else whole
-            sums[depth] = jnp.where(group == j, placed, sums[depth])
+        scr[step] = piece[...]
+    side = jnp.concatenate([scr[lax.bitwise_xor(s, j)] for j in range(count)], axis=1)
+    joined = jnp.dot(side, m_ref[...], preferred_element_type=F32)
     for depth in range(3):
-        out_ref[depth * block : (depth + 1) * block, :] = sums[depth]
-
-
-def in_grad_square_kernel(og, chans, count, w_ref, e_ref, order_ref, *refs):
+        out_ref[depth * block : depth * block + rows, :] = joined[:, depth * lanes : (depth + 1) * lanes]
+        at = (2 - depth) * rest
+        out_ref[depth * block + rows : (depth + 1) * block, :] = joined[at : at + rest, 3 * lanes :]
+
+
+def in_grad_square_kernel(og, chans, count, w_ref, *refs):
     sources, out_ref, p_scr = refs[:count], refs[count], refs[count + 1]
     i = lax.axis_index("chan")
     width = og * og
@@ -410,13 +432,13 @@
                 p_scr[pl.ds(at, chans), parity * width : (parity + 1) * width] = source[
                     index, parity * chans : (parity + 1) * chans, :
                 ]
-    joined = in_grad_planes(og, chans, all_chans, w_ref, e_ref, p_scr)
+    joined = in_grad_planes(og, chans, all_chans, w_ref, lane_matrix(og), p_scr)
     rows = [
         jnp.concatenate([joined[(plane * 4 + k) * chans : (plane * 4 + k + 1) * chans] for k in range(4)], axis=1)
         for plane in range(2)
     ]
     value = jnp.concatenate(rows, axis=0).astype(BF16)
-    value = lax.dot_general(order_ref[...], value, (((0,), (0,)), ((), ())), preferred_element_type=F32)
+    value = lax.dot_general(order_matrix(chans, 2), value, (((0,), (0,)), ((), ())), preferred_element_type=F32)
     out_ref[...] = value.astype(BF16).reshape(out_ref.shape)
 
 
@@ -571,6 +593,10 @@
     return [found[mask] for mask in range(count)]
 
 
+def paired(value, mask):
+    return lax.ppermute(value, "space", [(i, i ^ mask) for i in range(lax.axis_size("space"))])
+
+
 def square_shards(inputs, pre_act, out_grad, weight_one, weight_two):
     samples, chans, planes, cells = inputs.shape
     count = lax.axis_size("space")
@@ -582,23 +608,26 @@
     all_out = weight_two.shape[4]
     w1 = weight_one.reshape(3 * block, all_chans)
     w2 = weight_two.reshape(3 * block, all_out)
-    matrix = jnp.asarray(split_matrix(og), BF16)
     shape = jax.ShapeDtypeStruct
     both = ("space", "chan")
     scale_one = 1.0 / math.sqrt(samples * planes * count * cells)
     scale_two = 1.0 / math.sqrt(samples * out_grad.shape[2] * count * width)
 
-    order = jnp.asarray(plane_matrix(chans, planes), BF16)
     near = out_grad.reshape(-1, width)
-    around = [near] + [ring(near, step) for step in range(1, count)]
+    around = [near] + [paired(near, step) for step in range(1, count)]
     turn = [(mixed(j, count) * count + mixed(a, count), a * count + j) for a in range(count) for j in range(count)]
     x_turned = lax.ppermute(inputs.reshape(chans, planes, cells), both, turn)
     packed = local_call(pack_kernel, shape((count * near.shape[0], width), BF16), [], 0, *around)
-    gate = pre_act.reshape(chans, planes, cells)
-    gate, packed = lax.optimization_barrier((gate, packed))
-    gates = [gate] + [ring(gate, step) for step in range(1, count)]
+    gate = local_call(
+        lambda *r: gate_kernel(og, chans, *r),
+        shape((planes * half, width), BF16),
+        [],
+        2 * planes * half * width * width,
+        pre_act.reshape(chans, planes, cells),
+    )
+    gates = [gate] + [paired(gate, step) for step in range(1, count)]
     grads = lax.all_gather(packed, "chan", axis=0)
-    x_all = lax.all_gather(x_turned, "chan", axis=0)
+    x_all = spread(x_turned, (grads, *gates[1:]))
     rows = block_rows(chans)
     p_local, grads, act, piece = local_call(
         lambda *r: all_grad_kernel(og, chans, count, scale_one, *r),
@@ -617,17 +646,14 @@
         ],
         2 * 3 * count * block * (all_out * width + all_chans * cells),
         w2,
-        matrix,
-        order,
         grads,
         *gates,
-        x_all,
+        *x_all,
     )
     pieces = []
     for step in range(count):
-        pairs = [(a * count + j, (j + step) % count * count + mixed(a, count)) for a in range(count) for j in range(count)]
+        pairs = [(a * count + j, (j ^ step) * count + mixed(a, count)) for a in range(count) for j in range(count)]
         pieces.append(lax.ppermute(piece, both, pairs))
-    near_p = spread(p_local, pieces)
     filter_two = local_call(
         lambda *r: filter_two_square_kernel(og, chans, count, scale_two, *r),
         shape((3 * block, all_out), F32),
@@ -639,21 +665,21 @@
         grads,
         act,
     )
+    near_p = spread(p_local, (*pieces, filter_two))
     in_grad = local_call(
         lambda *r: in_grad_square_kernel(og, chans, count, *r),
         shape((chans, planes, cells), BF16),
         [pltpu.VMEM((4 * all_chans, 4 * width), BF16)],
         2 * 6 * block * all_chans * cells,
         w1,
-        matrix,
-        order,
         *near_p,
     )
     filter_one = local_call(
         lambda *r: join_kernel(chans, count, *r),
         shape((3 * block, all_chans), F32),
-        [pltpu.VMEM((count, rows, all_chans), F32)],
-        0,
+        [pltpu.VMEM((count, rows, all_chans), BF16)],
+        2 * rows * 16 * all_chans * all_chans,
+        jnp.asarray(join_matrix(chans, count), BF16),
         *pieces,
     )
     return (
@@ -665,7 +691,7 @@
 
 def shards(*arguments):
     count = lax.axis_size("space")
-    square = count == lax.axis_size("chan") and 4 * arguments[0].shape[1] == arguments[3].shape[4]
+    square = count == lax.axis_size("chan") and count & (count - 1) == 0 and 4 * arguments[0].shape[1] == arguments[3].shape[4]
     return (square_shards if square else ring_shards)(*arguments)
 
 

time: 55.5 us -> 49 us (0.88)
  blocking collectives: 16 us -> 9.41 us
  starting transfers between devices: 24 us -> 25 us
  local copies, waits for them, and re-layouts: 1.66 us -> 0.92 us
    all_gather x1 -> x0, blocking collectives: 7.42 us -> none  [square_shards(): x_all = lax.all_gather(x_turned, 'chan', axis=0)]
    ppermute x6, starting transfers between devices: 5.32 us -> 7.22 us  [paired(): lax.ppermute(value, 'space', [(i, i ^ mask) for i in range(lax.axis_size(...]
    ppermute x4, starting transfers between devices: 11.2 us -> 9.69 us  [square_shards(): pieces.append(lax.ppermute(piece, both, pairs))]
    ppermute x3 -> x6, waiting for transfers between devices: 0.01 us -> 1.11 us  [spread(): lax.ppermute(item, 'chan', pairs)]
    ppermute x4, waiting for transfers between devices: 3.89 us -> 2.88 us  [square_shards(): pieces.append(lax.ppermute(piece, both, pairs))]
    all_gather x1, blocking collectives: 8.57 us -> 9.41 us  [square_shards(): grads = lax.all_gather(packed, 'chan', axis=0)]
    unnamed x12 -> x10, local copies, waits for them, and re-layouts: 1.66 us -> 0.92 us
    ppermute x3 -> x6, starting transfers between devices: 1.69 us -> 2.31 us  [spread(): lax.ppermute(item, 'chan', pairs)]
  transfers between devices with their start and end apart: 14 -> 17, of which waited for: 2 -> 5; matrix products, arithmetic and copies ran while one was open for 0% -> 0% of each run, Pallas kernels for 5% -> 6%
where the time goes in v3:
time: 49 us; the launch traced here: 48.8 us
  starting transfers between devices  25 us (51%)
  blocking collectives  9.41 us (19%)
  Pallas kernels  8.79 us (18%)
  waiting for transfers between devices  4 us (8%)
  local copies, waits for them, and re-layouts  0.92 us (2%)
  between operations  0.74 us (2%)
    ppermute x4, starting transfers between devices, square_shards(): pieces.append(lax.ppermute(piece, both, pairs))  9.69 us
    all_gather x1, blocking collectives, square_shards(): grads = lax.all_gather(packed, 'chan', axis=0)  9.41 us
    pallas_call x6, Pallas kernels, local_call(): pl.pallas_call(kernel, out_shape=out_shape, in_specs=[pl.BlockSpec(memory...  8.79 us
    ppermute x6, starting transfers between devices, paired(): lax.ppermute(value, 'space', [(i, i ^ mask) for i in range(lax.axis_size(...  7.22 us
    ppermute x1, starting transfers between devices, square_shards(): x_turned = lax.ppermute(inputs.reshape(chans, planes, cells), both, turn)  5.76 us
    ppermute x4, waiting for transfers between devices, square_shards(): pieces.append(lax.ppermute(piece, both, pairs))  2.88 us
    ppermute x6, starting transfers between devices, spread(): lax.ppermute(item, 'chan', pairs)  2.31 us
    ppermute x6, waiting for transfers between devices, spread(): lax.ppermute(item, 'chan', pairs)  1.11 us
  transfers between devices with their start and end apart: 17, of which 5 were waited for; matrix products, arithmetic and copies ran while one was open for 0% of the time, Pallas kernels for 6%

profile of v3, /device:TPU:3, one launch (start us, length us, event | category | flops | bytes accessed | tf_op | source)
XLA Modules:
  0.0 48.8 jit_solution(14421261079136716450)
XLA Ops:
  0.6 5.8 %collective-permute-start.6 = (bf16[32,2,1024]{2,1,0:T(2,128)(2,1)}, bf16[32,2,1024]{2,1,0:T(2,128)(2,1)S(1)}, u32[]{:S(2)}, u32[]{:S(2)}) collective-permute-start(bf16[32,2,1024]{2,1,0:T(2,128)(2,1)} %bitcast.19), channel_id=1, source_target_pairs={{0,0},{8,1},{4,2},{12,3},{2,4},{10,5},{6,6},{14,7},{1,8},{9,9},{5,... | collective-permute-start | bytes 393224 | tf_op jit(solution)/shard_map/ppermute | solution.py:619
  6.5 1.5 %collective-permute-start.1 = (bf16[64,256]{1,0:T(8,128)(2,1)}, bf16[64,256]{1,0:T(8,128)(2,1)S(1)}, u32[]{:S(2)}, u32[]{:S(2)}) collective-permute-start(bf16[64,256]{1,0:T(8,128)(2,1)} %bitcast.12), channel_id=1, source_target_pairs={{0,8},{4,12},{8,0},{12,4},{1,9},{5,13},{9,1},{13,5},{2,10},{6,14},... | collective-permute-start | bytes 98312 | tf_op jit(solution)/shard_map/ppermute | solution.py:597
  8.0 2.1 %collective-permute-start = (bf16[64,256]{1,0:T(8,128)(2,1)}, bf16[64,256]{1,0:T(8,128)(2,1)S(1)}, u32[]{:S(2)}, u32[]{:S(2)}) collective-permute-start(bf16[64,256]{1,0:T(8,128)(2,1)} %bitcast.13), channel_id=1, source_target_pairs={{0,4},{4,0},{8,12},{12,8},{1,5},{5,1},{9,13},{13,9},{2,6},{6,2},{1... | collective-permute-start | bytes 98312 | tf_op jit(solution)/shard_map/ppermute | solution.py:597
  10.0 0.9 %copy-done.1 = bf16[1,32,2,1024]{3,2,1,0:T(2,128)(2,1)S(1)} copy-done((bf16[1,32,2,1024]{3,2,1,0:T(2,128)(2,1)S(1)}, bf16[1,32,2,1024]{3,2,1,0:T(2,128)(2,1)}, u32[]{:S(2)}) %copy-start.1) | copy-done | bytes 131096
  10.9 0.4 shard_map.86.r_2_
  11.3 0.1 collective-permute-start.5
  11.5 2.9 %collective-permute-start.4 = (bf16[256,256]{1,0:T(8,128)(2,1)S(1)}, bf16[256,256]{1,0:T(8,128)(2,1)S(1)}, u32[]{:S(2)}, u32[]{:S(2)}) collective-permute-start(bf16[256,256]{1,0:T(8,128)(2,1)S(1)} %shard_map.86.r_2_), channel_id=1, source_target_pairs={{0,8},{4,12},{8,0},{12,4},{1,9},{5,13},{9,1},{13,5},{2,10},{6,14},... | collective-permute-start | bytes 393224 | tf_op jit(solution)/shard_map/ppermute | solution.py:597
  14.4 0.5 %collective-permute-start.3 = (bf16[256,256]{1,0:T(8,128)(2,1)S(1)}, bf16[256,256]{1,0:T(8,128)(2,1)S(1)}, u32[]{:S(2)}, u32[]{:S(2)}) collective-permute-start(bf16[256,256]{1,0:T(8,128)(2,1)S(1)} %shard_map.86.r_2_), channel_id=1, source_target_pairs={{0,4},{4,0},{8,12},{12,8},{1,5},{5,1},{9,13},{13,9},{2,6},{6,2},{1... | collective-permute-start | bytes 393224 | tf_op jit(solution)/shard_map/ppermute | solution.py:597
  15.1 9.4 %all-gather = bf16[1024,256]{1,0:T(8,128)(2,1)S(1)} all-gather(bf16[256,256]{1,0:T(8,128)(2,1)S(1)} %shard_map.85), channel_id=2, replica_groups=mesh['groups'=2,'space'=4,'chan'=4] {'chan'}, dimensions={0}, use_global_device_ids=true | all-gather | bytes 655360 | tf_op jit(solution)/shard_map/all_gather | solution.py:629
  24.5 0.2 collective-permute-start.7
  24.6 0.4 collective-permute-start.9
  25.1 0.7 %collective-permute-done.7.r_7_ = bf16[32,2,1024]{2,1,0:T(2,128)(2,1)S(1)} collective-permute-done((bf16[32,2,1024]{2,1,0:T(2,128)(2,1)S(1)}, bf16[32,2,1024]{2,1,0:T(2,128)(2,1)S(1)}, u32[]{:S(2)}, u32[]{:S(2)}) %collective-permute-start.7) | collective-permute-done | bytes 131104 | tf_op jit(solution)/shard_map/ppermute | solution.py:591
  25.8 0.3 collective-permute-done.9.r_9_
  26.1 3.7 %shard_map.87 = (bf16[4,128,256]{2,1,0:T(8,128)(2,1)S(1)}, bf16[4,256,256]{2,1,0:T(8,128)(2,1)S(1)}, bf16[4,256,256]{2,1,0:T(8,128)(2,1)S(1)}, bf16[224,128]{1,0:T(8,128)(2,1)S(1)}) custom-call(bf16[864,256]{1,0:T(8,128)(2,1)S(1)} %bitcast.15, bf16[4,256,256]{2,1,0:T(8,128)(2,1)S(1)} %bitcast.9, bf16[256,256]{1,0:T(8,128)(2,1)S(1)} %shard_map.86.r_2_, ...), custom_call_target="tpu_custom_call" | custom-call | flops 1358954496 | bytes 3383296 | tf_op jit(solution)/shard_map/pallas_call | solution.py:448
  29.9 3.8 %collective-permute-start.15 = (bf16[224,128]{1,0:T(8,128)(2,1)S(1)}, bf16[224,128]{1,0:T(8,128)(2,1)S(1)}, u32[]{:S(2)}, u32[]{:S(2)}) collective-permute-start(bf16[224,128]{1,0:T(8,128)(2,1)S(1)} %get-tuple-element.11), channel_id=1, source_target_pairs={{0,12},{1,8},{2,4},{3,0},{4,14},{5,10},{6,6},{7,2},{8,13},{9,9},{1... | collective-permute-start | bytes 172040 | tf_op jit(solution)/shard_map/ppermute | solution.py:656
  33.7 2.4 %collective-permute-start.14 = (bf16[224,128]{1,0:T(8,128)(2,1)S(1)}, bf16[224,128]{1,0:T(8,128)(2,1)S(1)}, u32[]{:S(2)}, u32[]{:S(2)}) collective-permute-start(bf16[224,128]{1,0:T(8,128)(2,1)S(1)} %get-tuple-element.11), channel_id=1, source_target_pairs={{0,8},{1,12},{2,0},{3,4},{4,10},{5,14},{6,2},{7,6},{8,9},{9,13},{1... | collective-permute-start | bytes 172040 | tf_op jit(solution)/shard_map/ppermute | solution.py:656
  36.1 3.5 %collective-permute-start.12 = (bf16[224,128]{1,0:T(8,128)(2,1)S(1)}, bf16[224,128]{1,0:T(8,128)(2,1)S(1)}, u32[]{:S(2)}, u32[]{:S(2)}) collective-permute-start(bf16[224,128]{1,0:T(8,128)(2,1)S(1)} %get-tuple-element.11), channel_id=1, source_target_pairs={{0,0},{1,4},{2,8},{3,12},{4,2},{5,6},{6,10},{7,14},{8,1},{9,5},{10... | collective-permute-start | bytes 172040 | tf_op jit(solution)/shard_map/ppermute | solution.py:656
  39.6 1.6 %shard_map.88 = f32[864,256]{1,0:T(8,128)} custom-call(bf16[4,256,256]{2,1,0:T(8,128)(2,1)S(1)} %get-tuple-element.12.r_0_, bf16[4,256,256]{2,1,0:T(8,128)(2,1)S(1)} %get-tuple-element.13.r_1_), custom_call_target="tpu_custom_call" | custom-call | flops 452984832 | bytes 1933312 | tf_op jit(solution)/shard_map/pallas_call | solution.py:448
  41.2 0.4 collective-permute-start.10
  41.6 0.3 collective-permute-done.13.r_2_
  41.9 2.6 %collective-permute-done.12.r_1_ = bf16[224,128]{1,0:T(8,128)(2,1)S(1)} collective-permute-done((bf16[224,128]{1,0:T(8,128)(2,1)S(1)}, bf16[224,128]{1,0:T(8,128)(2,1)S(1)}, u32[]{:S(2)}, u32[]{:S(2)}) %collective-permute-start.12) | collective-permute-done | bytes 57376 | tf_op jit(solution)/shard_map/ppermute | solution.py:656
  44.5 1.1 %collective-permute-start.16 = (bf16[4,128,256]{2,1,0:T(8,128)(2,1)S(1)}, bf16[4,128,256]{2,1,0:T(8,128)(2,1)S(1)}, u32[]{:S(2)}, u32[]{:S(2)}) collective-permute-start(bf16[4,128,256]{2,1,0:T(8,128)(2,1)S(1)} %collective-permute-done.11.r_3_), channel_id=1, source_target_pairs={{0,1},{1,0},{2,3},{3,2},{4,5},{5,4},{6,7},{7,6},{8,9},{9,8},{10,11... | collective-permute-start | bytes 786440 | tf_op jit(solution)/shard_map/ppermute | solution.py:591
  45.6 1.1 %shard_map.90 = f32[864,128]{1,0:T(8,128)} custom-call(bf16[512,512]{1,0:T(8,128)(2,1)S(1)} %copy-done, bf16[224,128]{1,0:T(8,128)(2,1)S(1)} %collective-permute-done.12.r_1_, bf16[224,128]{1,0:T(8,128)(2,1)S(1)} %collective-permute-done.13.r_2_, bf16[224,128]{1,0:T(8,128)(2,1)S(1)} %collective-permute-done.14.r_3_, ...), custom_call_target="tpu_custom_call" | custom-call | flops 117440512 | bytes 1196032 | tf_op jit(solution)/shard_map/pallas_call | solution.py:448
  46.8 2.0 %shard_map.89 = bf16[32,2,1024]{2,1,0:T(2,128)(2,1)} custom-call(bf16[864,128]{1,0:T(8,128)(2,1)S(1)} %bitcast.16, bf16[4,128,256]{2,1,0:T(8,128)(2,1)S(1)} %get-tuple-element.10.r_1_, bf16[4,128,256]{2,1,0:T(8,128)(2,1)S(1)} %collective-permute-done.10.r_2_, bf16[4,128,256]{2,1,0:T(8,128)(2,1)S(1)} %collective-permute-done.11.r_3_, ...), custom_call_target="tpu_custom_call" | custom-call | flops 452984832 | bytes 1400832 | tf_op jit(solution)/shard_map/pallas_call | solution.py:448
  (27 shorter events, 0.5 us)
Async XLA Ops:
  0.6 14.3 %collective-permute-start.6 = (bf16[32,2,1024]{2,1,0:T(2,128)(2,1)}, bf16[32,2,1024]{2,1,0:T(2,128)(2,1)S(1)}, u32[]{:S(2)}, u32[]{:S(2)}) collective-permute-start(bf16[32,2,1024]{2,1,0:T(2,128)(2,1)} %bitcast.19), channel_id=1, source_target_pairs={{0,0},{8,1},{4,2},{12,3},{2,4},{10,5},{6,6},{14,7},{1,8},{9,9},{5,... | collective-permute-start | bytes 393224 | tf_op jit(solution)/shard_map/ppermute | solution.py:619
  6.4 5.1 %collective-permute-start.2 = (bf16[64,256]{1,0:T(8,128)(2,1)}, bf16[64,256]{1,0:T(8,128)(2,1)S(1)}, u32[]{:S(2)}, u32[]{:S(2)}) collective-permute-start(bf16[64,256]{1,0:T(8,128)(2,1)} %bitcast.11), channel_id=1, source_target_pairs={{0,12},{4,8},{8,4},{12,0},{1,13},{5,9},{9,5},{13,1},{2,14},{6,10},... | collective-permute-start | bytes 98312 | tf_op jit(solution)/shard_map/ppermute | solution.py:597
  6.5 7.9 %collective-permute-start.1 = (bf16[64,256]{1,0:T(8,128)(2,1)}, bf16[64,256]{1,0:T(8,128)(2,1)S(1)}, u32[]{:S(2)}, u32[]{:S(2)}) collective-permute-start(bf16[64,256]{1,0:T(8,128)(2,1)} %bitcast.12), channel_id=1, source_target_pairs={{0,8},{4,12},{8,0},{12,4},{1,9},{5,13},{9,1},{13,5},{2,10},{6,14},... | collective-permute-start | bytes 98312 | tf_op jit(solution)/shard_map/ppermute | solution.py:597
  8.0 7.0 %collective-permute-start = (bf16[64,256]{1,0:T(8,128)(2,1)}, bf16[64,256]{1,0:T(8,128)(2,1)S(1)}, u32[]{:S(2)}, u32[]{:S(2)}) collective-permute-start(bf16[64,256]{1,0:T(8,128)(2,1)} %bitcast.13), channel_id=1, source_target_pairs={{0,4},{4,0},{8,12},{12,8},{1,5},{5,1},{9,13},{13,9},{2,6},{6,2},{1... | collective-permute-start | bytes 98312 | tf_op jit(solution)/shard_map/ppermute | solution.py:597
  10.0 0.9 %copy-start.1 = (bf16[1,32,2,1024]{3,2,1,0:T(2,128)(2,1)S(1)}, bf16[1,32,2,1024]{3,2,1,0:T(2,128)(2,1)}, u32[]{:S(2)}) copy-start(bf16[1,32,2,1024]{3,2,1,0:T(2,128)(2,1)} %param.7) | copy-start | bytes 393220
  10.9 4.0 %copy-start.2 = (bf16[1,64,1,256]{3,1,2,0:T(8,128)(2,1)S(1)}, bf16[1,64,1,256]{3,1,2,0:T(8,128)(2,1)}, u32[]{:S(2)}) copy-start(bf16[1,64,1,256]{3,1,2,0:T(8,128)(2,1)} %param.8) | copy-start | bytes 98308
  11.3 14.8 %copy-start.3 = (bf16[3,3,3,32,256]{4,3,2,1,0:T(8,128)(2,1)S(1)}, bf16[3,3,3,32,256]{4,3,2,1,0:T(8,128)(2,1)}, u32[]{:S(2)}) copy-start(bf16[3,3,3,32,256]{4,3,2,1,0:T(8,128)(2,1)} %param.10) | copy-start | bytes 1327108
  11.3 13.3 %collective-permute-start.5 = (bf16[256,256]{1,0:T(8,128)(2,1)S(1)}, bf16[256,256]{1,0:T(8,128)(2,1)S(1)}, u32[]{:S(2)}, u32[]{:S(2)}) collective-permute-start(bf16[256,256]{1,0:T(8,128)(2,1)S(1)} %shard_map.86.r_2_), channel_id=1, source_target_pairs={{0,12},{4,8},{8,4},{12,0},{1,13},{5,9},{9,5},{13,1},{2,14},{6,10},... | collective-permute-start | bytes 393224 | tf_op jit(solution)/shard_map/ppermute | solution.py:597
  11.5 13.2 %collective-permute-start.4 = (bf16[256,256]{1,0:T(8,128)(2,1)S(1)}, bf16[256,256]{1,0:T(8,128)(2,1)S(1)}, u32[]{:S(2)}, u32[]{:S(2)}) collective-permute-start(bf16[256,256]{1,0:T(8,128)(2,1)S(1)} %shard_map.86.r_2_), channel_id=1, source_target_pairs={{0,8},{4,12},{8,0},{12,4},{1,9},{5,13},{9,1},{13,5},{2,10},{6,14},... | collective-permute-start | bytes 393224 | tf_op jit(solution)/shard_map/ppermute | solution.py:597
  14.4 10.2 %collective-permute-start.3 = (bf16[256,256]{1,0:T(8,128)(2,1)S(1)}, bf16[256,256]{1,0:T(8,128)(2,1)S(1)}, u32[]{:S(2)}, u32[]{:S(2)}) collective-permute-start(bf16[256,256]{1,0:T(8,128)(2,1)S(1)} %shard_map.86.r_2_), channel_id=1, source_target_pairs={{0,4},{4,0},{8,12},{12,8},{1,5},{5,1},{9,13},{13,9},{2,6},{6,2},{1... | collective-permute-start | bytes 393224 | tf_op jit(solution)/shard_map/ppermute | solution.py:597
  15.0 9.7 %collective-permute-start.8 = (bf16[32,2,1024]{2,1,0:T(2,128)(2,1)S(1)}, bf16[32,2,1024]{2,1,0:T(2,128)(2,1)S(1)}, u32[]{:S(2)}, u32[]{:S(2)}) collective-permute-start(bf16[32,2,1024]{2,1,0:T(2,128)(2,1)S(1)} %collective-permute-done.6.r_6_), channel_id=1, source_target_pairs={{0,2},{1,3},{2,0},{3,1},{4,6},{5,7},{6,4},{7,5},{8,10},{9,11},{10,... | collective-permute-start | bytes 393224 | tf_op jit(solution)/shard_map/ppermute | solution.py:591
  24.5 1.3 %collective-permute-start.7 = (bf16[32,2,1024]{2,1,0:T(2,128)(2,1)S(1)}, bf16[32,2,1024]{2,1,0:T(2,128)(2,1)S(1)}, u32[]{:S(2)}, u32[]{:S(2)}) collective-permute-start(bf16[32,2,1024]{2,1,0:T(2,128)(2,1)S(1)} %collective-permute-done.6.r_6_), channel_id=1, source_target_pairs={{0,1},{1,0},{2,3},{3,2},{4,5},{5,4},{6,7},{7,6},{8,9},{9,8},{10,11... | collective-permute-start | bytes 393224 | tf_op jit(solution)/shard_map/ppermute | solution.py:591
  24.6 1.4 %collective-permute-start.9 = (bf16[32,2,1024]{2,1,0:T(2,128)(2,1)S(1)}, bf16[32,2,1024]{2,1,0:T(2,128)(2,1)S(1)}, u32[]{:S(2)}, u32[]{:S(2)}) collective-permute-start(bf16[32,2,1024]{2,1,0:T(2,128)(2,1)S(1)} %collective-permute-done.8.r_8_), channel_id=1, source_target_pairs={{0,1},{1,0},{2,3},{3,2},{4,5},{5,4},{6,7},{7,6},{8,9},{9,8},{10,11... | collective-permute-start | bytes 393224 | tf_op jit(solution)/shard_map/ppermute | solution.py:591
  29.8 14.7 %collective-permute-start.11 = (bf16[4,128,256]{2,1,0:T(8,128)(2,1)S(1)}, bf16[4,128,256]{2,1,0:T(8,128)(2,1)S(1)}, u32[]{:S(2)}, u32[]{:S(2)}) collective-permute-start(bf16[4,128,256]{2,1,0:T(8,128)(2,1)S(1)} %get-tuple-element.10.r_1_), channel_id=1, source_target_pairs={{0,2},{1,3},{2,0},{3,1},{4,6},{5,7},{6,4},{7,5},{8,10},{9,11},{10,... | collective-permute-start | bytes 786440 | tf_op jit(solution)/shard_map/ppermute | solution.py:591
  29.9 11.3 %collective-permute-start.15 = (bf16[224,128]{1,0:T(8,128)(2,1)S(1)}, bf16[224,128]{1,0:T(8,128)(2,1)S(1)}, u32[]{:S(2)}, u32[]{:S(2)}) collective-permute-start(bf16[224,128]{1,0:T(8,128)(2,1)S(1)} %get-tuple-element.11), channel_id=1, source_target_pairs={{0,12},{1,8},{2,4},{3,0},{4,14},{5,10},{6,6},{7,2},{8,13},{9,9},{1... | collective-permute-start | bytes 172040 | tf_op jit(solution)/shard_map/ppermute | solution.py:656
  33.7 7.9 %collective-permute-start.14 = (bf16[224,128]{1,0:T(8,128)(2,1)S(1)}, bf16[224,128]{1,0:T(8,128)(2,1)S(1)}, u32[]{:S(2)}, u32[]{:S(2)}) collective-permute-start(bf16[224,128]{1,0:T(8,128)(2,1)S(1)} %get-tuple-element.11), channel_id=1, source_target_pairs={{0,8},{1,12},{2,0},{3,4},{4,10},{5,14},{6,2},{7,6},{8,9},{9,13},{1... | collective-permute-start | bytes 172040 | tf_op jit(solution)/shard_map/ppermute | solution.py:656
  36.1 5.8 %collective-permute-start.13 = (bf16[224,128]{1,0:T(8,128)(2,1)S(1)}, bf16[224,128]{1,0:T(8,128)(2,1)S(1)}, u32[]{:S(2)}, u32[]{:S(2)}) collective-permute-start(bf16[224,128]{1,0:T(8,128)(2,1)S(1)} %get-tuple-element.11), channel_id=1, source_target_pairs={{0,4},{1,0},{2,12},{3,8},{4,6},{5,2},{6,14},{7,10},{8,5},{9,1},{10... | collective-permute-start | bytes 172040 | tf_op jit(solution)/shard_map/ppermute | solution.py:656
  36.1 8.4 %collective-permute-start.12 = (bf16[224,128]{1,0:T(8,128)(2,1)S(1)}, bf16[224,128]{1,0:T(8,128)(2,1)S(1)}, u32[]{:S(2)}, u32[]{:S(2)}) collective-permute-start(bf16[224,128]{1,0:T(8,128)(2,1)S(1)} %get-tuple-element.11), channel_id=1, source_target_pairs={{0,0},{1,4},{2,8},{3,12},{4,2},{5,6},{6,10},{7,14},{8,1},{9,5},{10... | collective-permute-start | bytes 172040 | tf_op jit(solution)/shard_map/ppermute | solution.py:656
  39.6 6.0 %copy-start = (bf16[512,512]{1,0:T(8,128)(2,1)S(1)}, bf16[512,512]{1,0:T(8,128)(2,1)}, u32[]{:S(2)}) copy-start(bf16[512,512]{1,0:T(8,128)(2,1)} %constant.2.clone.r_0_) | copy-start | bytes 1572868
  41.2 5.6 %copy-start.4 = (bf16[3,3,3,32,128]{4,3,2,1,0:T(8,128)(2,1)S(1)}, bf16[3,3,3,32,128]{4,3,2,1,0:T(8,128)(2,1)}, u32[]{:S(2)}) copy-start(bf16[3,3,3,32,128]{4,3,2,1,0:T(8,128)(2,1)} %param.9) | copy-start | bytes 663556
  41.2 5.5 %collective-permute-start.10 = (bf16[4,128,256]{2,1,0:T(8,128)(2,1)S(1)}, bf16[4,128,256]{2,1,0:T(8,128)(2,1)S(1)}, u32[]{:S(2)}, u32[]{:S(2)}) collective-permute-start(bf16[4,128,256]{2,1,0:T(8,128)(2,1)S(1)} %get-tuple-element.10.r_1_), channel_id=1, source_target_pairs={{0,1},{1,0},{2,3},{3,2},{4,5},{5,4},{6,7},{7,6},{8,9},{9,8},{10,11... | collective-permute-start | bytes 786440 | tf_op jit(solution)/shard_map/ppermute | solution.py:591
  44.5 2.3 %collective-permute-start.16 = (bf16[4,128,256]{2,1,0:T(8,128)(2,1)S(1)}, bf16[4,128,256]{2,1,0:T(8,128)(2,1)S(1)}, u32[]{:S(2)}, u32[]{:S(2)}) collective-permute-start(bf16[4,128,256]{2,1,0:T(8,128)(2,1)S(1)} %collective-permute-done.11.r_3_), channel_id=1, source_target_pairs={{0,1},{1,0},{2,3},{3,2},{4,5},{5,4},{6,7},{7,6},{8,9},{9,8},{10,11... | collective-permute-start | bytes 786440 | tf_op jit(solution)/shard_map/ppermute | solution.py:591

commit v4 on v3

--- a/solution.py
+++ b/solution.py
@@ -208,12 +208,15 @@
     width = og * og
     part = width // 4
     block = 9 * chans
-    weights = jnp.concatenate([w_ref[depth * block : (depth + 1) * block, :] for depth in (2, 1, 0)], axis=1)
+    empty = jnp.zeros((block, all_chans), BF16)
+    weights = [w_ref[depth * block : (depth + 1) * block, :] for depth in (2, 1, 0)]
+    weights = jnp.concatenate(
+        [jnp.concatenate(weights + [empty], axis=1), jnp.concatenate([empty] + weights, axis=1)], axis=0
+    )
+    both = jnp.dot(weights, p_scr[...], preferred_element_type=F32)
     stacked = []
     for plane in range(2):
-        taps = jnp.dot(
-            weights, p_scr[plane * all_chans : (plane + 3) * all_chans, :], preferred_element_type=F32
-        )
+        taps = both[plane * block : (plane + 1) * block]
         sums = []
         for parity in range(4):
             terms = {}
@@ -317,10 +320,9 @@
     out_ref[...] = value.astype(BF16)
 
 
-def all_grad_kernel(og, chans, count, scale, w_ref, *refs):
-    grads, gates, sources, refs = refs[0], refs[1 : count + 1], refs[count + 1 : 2 * count + 1], refs[2 * count + 1 :]
-    local_ref, g_ref, act_ref, piece_ref, h_scr, p_scr, *block_refs = refs
-    matrix, order = lane_matrix(og), order_matrix(chans, 2)
+def all_grad_kernel(og, chans, count, w_ref, *refs):
+    grads, gates, refs = refs[0], refs[1 : count + 1], refs[count + 1 :]
+    local_ref, q_ref, g_ref, act_ref, h_scr = refs
     s = lax.axis_index("space")
     half = 4 * chans
     part = grads.shape[1] // count
@@ -332,16 +334,24 @@
         h_scr[at] = value
         value = value.astype(F32)
         act_ref[at] = leaky(value, value).astype(BF16)
-    empty = jnp.zeros((half, og * og), BF16)
-    p_scr[0] = empty
-    p_scr[2 * count + 1] = empty
+    empty = jnp.zeros((chans, q_ref.shape[1]), BF16)
+    for index in (0, 2 * count + 1, 2 * count + 2):
+        q_ref[index * chans : (index + 1) * chans, :] = empty
+    block = 9 * chans
     for q in range(count):
         here = g_ref[q]
-        plane_grad(w_ref, here, None, h_scr[q, 0:half, :], chans, og, p_scr.at[2 * q + 1], 0, None)
-        after = g_ref[q + 1] if q < count - 1 else jnp.zeros_like(here)
-        plane_grad(w_ref, here, after, h_scr[q, half : 2 * half, :], chans, og, p_scr.at[2 * q + 2], 0, None)
-    local_ref[...] = p_scr[pl.ds(2 * s, 4)]
-    filter_block(og, chans, count, scale, p_scr, matrix, order, sources, piece_ref, *block_refs)
+        even = jnp.dot(w_ref[block : 2 * block, :], here, preferred_element_type=F32)
+        odd = jnp.dot(w_ref[2 * block : 3 * block, :], here, preferred_element_type=F32)
+        if q < count - 1:
+            odd = odd + jnp.dot(w_ref[0:block, :], g_ref[q + 1], preferred_element_type=F32)
+        for plane, value in enumerate((even, odd)):
+            row = (2 * q + plane + 1) * chans
+            blocks = []
+            for parity, term in enumerate(transposed_taps(value, chans, og)):
+                at = (plane * 4 + parity) * chans
+                blocks.append(leaky(term, h_scr[q, at : at + chans, :].astype(F32)).astype(BF16))
+            q_ref[row : row + chans, :] = jnp.concatenate(blocks, axis=1)
+    local_ref[...] = q_ref[pl.ds(pl.multiple_of(2 * s * chans, chans), half), :]
 
 
 def mixed(index, count):
@@ -352,34 +362,34 @@
     return -(-27 * chans // 64) * 16
 
 
-def filter_block(og, chans, count, scale, p_ref, matrix, order, sources, out_ref, x_ref, p_scr, x_scr):
+def filter_block_kernel(og, chans, count, scale, q_ref, *refs):
+    sources, (out_ref, x_scr) = refs[:count], refs[count:]
+    matrix, order = lane_matrix(og), order_matrix(chans, 2)
     i = lax.axis_index("chan")
     width = og * og
     half = 4 * chans
     block = 9 * chans
     lanes = 4 * chans
-    planes = 2 * count
-    for mask, source in enumerate(sources):
+    across = 2 * count * chans
+    for index, source in enumerate(sources):
         value = split_planes(source[...], order, matrix, chans, 2, og)
-        x_ref[mixed(lax.bitwise_xor(i, mask), count)] = value.astype(BF16)
-    empty = jnp.zeros((chans, 4 * width), BF16)
-    for index in (0, planes + 1, planes + 2):
-        p_scr[index * chans : (index + 1) * chans, :] = empty
-    for plane in range(planes):
-        at = (plane + 1) * chans
-        for parity in range(4):
-            p_scr[at : at + chans, parity * width : (parity + 1) * width] = p_ref[
-                plane + 1, parity * chans : (parity + 1) * chans, :
-            ]
+        for plane in range(2):
+            blocks = moved_blocks(value[plane * half : (plane + 1) * half], chans, og)
+            at = (2 * index + plane) * block
+            for parity in range(4):
+                x_scr[at : at + block, parity * width : (parity + 1) * width] = window_rows(blocks, parity, og)
+    products = lax.dot_general(
+        x_scr[...], q_ref[chans : chans + across, :], CONTRACT_LAST, preferred_element_type=F32
+    )
+    group = lax.broadcasted_iota(jnp.int32, (block, lanes), 1) // chans
     total = jnp.zeros((block, lanes), F32)
-    for plane in range(planes):
-        first = (plane % 2) * half
-        blocks = moved_blocks(x_ref[plane // 2, first : first + half, :], chans, og)
-        for parity in range(4):
-            x_scr[plane % 2, :, parity * width : (parity + 1) * width] = window_rows(blocks, parity, og)
-        total = total + lax.dot_general(
-            x_scr[plane % 2], p_scr[plane * chans : plane * chans + lanes, :], CONTRACT_LAST, preferred_element_type=F32
-        )
+    for mask in range(count):
+        for plane in range(2):
+            place = 2 * mixed(lax.bitwise_xor(i, mask), count) + plane
+            at = (2 * mask + plane) * block
+            term = pltpu.roll(products[at : at + block], lax.rem(across + chans - place * chans, across), 1)[:, :lanes]
+            inside = (group + place > 0) & (group + place <= 2 * count)
+            total = total + jnp.where(inside, term, 0.0)
     total = total * scale
     rows = block_rows(chans)
     tail = total[rows:]
@@ -402,8 +412,15 @@
     return result
 
 
+def pair_kernel(own_ref, mate_ref, out_ref):
+    odd = lax.axis_index("chan") % 2
+    rows = own_ref.shape[0]
+    out_ref[pl.ds(pl.multiple_of(odd * rows, 16), rows), :] = own_ref[...]
+    out_ref[pl.ds(pl.multiple_of((1 - odd) * rows, 16), rows), :] = mate_ref[...]
+
+
 def join_kernel(chans, count, m_ref, *refs):
-    pieces, out_ref, scr = refs[:count], refs[count], refs[count + 1]
+    pieces, out_ref, scr = refs[:-2], refs[-2], refs[-1]
     s = lax.axis_index("space")
     lanes = 4 * chans
     block = 9 * chans
@@ -411,8 +428,10 @@
     rest = block - rows
     for step, piece in enumerate(pieces):
         scr[step] = piece[...]
-    side = jnp.concatenate([scr[lax.bitwise_xor(s, j)] for j in range(count)], axis=1)
-    joined = jnp.dot(side, m_ref[...], preferred_element_type=F32)
+    side = [
+        scr[lax.bitwise_xor(s // 2, j // 2), j % 2 * rows : (j % 2 + 1) * rows, :] for j in range(count)
+    ]
+    joined = jnp.dot(jnp.concatenate(side, axis=1), m_ref[...], preferred_element_type=F32)
     for depth in range(3):
         out_ref[depth * block : depth * block + rows, :] = joined[:, depth * lanes : (depth + 1) * lanes]
         at = (2 - depth) * rest
@@ -428,10 +447,7 @@
         j = lax.bitwise_xor(i, mask)
         for index in range(4):
             at = pl.multiple_of(index * all_chans + j * chans, chans)
-            for parity in range(4):
-                p_scr[pl.ds(at, chans), parity * width : (parity + 1) * width] = source[
-                    index, parity * chans : (parity + 1) * chans, :
-                ]
+            p_scr[pl.ds(at, chans), :] = source[index * chans : (index + 1) * chans, :]
     joined = in_grad_planes(og, chans, all_chans, w_ref, lane_matrix(og), p_scr)
     rows = [
         jnp.concatenate([joined[(plane * 4 + k) * chans : (plane * 4 + k + 1) * chans] for k in range(4)], axis=1)
@@ -627,33 +643,47 @@
     )
     gates = [gate] + [paired(gate, step) for step in range(1, count)]
     grads = lax.all_gather(packed, "chan", axis=0)
-    x_all = spread(x_turned, (grads, *gates[1:]))
     rows = block_rows(chans)
-    p_local, grads, act, piece = local_call(
-        lambda *r: all_grad_kernel(og, chans, count, scale_one, *r),
+    p_local, p_all, grads, act = local_call(
+        lambda *r: all_grad_kernel(og, chans, count, *r),
         [
-            shape((4, half, width), BF16),
+            shape((half, 4 * width), BF16),
+            shape(((planes * count + 3) * chans, 4 * width), BF16),
             shape((count, all_out, width), BF16),
             shape((count, planes * half, width), BF16),
-            shape((rows, all_chans), BF16),
         ],
-        [
-            pltpu.VMEM((count, planes * half, width), BF16),
-            pltpu.VMEM((planes * count + 2, half, width), BF16),
-            pltpu.VMEM((count, planes * half, width), BF16),
-            pltpu.VMEM(((planes * count + 3) * chans, 4 * width), BF16),
-            pltpu.VMEM((2, block, 4 * width), BF16),
-        ],
-        2 * 3 * count * block * (all_out * width + all_chans * cells),
+        [pltpu.VMEM((count, planes * half, width), BF16)],
+        2 * 3 * count * block * all_out * width,
         w2,
         grads,
         *gates,
+    )
+    x_all = spread(x_turned, (p_local,))
+    piece = local_call(
+        lambda *r: filter_block_kernel(og, chans, count, scale_one, *r),
+        shape((rows, all_chans), BF16),
+        [pltpu.VMEM((planes * count * block, 4 * width), BF16)],
+        2 * 3 * count * block * all_chans * cells,
+        p_all,
         *x_all,
     )
+    mate = lax.ppermute(piece, "chan", [(j, j ^ 1) for j in range(count)])
+    pair = local_call(
+        lambda *r: pair_kernel(*r),
+        shape((2 * rows, all_chans), BF16),
+        [],
+        0,
+        piece,
+        mate,
+    )
     pieces = []
-    for step in range(count):
-        pairs = [(a * count + j, (j ^ step) * count + mixed(a, count)) for a in range(count) for j in range(count)]
-        pieces.append(lax.ppermute(piece, both, pairs))
+    for step in range(count // 2):
+        pairs = [
+            (a * count + j, (j % 2 + (step ^ j // 2) * 2) * count + mixed(a, count))
+            for a in range(count)
+            for j in range(count)
+        ]
+        pieces.append(lax.ppermute(pair, both, pairs))
     filter_two = local_call(
         lambda *r: filter_two_square_kernel(og, chans, count, scale_two, *r),
         shape((3 * block, all_out), F32),
@@ -665,7 +695,9 @@
         grads,
         act,
     )
-    near_p = spread(p_local, (*pieces, filter_two))
+    near_p = [p_local] + [
+        lax.ppermute(p_local, "chan", [(i, i ^ mask) for i in range(count)]) for mask in range(1, count)
+    ]
     in_grad = local_call(
         lambda *r: in_grad_square_kernel(og, chans, count, *r),
         shape((chans, planes, cells), BF16),
@@ -677,7 +709,7 @@
     filter_one = local_call(
         lambda *r: join_kernel(chans, count, *r),
         shape((3 * block, all_chans), F32),
-        [pltpu.VMEM((count, rows, all_chans), BF16)],
+        [pltpu.VMEM((count // 2, 2 * rows, all_chans), BF16)],
         2 * rows * 16 * all_chans * all_chans,
         jnp.asarray(join_matrix(chans, count), BF16),
         *pieces,

time: 49 us -> 46.8 us (0.955); the launches traced: 48.8 us -> 45.9 us
  starting transfers between devices: 25 us -> 20.4 us
  waiting for transfers between devices: 4 us -> 6.4 us
  Pallas kernels: 8.79 us -> 8.28 us
    ppermute x4 -> x6, waiting for transfers between devices: 2.88 us -> 5.77 us  [the longest x3 4.53 us: square_shards(): lax.ppermute(p_local, 'chan', [(i, i ^ mask) for i in range(count)])]
    ppermute x4 -> x6, starting transfers between devices: 9.69 us -> 6.9 us  [the longest x2 4.65 us: square_shards(): pieces.append(lax.ppermute(pair, both, pairs))]
    ppermute x6 -> x3, starting transfers between devices: 2.31 us -> 0.87 us  [spread(): lax.ppermute(item, 'chan', pairs)]
    ppermute x6 -> x3, waiting for transfers between devices: 1.11 us -> 0.01 us  [spread(): lax.ppermute(item, 'chan', pairs)]
    ppermute x6, waiting for transfers between devices: 0.02 us -> 0.62 us  [paired(): lax.ppermute(value, 'space', [(i, i ^ mask) for i in range(lax.axis_size(...]
    pallas_call x6 -> x8, Pallas kernels: 8.79 us -> 8.28 us  [local_call(): pl.pallas_call(kernel, out_shape=out_shape, in_specs=[pl.BlockSpec(memory...]
  transfers between devices with their start and end apart: 17 -> 16, of which waited for: 5 -> 3; matrix products, arithmetic and copies ran while one was open for 0% -> 0% of each run, Pallas kernels for 6% -> 16%
where the time goes in v4:
time: 46.8 us; the launch traced here: 45.9 us
  starting transfers between devices  20.4 us (44%)
  blocking collectives  9.19 us (20%)
  Pallas kernels  8.28 us (18%)
  waiting for transfers between devices  6.4 us (14%)
  local copies, waits for them, and re-layouts  0.92 us (2%)
  between operations  0.75 us (2%)
    all_gather x1, blocking collectives, square_shards(): grads = lax.all_gather(packed, 'chan', axis=0)  9.19 us
    pallas_call x8, Pallas kernels, local_call(): pl.pallas_call(kernel, out_shape=out_shape, in_specs=[pl.BlockSpec(memory...  8.28 us
    ppermute x6, starting transfers between devices, paired(): lax.ppermute(value, 'space', [(i, i ^ mask) for i in range(lax.axis_size(...  6.88 us
    ppermute x1, starting transfers between devices, square_shards(): x_turned = lax.ppermute(inputs.reshape(chans, planes, cells), both, turn)  5.76 us
    ppermute x2, starting transfers between devices, square_shards(): pieces.append(lax.ppermute(pair, both, pairs))  4.65 us
    ppermute x3, waiting for transfers between devices, square_shards(): lax.ppermute(p_local, 'chan', [(i, i ^ mask) for i in range(count)])  4.53 us
    ppermute x3, starting transfers between devices, square_shards(): lax.ppermute(p_local, 'chan', [(i, i ^ mask) for i in range(count)])  2.17 us
    ppermute x1, waiting for transfers between devices, square_shards(): mate = lax.ppermute(piece, 'chan', [(j, j ^ 1) for j in range(count)])  1.23 us
  transfers between devices with their start and end apart: 16, of which 3 were waited for; matrix products, arithmetic and copies ran while one was open for 0% of the time, Pallas kernels for 16%

profile of v4, /device:TPU:3, one launch (start us, length us, event | category | flops | bytes accessed | tf_op | source)
XLA Modules:
  0.0 45.9 jit_solution(172495115117548147)
XLA Ops:
  0.6 5.8 %collective-permute-start.9 = (bf16[32,2,1024]{2,1,0:T(2,128)(2,1)}, bf16[32,2,1024]{2,1,0:T(2,128)(2,1)S(1)}, u32[]{:S(2)}, u32[]{:S(2)}) collective-permute-start(bf16[32,2,1024]{2,1,0:T(2,128)(2,1)} %bitcast.19), channel_id=1, source_target_pairs={{0,0},{8,1},{4,2},{12,3},{2,4},{10,5},{6,6},{14,7},{1,8},{9,9},{5,... | collective-permute-start | bytes 393224 | tf_op jit(solution)/shard_map/ppermute | solution.py:635
  6.4 0.4 collective-permute-start
  6.8 3.2 %collective-permute-start.2 = (bf16[64,256]{1,0:T(8,128)(2,1)}, bf16[64,256]{1,0:T(8,128)(2,1)S(1)}, u32[]{:S(2)}, u32[]{:S(2)}) collective-permute-start(bf16[64,256]{1,0:T(8,128)(2,1)} %bitcast.13), channel_id=1, source_target_pairs={{0,12},{4,8},{8,4},{12,0},{1,13},{5,9},{9,5},{13,1},{2,14},{6,10},... | collective-permute-start | bytes 98312 | tf_op jit(solution)/shard_map/ppermute | solution.py:613
  10.0 0.9 %copy-done.1 = bf16[1,32,2,1024]{3,2,1,0:T(2,128)(2,1)S(1)} copy-done((bf16[1,32,2,1024]{3,2,1,0:T(2,128)(2,1)S(1)}, bf16[1,32,2,1024]{3,2,1,0:T(2,128)(2,1)}, u32[]{:S(2)}) %copy-start.1) | copy-done | bytes 131096
  10.9 0.4 shard_map.86.r_2_
  11.4 0.3 collective-permute-start.4
  11.7 0.6 %collective-permute-done.1.refs_2_ = bf16[64,256]{1,0:T(8,128)(2,1)S(1)} collective-permute-done((bf16[64,256]{1,0:T(8,128)(2,1)}, bf16[64,256]{1,0:T(8,128)(2,1)S(1)}, u32[]{:S(2)}, u32[]{:S(2)}) %collective-permute-start.1) | collective-permute-done | bytes 32800 | tf_op jit(solution)/shard_map/ppermute | solution.py:613
  12.3 2.9 %collective-permute-start.5 = (bf16[256,256]{1,0:T(8,128)(2,1)S(1)}, bf16[256,256]{1,0:T(8,128)(2,1)S(1)}, u32[]{:S(2)}, u32[]{:S(2)}) collective-permute-start(bf16[256,256]{1,0:T(8,128)(2,1)S(1)} %shard_map.86.r_2_), channel_id=1, source_target_pairs={{0,12},{4,8},{8,4},{12,0},{1,13},{5,9},{9,5},{13,1},{2,14},{6,10},... | collective-permute-start | bytes 393224 | tf_op jit(solution)/shard_map/ppermute | solution.py:613
  15.2 0.3 collective-permute-start.11
  15.5 9.2 %all-gather = bf16[1024,256]{1,0:T(8,128)(2,1)S(1)} all-gather(bf16[256,256]{1,0:T(8,128)(2,1)S(1)} %shard_map.85), channel_id=2, replica_groups=mesh['groups'=2,'space'=4,'chan'=4] {'chan'}, dimensions={0}, use_global_device_ids=true | all-gather | bytes 655360 | tf_op jit(solution)/shard_map/all_gather | solution.py:645
  24.7 0.2 collective-permute-start.10
  24.9 0.9 %shard_map.87 = (bf16[128,1024]{1,0:T(8,128)(2,1)S(1)}, bf16[352,1024]{1,0:T(8,128)(2,1)S(1)}, bf16[4,256,256]{2,1,0:T(8,128)(2,1)S(1)}, bf16[4,256,256]{2,1,0:T(8,128)(2,1)S(1)}) custom-call(bf16[864,256]{1,0:T(8,128)(2,1)S(1)} %bitcast.15, bf16[4,256,256]{2,1,0:T(8,128)(2,1)S(1)} %bitcast.9, bf16[256,256]{1,0:T(8,128)(2,1)S(1)} %shard_map.86.r_2_, ...), custom_call_target="tpu_custom_call" | custom-call | flops 452984832 | bytes 3522560 | tf_op jit(solution)/shard_map/pallas_call | solution.py:464
  25.9 0.4 collective-permute-start.12
  26.3 0.2 collective-permute-start.6
  26.4 0.2 collective-permute-start.7
  26.7 1.8 %collective-permute-start.8 = (bf16[128,1024]{1,0:T(8,128)(2,1)S(1)}, bf16[128,1024]{1,0:T(8,128)(2,1)S(1)}, u32[]{:S(2)}, u32[]{:S(2)}) collective-permute-start(bf16[128,1024]{1,0:T(8,128)(2,1)S(1)} %get-tuple-element.8.r_1_), channel_id=1, source_target_pairs={{0,3},{1,2},{2,1},{3,0},{4,7},{5,6},{6,5},{7,4},{8,11},{9,10},{10,... | collective-permute-start | bytes 786440 | tf_op jit(solution)/shard_map/ppermute | solution.py:699
  28.5 2.3 %shard_map.89.r_0_ = bf16[224,128]{1,0:T(8,128)(2,1)S(1)} custom-call(bf16[352,1024]{1,0:T(8,128)(2,1)S(1)} %get-tuple-element.9.r_0_, bf16[32,2,1024]{2,1,0:T(2,128)(2,1)S(1)} %collective-permute-done.9.r_1_, bf16[32,2,1024]{2,1,0:T(2,128)(2,1)S(1)} %collective-permute-done.10.r_2_, bf16[32,2,1024]{2,1,0:T(2,128)(2,1)S(1)} %collective-permute-done.11.r_3_, ...), custom_call_target="tpu_custom_call" | custom-call | flops 905969664 | bytes 1302528 | tf_op jit(solution)/shard_map/pallas_call | solution.py:464
  30.8 1.2 %collective-permute-done.13.r_1_ = bf16[224,128]{1,0:T(8,128)(2,1)S(1)} collective-permute-done((bf16[224,128]{1,0:T(8,128)(2,1)S(1)}, bf16[224,128]{1,0:T(8,128)(2,1)S(1)}, u32[]{:S(2)}, u32[]{:S(2)}) %collective-permute-start.13) | collective-permute-done | bytes 57376 | tf_op jit(solution)/shard_map/ppermute | solution.py:670
  32.1 3.3 %collective-permute-start.14 = (bf16[448,128]{1,0:T(8,128)(2,1)S(1)}, bf16[448,128]{1,0:T(8,128)(2,1)S(1)}, u32[]{:S(2)}, u32[]{:S(2)}) collective-permute-start(bf16[448,128]{1,0:T(8,128)(2,1)S(1)} %shard_map.90), channel_id=1, source_target_pairs={{0,0},{1,4},{2,8},{3,12},{4,2},{5,6},{6,10},{7,14},{8,1},{9,5},{10... | collective-permute-start | bytes 344072 | tf_op jit(solution)/shard_map/ppermute | solution.py:686
  35.4 1.3 %collective-permute-start.15 = (bf16[448,128]{1,0:T(8,128)(2,1)S(1)}, bf16[448,128]{1,0:T(8,128)(2,1)S(1)}, u32[]{:S(2)}, u32[]{:S(2)}) collective-permute-start(bf16[448,128]{1,0:T(8,128)(2,1)S(1)} %shard_map.90), channel_id=1, source_target_pairs={{0,8},{1,12},{2,0},{3,4},{4,10},{5,14},{6,2},{7,6},{8,9},{9,13},{1... | collective-permute-start | bytes 344072 | tf_op jit(solution)/shard_map/ppermute | solution.py:686
  36.7 1.6 %shard_map.92 = f32[864,256]{1,0:T(8,128)} custom-call(bf16[4,256,256]{2,1,0:T(8,128)(2,1)S(1)} %get-tuple-element.11.r_0_, bf16[4,256,256]{2,1,0:T(8,128)(2,1)S(1)} %get-tuple-element.12.r_1_), custom_call_target="tpu_custom_call" | custom-call | flops 452984832 | bytes 1933312 | tf_op jit(solution)/shard_map/pallas_call | solution.py:464
  38.3 4.5 %collective-permute-done.8.r_4_ = bf16[128,1024]{1,0:T(8,128)(2,1)S(1)} collective-permute-done((bf16[128,1024]{1,0:T(8,128)(2,1)S(1)}, bf16[128,1024]{1,0:T(8,128)(2,1)S(1)}, u32[]{:S(2)}, u32[]{:S(2)}) %collective-permute-start.8) | collective-permute-done | bytes 262176 | tf_op jit(solution)/shard_map/ppermute | solution.py:699
  42.8 2.0 %shard_map.88 = bf16[32,2,1024]{2,1,0:T(2,128)(2,1)} custom-call(bf16[864,128]{1,0:T(8,128)(2,1)S(1)} %bitcast.16, bf16[128,1024]{1,0:T(8,128)(2,1)S(1)} %get-tuple-element.8.r_1_, bf16[128,1024]{1,0:T(8,128)(2,1)S(1)} %collective-permute-done.6.r_2_, bf16[128,1024]{1,0:T(8,128)(2,1)S(1)} %collective-permute-done.7.r_3_, ...), custom_call_target="tpu_custom_call" | custom-call | flops 452984832 | bytes 1400832 | tf_op jit(solution)/shard_map/pallas_call | solution.py:464
  44.9 1.0 %shard_map.91 = f32[864,128]{1,0:T(8,128)} custom-call(bf16[512,512]{1,0:T(8,128)(2,1)S(1)} %copy-done, bf16[448,128]{1,0:T(8,128)(2,1)S(1)} %collective-permute-done.14.r_1_, bf16[448,128]{1,0:T(8,128)(2,1)S(1)} %collective-permute-done.15.r_2_), custom_call_target="tpu_custom_call" | custom-call | flops 117440512 | bytes 1196032 | tf_op jit(solution)/shard_map/pallas_call | solution.py:464
  (27 shorter events, 0.2 us)
Async XLA Ops:
  0.6 14.6 %collective-permute-start.9 = (bf16[32,2,1024]{2,1,0:T(2,128)(2,1)}, bf16[32,2,1024]{2,1,0:T(2,128)(2,1)S(1)}, u32[]{:S(2)}, u32[]{:S(2)}) collective-permute-start(bf16[32,2,1024]{2,1,0:T(2,128)(2,1)} %bitcast.19), channel_id=1, source_target_pairs={{0,0},{8,1},{4,2},{12,3},{2,4},{10,5},{6,6},{14,7},{1,8},{9,9},{5,... | collective-permute-start | bytes 393224 | tf_op jit(solution)/shard_map/ppermute | solution.py:635
  6.4 5.0 %collective-permute-start = (bf16[64,256]{1,0:T(8,128)(2,1)}, bf16[64,256]{1,0:T(8,128)(2,1)S(1)}, u32[]{:S(2)}, u32[]{:S(2)}) collective-permute-start(bf16[64,256]{1,0:T(8,128)(2,1)} %bitcast.11), channel_id=1, source_target_pairs={{0,4},{4,0},{8,12},{12,8},{1,5},{5,1},{9,13},{13,9},{2,6},{6,2},{1... | collective-permute-start | bytes 98312 | tf_op jit(solution)/shard_map/ppermute | solution.py:613
  6.8 5.5 %collective-permute-start.1 = (bf16[64,256]{1,0:T(8,128)(2,1)}, bf16[64,256]{1,0:T(8,128)(2,1)S(1)}, u32[]{:S(2)}, u32[]{:S(2)}) collective-permute-start(bf16[64,256]{1,0:T(8,128)(2,1)} %bitcast.12), channel_id=1, source_target_pairs={{0,8},{4,12},{8,0},{12,4},{1,9},{5,13},{9,1},{13,5},{2,10},{6,14},... | collective-permute-start | bytes 98312 | tf_op jit(solution)/shard_map/ppermute | solution.py:613
  6.8 8.4 %collective-permute-start.2 = (bf16[64,256]{1,0:T(8,128)(2,1)}, bf16[64,256]{1,0:T(8,128)(2,1)S(1)}, u32[]{:S(2)}, u32[]{:S(2)}) collective-permute-start(bf16[64,256]{1,0:T(8,128)(2,1)} %bitcast.13), channel_id=1, source_target_pairs={{0,12},{4,8},{8,4},{12,0},{1,13},{5,9},{9,5},{13,1},{2,14},{6,10},... | collective-permute-start | bytes 98312 | tf_op jit(solution)/shard_map/ppermute | solution.py:613
  10.0 0.9 %copy-start.1 = (bf16[1,32,2,1024]{3,2,1,0:T(2,128)(2,1)S(1)}, bf16[1,32,2,1024]{3,2,1,0:T(2,128)(2,1)}, u32[]{:S(2)}) copy-start(bf16[1,32,2,1024]{3,2,1,0:T(2,128)(2,1)} %param.7) | copy-start | bytes 393220
  10.9 4.3 %copy-start.2 = (bf16[1,64,1,256]{3,1,2,0:T(8,128)(2,1)S(1)}, bf16[1,64,1,256]{3,1,2,0:T(8,128)(2,1)}, u32[]{:S(2)}) copy-start(bf16[1,64,1,256]{3,1,2,0:T(8,128)(2,1)} %param.8) | copy-start | bytes 98308
  11.3 13.6 %copy-start.3 = (bf16[3,3,3,32,256]{4,3,2,1,0:T(8,128)(2,1)S(1)}, bf16[3,3,3,32,256]{4,3,2,1,0:T(8,128)(2,1)}, u32[]{:S(2)}) copy-start(bf16[3,3,3,32,256]{4,3,2,1,0:T(8,128)(2,1)} %param.10) | copy-start | bytes 1327108
  11.3 13.6 %collective-permute-start.3 = (bf16[256,256]{1,0:T(8,128)(2,1)S(1)}, bf16[256,256]{1,0:T(8,128)(2,1)S(1)}, u32[]{:S(2)}, u32[]{:S(2)}) collective-permute-start(bf16[256,256]{1,0:T(8,128)(2,1)S(1)} %shard_map.86.r_2_), channel_id=1, source_target_pairs={{0,4},{4,0},{8,12},{12,8},{1,5},{5,1},{9,13},{13,9},{2,6},{6,2},{1... | collective-permute-start | bytes 393224 | tf_op jit(solution)/shard_map/ppermute | solution.py:613
  11.4 13.5 %collective-permute-start.4 = (bf16[256,256]{1,0:T(8,128)(2,1)S(1)}, bf16[256,256]{1,0:T(8,128)(2,1)S(1)}, u32[]{:S(2)}, u32[]{:S(2)}) collective-permute-start(bf16[256,256]{1,0:T(8,128)(2,1)S(1)} %shard_map.86.r_2_), channel_id=1, source_target_pairs={{0,8},{4,12},{8,0},{12,4},{1,9},{5,13},{9,1},{13,5},{2,10},{6,14},... | collective-permute-start | bytes 393224 | tf_op jit(solution)/shard_map/ppermute | solution.py:613
  12.3 12.6 %collective-permute-start.5 = (bf16[256,256]{1,0:T(8,128)(2,1)S(1)}, bf16[256,256]{1,0:T(8,128)(2,1)S(1)}, u32[]{:S(2)}, u32[]{:S(2)}) collective-permute-start(bf16[256,256]{1,0:T(8,128)(2,1)S(1)} %shard_map.86.r_2_), channel_id=1, source_target_pairs={{0,12},{4,8},{8,4},{12,0},{1,13},{5,9},{9,5},{13,1},{2,14},{6,10},... | collective-permute-start | bytes 393224 | tf_op jit(solution)/shard_map/ppermute | solution.py:613
  15.2 10.6 %collective-permute-start.11 = (bf16[32,2,1024]{2,1,0:T(2,128)(2,1)S(1)}, bf16[32,2,1024]{2,1,0:T(2,128)(2,1)S(1)}, u32[]{:S(2)}, u32[]{:S(2)}) collective-permute-start(bf16[32,2,1024]{2,1,0:T(2,128)(2,1)S(1)} %collective-permute-done.9.r_1_), channel_id=1, source_target_pairs={{0,2},{1,3},{2,0},{3,1},{4,6},{5,7},{6,4},{7,5},{8,10},{9,11},{10,... | collective-permute-start | bytes 393224 | tf_op jit(solution)/shard_map/ppermute | solution.py:607
  24.7 3.7 %collective-permute-start.10 = (bf16[32,2,1024]{2,1,0:T(2,128)(2,1)S(1)}, bf16[32,2,1024]{2,1,0:T(2,128)(2,1)S(1)}, u32[]{:S(2)}, u32[]{:S(2)}) collective-permute-start(bf16[32,2,1024]{2,1,0:T(2,128)(2,1)S(1)} %collective-permute-done.9.r_1_), channel_id=1, source_target_pairs={{0,1},{1,0},{2,3},{3,2},{4,5},{5,4},{6,7},{7,6},{8,9},{9,8},{10,11... | collective-permute-start | bytes 393224 | tf_op jit(solution)/shard_map/ppermute | solution.py:607
  25.9 2.6 %collective-permute-start.12 = (bf16[32,2,1024]{2,1,0:T(2,128)(2,1)S(1)}, bf16[32,2,1024]{2,1,0:T(2,128)(2,1)S(1)}, u32[]{:S(2)}, u32[]{:S(2)}) collective-permute-start(bf16[32,2,1024]{2,1,0:T(2,128)(2,1)S(1)} %collective-permute-done.11.r_3_), channel_id=1, source_target_pairs={{0,1},{1,0},{2,3},{3,2},{4,5},{5,4},{6,7},{7,6},{8,9},{9,8},{10,11... | collective-permute-start | bytes 393224 | tf_op jit(solution)/shard_map/ppermute | solution.py:607
  26.3 12.0 %collective-permute-start.6 = (bf16[128,1024]{1,0:T(8,128)(2,1)S(1)}, bf16[128,1024]{1,0:T(8,128)(2,1)S(1)}, u32[]{:S(2)}, u32[]{:S(2)}) collective-permute-start(bf16[128,1024]{1,0:T(8,128)(2,1)S(1)} %get-tuple-element.8.r_1_), channel_id=1, source_target_pairs={{0,1},{1,0},{2,3},{3,2},{4,5},{5,4},{6,7},{7,6},{8,9},{9,8},{10,11... | collective-permute-start | bytes 786440 | tf_op jit(solution)/shard_map/ppermute | solution.py:699
  26.4 11.9 %collective-permute-start.7 = (bf16[128,1024]{1,0:T(8,128)(2,1)S(1)}, bf16[128,1024]{1,0:T(8,128)(2,1)S(1)}, u32[]{:S(2)}, u32[]{:S(2)}) collective-permute-start(bf16[128,1024]{1,0:T(8,128)(2,1)S(1)} %get-tuple-element.8.r_1_), channel_id=1, source_target_pairs={{0,2},{1,3},{2,0},{3,1},{4,6},{5,7},{6,4},{7,5},{8,10},{9,11},{10,... | collective-permute-start | bytes 786440 | tf_op jit(solution)/shard_map/ppermute | solution.py:699
  26.7 16.2 %collective-permute-start.8 = (bf16[128,1024]{1,0:T(8,128)(2,1)S(1)}, bf16[128,1024]{1,0:T(8,128)(2,1)S(1)}, u32[]{:S(2)}, u32[]{:S(2)}) collective-permute-start(bf16[128,1024]{1,0:T(8,128)(2,1)S(1)} %get-tuple-element.8.r_1_), channel_id=1, source_target_pairs={{0,3},{1,2},{2,1},{3,0},{4,7},{5,6},{6,5},{7,4},{8,11},{9,10},{10,... | collective-permute-start | bytes 786440 | tf_op jit(solution)/shard_map/ppermute | solution.py:699
  30.7 1.3 %collective-permute-start.13 = (bf16[224,128]{1,0:T(8,128)(2,1)S(1)}, bf16[224,128]{1,0:T(8,128)(2,1)S(1)}, u32[]{:S(2)}, u32[]{:S(2)}) collective-permute-start(bf16[224,128]{1,0:T(8,128)(2,1)S(1)} %shard_map.89.r_0_), channel_id=1, source_target_pairs={{0,1},{1,0},{2,3},{3,2},{4,5},{5,4},{6,7},{7,6},{8,9},{9,8},{10,11... | collective-permute-start | bytes 172040 | tf_op jit(solution)/shard_map/ppermute | solution.py:670
  32.1 12.8 %collective-permute-start.14 = (bf16[448,128]{1,0:T(8,128)(2,1)S(1)}, bf16[448,128]{1,0:T(8,128)(2,1)S(1)}, u32[]{:S(2)}, u32[]{:S(2)}) collective-permute-start(bf16[448,128]{1,0:T(8,128)(2,1)S(1)} %shard_map.90), channel_id=1, source_target_pairs={{0,0},{1,4},{2,8},{3,12},{4,2},{5,6},{6,10},{7,14},{8,1},{9,5},{10... | collective-permute-start | bytes 344072 | tf_op jit(solution)/shard_map/ppermute | solution.py:686
  35.4 9.5 %collective-permute-start.15 = (bf16[448,128]{1,0:T(8,128)(2,1)S(1)}, bf16[448,128]{1,0:T(8,128)(2,1)S(1)}, u32[]{:S(2)}, u32[]{:S(2)}) collective-permute-start(bf16[448,128]{1,0:T(8,128)(2,1)S(1)} %shard_map.90), channel_id=1, source_target_pairs={{0,8},{1,12},{2,0},{3,4},{4,10},{5,14},{6,2},{7,6},{8,9},{9,13},{1... | collective-permute-start | bytes 344072 | tf_op jit(solution)/shard_map/ppermute | solution.py:686
  36.7 6.1 %copy-start.4 = (bf16[3,3,3,32,128]{4,3,2,1,0:T(8,128)(2,1)S(1)}, bf16[3,3,3,32,128]{4,3,2,1,0:T(8,128)(2,1)}, u32[]{:S(2)}) copy-start(bf16[3,3,3,32,128]{4,3,2,1,0:T(8,128)(2,1)} %param.9) | copy-start | bytes 663556
  42.8 2.1 %copy-start = (bf16[512,512]{1,0:T(8,128)(2,1)S(1)}, bf16[512,512]{1,0:T(8,128)(2,1)}, u32[]{:S(2)}) copy-start(bf16[512,512]{1,0:T(8,128)(2,1)} %constant.2.clone.r_0_) | copy-start | bytes 1572868

commit v5 on v4

--- a/solution.py
+++ b/solution.py
@@ -321,15 +321,17 @@
 
 
 def all_grad_kernel(og, chans, count, w_ref, *refs):
-    grads, gates, refs = refs[0], refs[1 : count + 1], refs[count + 1 :]
+    grads, gates, refs = refs[:count], refs[count : 2 * count], refs[2 * count :]
     local_ref, q_ref, g_ref, act_ref, h_scr = refs
     s = lax.axis_index("space")
     half = 4 * chans
-    part = grads.shape[1] // count
+    i = lax.axis_index("chan")
+    part = grads[0].shape[0] // count
     for step in range(count):
         at = lax.bitwise_xor(s, step)
-        for j in range(count):
-            g_ref[at, j * part : (j + 1) * part, :] = grads[j, step * part : (step + 1) * part, :]
+        for mask in range(count):
+            row = pl.multiple_of(lax.bitwise_xor(i, mask) * part, part)
+            g_ref[at, pl.ds(row, part), :] = grads[mask][step * part : (step + 1) * part, :]
         value = gates[step][...]
         h_scr[at] = value
         value = value.astype(F32)
@@ -594,8 +596,8 @@
     )
 
 
-def spread(value, before_last=()):
-    count = lax.axis_size("chan")
+def spread(value, before_last=(), axis="chan"):
+    count = lax.axis_size(axis)
     found = {0: value}
     bit = count // 2
     while bit:
@@ -604,7 +606,7 @@
             for mask in found:
                 if mask:
                     found[mask] = lax.optimization_barrier((found[mask], *before_last))[0]
-        found.update({mask ^ bit: lax.ppermute(item, "chan", pairs) for mask, item in found.items()})
+        found.update({mask ^ bit: lax.ppermute(item, axis, pairs) for mask, item in found.items()})
         bit //= 2
     return [found[mask] for mask in range(count)]
 
@@ -641,8 +643,8 @@
         2 * planes * half * width * width,
         pre_act.reshape(chans, planes, cells),
     )
-    gates = [gate] + [paired(gate, step) for step in range(1, count)]
-    grads = lax.all_gather(packed, "chan", axis=0)
+    gates = spread(gate, (), "space")
+    grads = spread(packed)
     rows = block_rows(chans)
     p_local, p_all, grads, act = local_call(
         lambda *r: all_grad_kernel(og, chans, count, *r),
@@ -655,10 +657,10 @@
         [pltpu.VMEM((count, planes * half, width), BF16)],
         2 * 3 * count * block * all_out * width,
         w2,
-        grads,
+        *grads,
         *gates,
     )
-    x_all = spread(x_turned, (p_local,))
+    x_all = spread(x_turned)
     piece = local_call(
         lambda *r: filter_block_kernel(og, chans, count, scale_one, *r),
         shape((rows, all_chans), BF16),

time: 46.8 us -> 45 us (0.962)
  blocking collectives: 9.19 us -> 0 us
  waiting for transfers between devices: 6.4 us -> 10.3 us
  starting transfers between devices: 20.4 us -> 24.2 us
    all_gather x1 -> x0, blocking collectives: 9.19 us -> none  [square_shards(): grads = lax.all_gather(packed, 'chan', axis=0)]
    ppermute x3 -> x9, starting transfers between devices: 0.87 us -> 6.45 us  [spread(): lax.ppermute(item, axis, pairs)]
    ppermute x3 -> x9, waiting for transfers between devices: 0.01 us -> 5.43 us  [spread(): lax.ppermute(item, axis, pairs)]
    ppermute x6 -> x3, starting transfers between devices: 6.88 us -> 3.61 us  [paired(): lax.ppermute(value, 'space', [(i, i ^ mask) for i in range(lax.axis_size(...]
    ppermute x3, waiting for transfers between devices: 4.53 us -> 3.08 us  [square_shards(): lax.ppermute(p_local, 'chan', [(i, i ^ mask) for i in range(count)])]
    ppermute x3, starting transfers between devices: 2.17 us -> 2.99 us  [square_shards(): lax.ppermute(p_local, 'chan', [(i, i ^ mask) for i in range(count)])]
    ppermute x1, starting transfers between devices: 0.07 us -> 0.57 us  [square_shards(): mate = lax.ppermute(piece, 'chan', [(j, j ^ 1) for j in range(count)])]
  transfers between devices with their start and end apart: 16 -> 19, of which waited for: 3 -> 6; matrix products, arithmetic and copies ran while one was open for 0% -> 0% of each run, Pallas kernels for 16% -> 16%
where the time goes in v5:
time: 45 us; the launch traced here: 44.5 us
  starting transfers between devices  24.2 us (54%)
  waiting for transfers between devices  10.3 us (23%)
  Pallas kernels  8.28 us (18%)
  local copies, waits for them, and re-layouts  0.92 us (2%)
  between operations  0.72 us (2%)
    pallas_call x8, Pallas kernels, local_call(): pl.pallas_call(kernel, out_shape=out_shape, in_specs=[pl.BlockSpec(memory...  8.28 us
    ppermute x9, starting transfers between devices, spread(): lax.ppermute(item, axis, pairs)  6.45 us
    ppermute x1, starting transfers between devices, square_shards(): x_turned = lax.ppermute(inputs.reshape(chans, planes, cells), both, turn)  5.76 us
    ppermute x9, waiting for transfers between devices, spread(): lax.ppermute(item, axis, pairs)  5.43 us
    ppermute x2, starting transfers between devices, square_shards(): pieces.append(lax.ppermute(pair, both, pairs))  4.85 us
    ppermute x3, starting transfers between devices, paired(): lax.ppermute(value, 'space', [(i, i ^ mask) for i in range(lax.axis_size(...  3.61 us
    ppermute x3, waiting for transfers between devices, square_shards(): lax.ppermute(p_local, 'chan', [(i, i ^ mask) for i in range(count)])  3.08 us
    ppermute x3, starting transfers between devices, square_shards(): lax.ppermute(p_local, 'chan', [(i, i ^ mask) for i in range(count)])  2.99 us
  transfers between devices with their start and end apart: 19, of which 6 were waited for; matrix products, arithmetic and copies ran while one was open for 0% of the time, Pallas kernels for 16%

profile of v5, /device:TPU:3, one launch (start us, length us, event | category | flops | bytes accessed | tf_op | source)
XLA Modules:
  0.0 44.5 jit_solution(9487893929869338797)
XLA Ops:
  0.6 5.8 %collective-permute-start.12 = (bf16[32,2,1024]{2,1,0:T(2,128)(2,1)}, bf16[32,2,1024]{2,1,0:T(2,128)(2,1)S(1)}, u32[]{:S(2)}, u32[]{:S(2)}) collective-permute-start(bf16[32,2,1024]{2,1,0:T(2,128)(2,1)} %bitcast.17), channel_id=1, source_target_pairs={{0,0},{8,1},{4,2},{12,3},{2,4},{10,5},{6,6},{14,7},{1,8},{9,9},{5,... | collective-permute-start | bytes 393224 | tf_op jit(solution)/shard_map/ppermute | solution.py:637
  6.8 3.2 %collective-permute-start.2 = (bf16[64,256]{1,0:T(8,128)(2,1)}, bf16[64,256]{1,0:T(8,128)(2,1)S(1)}, u32[]{:S(2)}, u32[]{:S(2)}) collective-permute-start(bf16[64,256]{1,0:T(8,128)(2,1)} %bitcast.11), channel_id=1, source_target_pairs={{0,12},{4,8},{8,4},{12,0},{1,13},{5,9},{9,5},{13,1},{2,14},{6,10},... | collective-permute-start | bytes 98312 | tf_op jit(solution)/shard_map/ppermute | solution.py:615
  10.0 0.9 %copy-done.1 = bf16[1,32,2,1024]{3,2,1,0:T(2,128)(2,1)S(1)} copy-done((bf16[1,32,2,1024]{3,2,1,0:T(2,128)(2,1)S(1)}, bf16[1,32,2,1024]{3,2,1,0:T(2,128)(2,1)}, u32[]{:S(2)}) %copy-start.1) | copy-done | bytes 131096
  10.9 0.4 shard_map.86.r_5_
  11.4 0.9 %collective-permute-done.1.refs_2_ = bf16[64,256]{1,0:T(8,128)(2,1)S(1)} collective-permute-done((bf16[64,256]{1,0:T(8,128)(2,1)}, bf16[64,256]{1,0:T(8,128)(2,1)S(1)}, u32[]{:S(2)}, u32[]{:S(2)}) %collective-permute-start.1) | collective-permute-done | bytes 32800 | tf_op jit(solution)/shard_map/ppermute | solution.py:615
  12.3 0.8 %collective-permute-start.4 = (bf16[256,256]{1,0:T(8,128)(2,1)S(1)}, bf16[256,256]{1,0:T(8,128)(2,1)S(1)}, u32[]{:S(2)}, u32[]{:S(2)}) collective-permute-start(bf16[256,256]{1,0:T(8,128)(2,1)S(1)} %shard_map.85.r_1_), channel_id=1, source_target_pairs={{0,2},{1,3},{2,0},{3,1},{4,6},{5,7},{6,4},{7,5},{8,10},{9,11},{10,... | collective-permute-start | bytes 393224 | tf_op jit(solution)/shard_map/ppermute | solution.py:609
  13.2 3.6 %collective-permute-start.6 = (bf16[256,256]{1,0:T(8,128)(2,1)S(1)}, bf16[256,256]{1,0:T(8,128)(2,1)S(1)}, u32[]{:S(2)}, u32[]{:S(2)}) collective-permute-start(bf16[256,256]{1,0:T(8,128)(2,1)S(1)} %shard_map.86.r_5_), channel_id=1, source_target_pairs={{0,4},{4,0},{8,12},{12,8},{1,5},{5,1},{9,13},{13,9},{2,6},{6,2},{1... | collective-permute-start | bytes 393224 | tf_op jit(solution)/shard_map/ppermute | solution.py:609
  16.8 0.9 %collective-permute-start.14 = (bf16[32,2,1024]{2,1,0:T(2,128)(2,1)S(1)}, bf16[32,2,1024]{2,1,0:T(2,128)(2,1)S(1)}, u32[]{:S(2)}, u32[]{:S(2)}) collective-permute-start(bf16[32,2,1024]{2,1,0:T(2,128)(2,1)S(1)} %collective-permute-done.12.r_1_), channel_id=1, source_target_pairs={{0,2},{1,3},{2,0},{3,1},{4,6},{5,7},{6,4},{7,5},{8,10},{9,11},{10,... | collective-permute-start | bytes 393224 | tf_op jit(solution)/shard_map/ppermute | solution.py:609
  17.7 1.7 %collective-permute-done.7.r_7_ = bf16[256,256]{1,0:T(8,128)(2,1)S(1)} collective-permute-done((bf16[256,256]{1,0:T(8,128)(2,1)S(1)}, bf16[256,256]{1,0:T(8,128)(2,1)S(1)}, u32[]{:S(2)}, u32[]{:S(2)}) %collective-permute-start.7) | collective-permute-done | bytes 131104 | tf_op jit(solution)/shard_map/ppermute | solution.py:609
  19.4 0.5 %collective-permute-start.5 = (bf16[256,256]{1,0:T(8,128)(2,1)S(1)}, bf16[256,256]{1,0:T(8,128)(2,1)S(1)}, u32[]{:S(2)}, u32[]{:S(2)}) collective-permute-start(bf16[256,256]{1,0:T(8,128)(2,1)S(1)} %collective-permute-done.4.r_3_), channel_id=1, source_target_pairs={{0,1},{1,0},{2,3},{3,2},{4,5},{5,4},{6,7},{7,6},{8,9},{9,8},{10,11... | collective-permute-start | bytes 393224 | tf_op jit(solution)/shard_map/ppermute | solution.py:609
  19.9 2.3 %collective-permute-done.6.r_6_ = bf16[256,256]{1,0:T(8,128)(2,1)S(1)} collective-permute-done((bf16[256,256]{1,0:T(8,128)(2,1)S(1)}, bf16[256,256]{1,0:T(8,128)(2,1)S(1)}, u32[]{:S(2)}, u32[]{:S(2)}) %collective-permute-start.6) | collective-permute-done | bytes 131104 | tf_op jit(solution)/shard_map/ppermute | solution.py:609
  22.2 0.4 collective-permute-start.13
  22.7 1.4 %collective-permute-done.8.r_8_ = bf16[256,256]{1,0:T(8,128)(2,1)S(1)} collective-permute-done((bf16[256,256]{1,0:T(8,128)(2,1)S(1)}, bf16[256,256]{1,0:T(8,128)(2,1)S(1)}, u32[]{:S(2)}, u32[]{:S(2)}) %collective-permute-start.8) | collective-permute-done | bytes 131104 | tf_op jit(solution)/shard_map/ppermute | solution.py:609
  24.2 0.9 %shard_map.87 = (bf16[128,1024]{1,0:T(8,128)(2,1)S(1)}, bf16[352,1024]{1,0:T(8,128)(2,1)S(1)}, bf16[4,256,256]{2,1,0:T(8,128)(2,1)S(1)}, bf16[4,256,256]{2,1,0:T(8,128)(2,1)S(1)}) custom-call(bf16[864,256]{1,0:T(8,128)(2,1)S(1)} %bitcast.13, bf16[256,256]{1,0:T(8,128)(2,1)S(1)} %shard_map.85.r_1_, bf16[256,256]{1,0:T(8,128)(2,1)S(1)} %collective-permute-done.3.r_2_, ...), custom_call_target="tpu_custom_call" | custom-call | flops 452984832 | bytes 3522560 | tf_op jit(solution)/shard_map/pallas_call | solution.py:466
  25.1 0.5 %collective-permute-start.10 = (bf16[128,1024]{1,0:T(8,128)(2,1)S(1)}, bf16[128,1024]{1,0:T(8,128)(2,1)S(1)}, u32[]{:S(2)}, u32[]{:S(2)}) collective-permute-start(bf16[128,1024]{1,0:T(8,128)(2,1)S(1)} %get-tuple-element.7.r_1_), channel_id=1, source_target_pairs={{0,2},{1,3},{2,0},{3,1},{4,6},{5,7},{6,4},{7,5},{8,10},{9,11},{10,... | collective-permute-start | bytes 786440 | tf_op jit(solution)/shard_map/ppermute | solution.py:701
  25.6 2.5 %collective-permute-start.11 = (bf16[128,1024]{1,0:T(8,128)(2,1)S(1)}, bf16[128,1024]{1,0:T(8,128)(2,1)S(1)}, u32[]{:S(2)}, u32[]{:S(2)}) collective-permute-start(bf16[128,1024]{1,0:T(8,128)(2,1)S(1)} %get-tuple-element.7.r_1_), channel_id=1, source_target_pairs={{0,3},{1,2},{2,1},{3,0},{4,7},{5,6},{6,5},{7,4},{8,11},{9,10},{10,... | collective-permute-start | bytes 786440 | tf_op jit(solution)/shard_map/ppermute | solution.py:701
  28.1 2.3 %shard_map.89.r_0_ = bf16[224,128]{1,0:T(8,128)(2,1)S(1)} custom-call(bf16[352,1024]{1,0:T(8,128)(2,1)S(1)} %get-tuple-element.8.r_0_, bf16[32,2,1024]{2,1,0:T(2,128)(2,1)S(1)} %collective-permute-done.12.r_1_, bf16[32,2,1024]{2,1,0:T(2,128)(2,1)S(1)} %collective-permute-done.13.r_2_, bf16[32,2,1024]{2,1,0:T(2,128)(2,1)S(1)} %collective-permute-done.14.r_3_, ...), custom_call_target="tpu_custom_call" | custom-call | flops 905969664 | bytes 1302528 | tf_op jit(solution)/shard_map/pallas_call | solution.py:466
  30.4 0.6 %collective-permute-start.16 = (bf16[224,128]{1,0:T(8,128)(2,1)S(1)}, bf16[224,128]{1,0:T(8,128)(2,1)S(1)}, u32[]{:S(2)}, u32[]{:S(2)}) collective-permute-start(bf16[224,128]{1,0:T(8,128)(2,1)S(1)} %shard_map.89.r_0_), channel_id=1, source_target_pairs={{0,1},{1,0},{2,3},{3,2},{4,5},{5,4},{6,7},{7,6},{8,9},{9,8},{10,11... | collective-permute-start | bytes 172040 | tf_op jit(solution)/shard_map/ppermute | solution.py:672
  30.9 0.9 %collective-permute-done.16.r_1_ = bf16[224,128]{1,0:T(8,128)(2,1)S(1)} collective-permute-done((bf16[224,128]{1,0:T(8,128)(2,1)S(1)}, bf16[224,128]{1,0:T(8,128)(2,1)S(1)}, u32[]{:S(2)}, u32[]{:S(2)}) %collective-permute-start.16) | collective-permute-done | bytes 57376 | tf_op jit(solution)/shard_map/ppermute | solution.py:672
  31.8 4.7 %collective-permute-start.17 = (bf16[448,128]{1,0:T(8,128)(2,1)S(1)}, bf16[448,128]{1,0:T(8,128)(2,1)S(1)}, u32[]{:S(2)}, u32[]{:S(2)}) collective-permute-start(bf16[448,128]{1,0:T(8,128)(2,1)S(1)} %shard_map.90), channel_id=1, source_target_pairs={{0,0},{1,4},{2,8},{3,12},{4,2},{5,6},{6,10},{7,14},{8,1},{9,5},{10... | collective-permute-start | bytes 344072 | tf_op jit(solution)/shard_map/ppermute | solution.py:688
  36.7 1.6 %shard_map.92 = f32[864,256]{1,0:T(8,128)} custom-call(bf16[4,256,256]{2,1,0:T(8,128)(2,1)S(1)} %get-tuple-element.9.r_0_, bf16[4,256,256]{2,1,0:T(8,128)(2,1)S(1)} %get-tuple-element.10.r_1_), custom_call_target="tpu_custom_call" | custom-call | flops 452984832 | bytes 1933312 | tf_op jit(solution)/shard_map/pallas_call | solution.py:466
  38.3 3.1 %collective-permute-done.11.r_4_ = bf16[128,1024]{1,0:T(8,128)(2,1)S(1)} collective-permute-done((bf16[128,1024]{1,0:T(8,128)(2,1)S(1)}, bf16[128,1024]{1,0:T(8,128)(2,1)S(1)}, u32[]{:S(2)}, u32[]{:S(2)}) %collective-permute-start.11) | collective-permute-done | bytes 262176 | tf_op jit(solution)/shard_map/ppermute | solution.py:701
  41.4 2.0 %shard_map.88 = bf16[32,2,1024]{2,1,0:T(2,128)(2,1)} custom-call(bf16[864,128]{1,0:T(8,128)(2,1)S(1)} %bitcast.14, bf16[128,1024]{1,0:T(8,128)(2,1)S(1)} %get-tuple-element.7.r_1_, bf16[128,1024]{1,0:T(8,128)(2,1)S(1)} %collective-permute-done.9.r_2_, bf16[128,1024]{1,0:T(8,128)(2,1)S(1)} %collective-permute-done.10.r_3_, ...), custom_call_target="tpu_custom_call" | custom-call | flops 452984832 | bytes 1400832 | tf_op jit(solution)/shard_map/pallas_call | solution.py:466
  43.4 1.0 %shard_map.91 = f32[864,128]{1,0:T(8,128)} custom-call(bf16[512,512]{1,0:T(8,128)(2,1)S(1)} %copy-done, bf16[448,128]{1,0:T(8,128)(2,1)S(1)} %collective-permute-done.17.r_1_, bf16[448,128]{1,0:T(8,128)(2,1)S(1)} %collective-permute-done.18.r_2_), custom_call_target="tpu_custom_call" | custom-call | flops 117440512 | bytes 1196032 | tf_op jit(solution)/shard_map/pallas_call | solution.py:466
  (32 shorter events, 0.8 us)
Async XLA Ops:
  0.6 16.2 %collective-permute-start.12 = (bf16[32,2,1024]{2,1,0:T(2,128)(2,1)}, bf16[32,2,1024]{2,1,0:T(2,128)(2,1)S(1)}, u32[]{:S(2)}, u32[]{:S(2)}) collective-permute-start(bf16[32,2,1024]{2,1,0:T(2,128)(2,1)} %bitcast.17), channel_id=1, source_target_pairs={{0,0},{8,1},{4,2},{12,3},{2,4},{10,5},{6,6},{14,7},{1,8},{9,9},{5,... | collective-permute-start | bytes 393224 | tf_op jit(solution)/shard_map/ppermute | solution.py:637
  6.4 5.0 %collective-permute-start = (bf16[64,256]{1,0:T(8,128)(2,1)}, bf16[64,256]{1,0:T(8,128)(2,1)S(1)}, u32[]{:S(2)}, u32[]{:S(2)}) collective-permute-start(bf16[64,256]{1,0:T(8,128)(2,1)} %bitcast.9), channel_id=1, source_target_pairs={{0,4},{4,0},{8,12},{12,8},{1,5},{5,1},{9,13},{13,9},{2,6},{6,2},{1... | collective-permute-start | bytes 98312 | tf_op jit(solution)/shard_map/ppermute | solution.py:615
  6.8 5.5 %collective-permute-start.1 = (bf16[64,256]{1,0:T(8,128)(2,1)}, bf16[64,256]{1,0:T(8,128)(2,1)S(1)}, u32[]{:S(2)}, u32[]{:S(2)}) collective-permute-start(bf16[64,256]{1,0:T(8,128)(2,1)} %bitcast.10), channel_id=1, source_target_pairs={{0,8},{4,12},{8,0},{12,4},{1,9},{5,13},{9,1},{13,5},{2,10},{6,14},... | collective-permute-start | bytes 98312 | tf_op jit(solution)/shard_map/ppermute | solution.py:615
  6.8 5.5 %collective-permute-start.2 = (bf16[64,256]{1,0:T(8,128)(2,1)}, bf16[64,256]{1,0:T(8,128)(2,1)S(1)}, u32[]{:S(2)}, u32[]{:S(2)}) collective-permute-start(bf16[64,256]{1,0:T(8,128)(2,1)} %bitcast.11), channel_id=1, source_target_pairs={{0,12},{4,8},{8,4},{12,0},{1,13},{5,9},{9,5},{13,1},{2,14},{6,10},... | collective-permute-start | bytes 98312 | tf_op jit(solution)/shard_map/ppermute | solution.py:615
  10.0 0.9 %copy-start.1 = (bf16[1,32,2,1024]{3,2,1,0:T(2,128)(2,1)S(1)}, bf16[1,32,2,1024]{3,2,1,0:T(2,128)(2,1)}, u32[]{:S(2)}) copy-start(bf16[1,32,2,1024]{3,2,1,0:T(2,128)(2,1)} %param.7) | copy-start | bytes 393220
  10.9 1.4 %copy-start.2 = (bf16[1,64,1,256]{3,1,2,0:T(8,128)(2,1)S(1)}, bf16[1,64,1,256]{3,1,2,0:T(8,128)(2,1)}, u32[]{:S(2)}) copy-start(bf16[1,64,1,256]{3,1,2,0:T(8,128)(2,1)} %param.8) | copy-start | bytes 98308
  10.9 13.2 %copy-start.3 = (bf16[3,3,3,32,256]{4,3,2,1,0:T(8,128)(2,1)S(1)}, bf16[3,3,3,32,256]{4,3,2,1,0:T(8,128)(2,1)}, u32[]{:S(2)}) copy-start(bf16[3,3,3,32,256]{4,3,2,1,0:T(8,128)(2,1)} %param.10) | copy-start | bytes 1327108
  11.3 8.1 %collective-permute-start.7 = (bf16[256,256]{1,0:T(8,128)(2,1)S(1)}, bf16[256,256]{1,0:T(8,128)(2,1)S(1)}, u32[]{:S(2)}, u32[]{:S(2)}) collective-permute-start(bf16[256,256]{1,0:T(8,128)(2,1)S(1)} %shard_map.86.r_5_), channel_id=1, source_target_pairs={{0,8},{4,12},{8,0},{12,4},{1,9},{5,13},{9,1},{13,5},{2,10},{6,14},... | collective-permute-start | bytes 393224 | tf_op jit(solution)/shard_map/ppermute | solution.py:609
  12.3 7.1 %collective-permute-start.4 = (bf16[256,256]{1,0:T(8,128)(2,1)S(1)}, bf16[256,256]{1,0:T(8,128)(2,1)S(1)}, u32[]{:S(2)}, u32[]{:S(2)}) collective-permute-start(bf16[256,256]{1,0:T(8,128)(2,1)S(1)} %shard_map.85.r_1_), channel_id=1, source_target_pairs={{0,2},{1,3},{2,0},{3,1},{4,6},{5,7},{6,4},{7,5},{8,10},{9,11},{10,... | collective-permute-start | bytes 393224 | tf_op jit(solution)/shard_map/ppermute | solution.py:609
  13.2 9.0 %collective-permute-start.6 = (bf16[256,256]{1,0:T(8,128)(2,1)S(1)}, bf16[256,256]{1,0:T(8,128)(2,1)S(1)}, u32[]{:S(2)}, u32[]{:S(2)}) collective-permute-start(bf16[256,256]{1,0:T(8,128)(2,1)S(1)} %shard_map.86.r_5_), channel_id=1, source_target_pairs={{0,4},{4,0},{8,12},{12,8},{1,5},{5,1},{9,13},{13,9},{2,6},{6,2},{1... | collective-permute-start | bytes 393224 | tf_op jit(solution)/shard_map/ppermute | solution.py:609
  16.8 5.8 %collective-permute-start.14 = (bf16[32,2,1024]{2,1,0:T(2,128)(2,1)S(1)}, bf16[32,2,1024]{2,1,0:T(2,128)(2,1)S(1)}, u32[]{:S(2)}, u32[]{:S(2)}) collective-permute-start(bf16[32,2,1024]{2,1,0:T(2,128)(2,1)S(1)} %collective-permute-done.12.r_1_), channel_id=1, source_target_pairs={{0,2},{1,3},{2,0},{3,1},{4,6},{5,7},{6,4},{7,5},{8,10},{9,11},{10,... | collective-permute-start | bytes 393224 | tf_op jit(solution)/shard_map/ppermute | solution.py:609
  17.7 5.0 %collective-permute-start.3 = (bf16[256,256]{1,0:T(8,128)(2,1)S(1)}, bf16[256,256]{1,0:T(8,128)(2,1)S(1)}, u32[]{:S(2)}, u32[]{:S(2)}) collective-permute-start(bf16[256,256]{1,0:T(8,128)(2,1)S(1)} %shard_map.85.r_1_), channel_id=1, source_target_pairs={{0,1},{1,0},{2,3},{3,2},{4,5},{5,4},{6,7},{7,6},{8,9},{9,8},{10,11... | collective-permute-start | bytes 393224 | tf_op jit(solution)/shard_map/ppermute | solution.py:609
  19.4 4.7 %collective-permute-start.8 = (bf16[256,256]{1,0:T(8,128)(2,1)S(1)}, bf16[256,256]{1,0:T(8,128)(2,1)S(1)}, u32[]{:S(2)}, u32[]{:S(2)}) collective-permute-start(bf16[256,256]{1,0:T(8,128)(2,1)S(1)} %collective-permute-done.7.r_7_), channel_id=1, source_target_pairs={{0,4},{4,0},{8,12},{12,8},{1,5},{5,1},{9,13},{13,9},{2,6},{6,2},{1... | collective-permute-start | bytes 393224 | tf_op jit(solution)/shard_map/ppermute | solution.py:609
  19.4 4.7 %collective-permute-start.5 = (bf16[256,256]{1,0:T(8,128)(2,1)S(1)}, bf16[256,256]{1,0:T(8,128)(2,1)S(1)}, u32[]{:S(2)}, u32[]{:S(2)}) collective-permute-start(bf16[256,256]{1,0:T(8,128)(2,1)S(1)} %collective-permute-done.4.r_3_), channel_id=1, source_target_pairs={{0,1},{1,0},{2,3},{3,2},{4,5},{5,4},{6,7},{7,6},{8,9},{9,8},{10,11... | collective-permute-start | bytes 393224 | tf_op jit(solution)/shard_map/ppermute | solution.py:609
  22.2 5.9 %collective-permute-start.13 = (bf16[32,2,1024]{2,1,0:T(2,128)(2,1)S(1)}, bf16[32,2,1024]{2,1,0:T(2,128)(2,1)S(1)}, u32[]{:S(2)}, u32[]{:S(2)}) collective-permute-start(bf16[32,2,1024]{2,1,0:T(2,128)(2,1)S(1)} %collective-permute-done.12.r_1_), channel_id=1, source_target_pairs={{0,1},{1,0},{2,3},{3,2},{4,5},{5,4},{6,7},{7,6},{8,9},{9,8},{10,11... | collective-permute-start | bytes 393224 | tf_op jit(solution)/shard_map/ppermute | solution.py:609
  22.6 5.5 %collective-permute-start.15 = (bf16[32,2,1024]{2,1,0:T(2,128)(2,1)S(1)}, bf16[32,2,1024]{2,1,0:T(2,128)(2,1)S(1)}, u32[]{:S(2)}, u32[]{:S(2)}) collective-permute-start(bf16[32,2,1024]{2,1,0:T(2,128)(2,1)S(1)} %collective-permute-done.14.r_3_), channel_id=1, source_target_pairs={{0,1},{1,0},{2,3},{3,2},{4,5},{5,4},{6,7},{7,6},{8,9},{9,8},{10,11... | collective-permute-start | bytes 393224 | tf_op jit(solution)/shard_map/ppermute | solution.py:609
  25.1 13.2 %collective-permute-start.10 = (bf16[128,1024]{1,0:T(8,128)(2,1)S(1)}, bf16[128,1024]{1,0:T(8,128)(2,1)S(1)}, u32[]{:S(2)}, u32[]{:S(2)}) collective-permute-start(bf16[128,1024]{1,0:T(8,128)(2,1)S(1)} %get-tuple-element.7.r_1_), channel_id=1, source_target_pairs={{0,2},{1,3},{2,0},{3,1},{4,6},{5,7},{6,4},{7,5},{8,10},{9,11},{10,... | collective-permute-start | bytes 786440 | tf_op jit(solution)/shard_map/ppermute | solution.py:701
  25.6 15.8 %collective-permute-start.11 = (bf16[128,1024]{1,0:T(8,128)(2,1)S(1)}, bf16[128,1024]{1,0:T(8,128)(2,1)S(1)}, u32[]{:S(2)}, u32[]{:S(2)}) collective-permute-start(bf16[128,1024]{1,0:T(8,128)(2,1)S(1)} %get-tuple-element.7.r_1_), channel_id=1, source_target_pairs={{0,3},{1,2},{2,1},{3,0},{4,7},{5,6},{6,5},{7,4},{8,11},{9,10},{10,... | collective-permute-start | bytes 786440 | tf_op jit(solution)/shard_map/ppermute | solution.py:701
  28.1 13.3 %collective-permute-start.9 = (bf16[128,1024]{1,0:T(8,128)(2,1)S(1)}, bf16[128,1024]{1,0:T(8,128)(2,1)S(1)}, u32[]{:S(2)}, u32[]{:S(2)}) collective-permute-start(bf16[128,1024]{1,0:T(8,128)(2,1)S(1)} %get-tuple-element.7.r_1_), channel_id=1, source_target_pairs={{0,1},{1,0},{2,3},{3,2},{4,5},{5,4},{6,7},{7,6},{8,9},{9,8},{10,11... | collective-permute-start | bytes 786440 | tf_op jit(solution)/shard_map/ppermute | solution.py:701
  30.4 1.5 %collective-permute-start.16 = (bf16[224,128]{1,0:T(8,128)(2,1)S(1)}, bf16[224,128]{1,0:T(8,128)(2,1)S(1)}, u32[]{:S(2)}, u32[]{:S(2)}) collective-permute-start(bf16[224,128]{1,0:T(8,128)(2,1)S(1)} %shard_map.89.r_0_), channel_id=1, source_target_pairs={{0,1},{1,0},{2,3},{3,2},{4,5},{5,4},{6,7},{7,6},{8,9},{9,8},{10,11... | collective-permute-start | bytes 172040 | tf_op jit(solution)/shard_map/ppermute | solution.py:672
  31.8 11.6 %collective-permute-start.17 = (bf16[448,128]{1,0:T(8,128)(2,1)S(1)}, bf16[448,128]{1,0:T(8,128)(2,1)S(1)}, u32[]{:S(2)}, u32[]{:S(2)}) collective-permute-start(bf16[448,128]{1,0:T(8,128)(2,1)S(1)} %shard_map.90), channel_id=1, source_target_pairs={{0,0},{1,4},{2,8},{3,12},{4,2},{5,6},{6,10},{7,14},{8,1},{9,5},{10... | collective-permute-start | bytes 344072 | tf_op jit(solution)/shard_map/ppermute | solution.py:688
  36.6 6.8 %collective-permute-start.18 = (bf16[448,128]{1,0:T(8,128)(2,1)S(1)}, bf16[448,128]{1,0:T(8,128)(2,1)S(1)}, u32[]{:S(2)}, u32[]{:S(2)}) collective-permute-start(bf16[448,128]{1,0:T(8,128)(2,1)S(1)} %shard_map.90), channel_id=1, source_target_pairs={{0,8},{1,12},{2,0},{3,4},{4,10},{5,14},{6,2},{7,6},{8,9},{9,13},{1... | collective-permute-start | bytes 344072 | tf_op jit(solution)/shard_map/ppermute | solution.py:688
  36.7 4.7 %copy-start.4 = (bf16[3,3,3,32,128]{4,3,2,1,0:T(8,128)(2,1)S(1)}, bf16[3,3,3,32,128]{4,3,2,1,0:T(8,128)(2,1)}, u32[]{:S(2)}) copy-start(bf16[3,3,3,32,128]{4,3,2,1,0:T(8,128)(2,1)} %param.9) | copy-start | bytes 663556
  41.4 2.1 %copy-start = (bf16[512,512]{1,0:T(8,128)(2,1)S(1)}, bf16[512,512]{1,0:T(8,128)(2,1)}, u32[]{:S(2)}) copy-start(bf16[512,512]{1,0:T(8,128)(2,1)} %constant.2.clone.r_0_) | copy-start | bytes 1572868

commit v6 on v5

--- a/solution.py
+++ b/solution.py
@@ -258,13 +258,27 @@
     filter_two_sums(count, block, scale, g_scr, even_scr, odd_scr, out_ref)
 
 
-def filter_two_square_kernel(og, chans, count, scale, g_ref, act_ref, out_ref, even_scr, odd_scr):
-    half = 4 * chans
+def filter_two_square_kernel(og, chans, count, scale, g_ref, act_ref, out_ref, even_scr, odd_scr, stage, sems):
+    half = 4 * chans
+    block = 9 * chans
     for at in range(count):
         for plane, target in enumerate((even_scr, odd_scr)):
             blocks = moved_blocks(act_ref[at, plane * half : (plane + 1) * half, :], chans, og)
             target[at] = window_rows(blocks, 0, og)
-    filter_two_sums(count, 9 * chans, scale, g_ref, even_scr, odd_scr, out_ref)
+    copies = []
+    for depth in range(3):
+        total = None
+        for at in range(count):
+            if depth == 0 and at == 0:
+                continue
+            source = even_scr[at] if depth == 1 else odd_scr[at - 1 if depth == 0 else at]
+            term = lax.dot_general(source, g_ref[at], CONTRACT_LAST, preferred_element_type=F32)
+            total = term if total is None else total + term
+        stage[depth] = total * scale
+        copies.append(pltpu.make_async_copy(stage.at[depth], out_ref.at[depth], sems.at[depth]))
+        copies[-1].start()
+    for copy in copies:
+        copy.wait()
 
 
 def filter_two_sums(count, block, scale, g_scr, even_scr, odd_scr, out_ref):
@@ -422,7 +436,7 @@
 
 
 def join_kernel(chans, count, m_ref, *refs):
-    pieces, out_ref, scr = refs[:-2], refs[-2], refs[-1]
+    pieces, (out_ref, scr, stage, sems) = refs[:-4], refs[-4:]
     s = lax.axis_index("space")
     lanes = 4 * chans
     block = 9 * chans
@@ -433,11 +447,17 @@
     side = [
         scr[lax.bitwise_xor(s // 2, j // 2), j % 2 * rows : (j % 2 + 1) * rows, :] for j in range(count)
     ]
-    joined = jnp.dot(jnp.concatenate(side, axis=1), m_ref[...], preferred_element_type=F32)
+    side = jnp.concatenate(side, axis=1)
+    spare = jnp.dot(side, m_ref[:, 3 * lanes :], preferred_element_type=F32)
+    copies = []
     for depth in range(3):
-        out_ref[depth * block : depth * block + rows, :] = joined[:, depth * lanes : (depth + 1) * lanes]
         at = (2 - depth) * rest
-        out_ref[depth * block + rows : (depth + 1) * block, :] = joined[at : at + rest, 3 * lanes :]
+        stage[depth, :rows, :] = jnp.dot(side, m_ref[:, depth * lanes : (depth + 1) * lanes], preferred_element_type=F32)
+        stage[depth, rows:, :] = spare[at : at + rest]
+        copies.append(pltpu.make_async_copy(stage.at[depth], out_ref.at[depth], sems.at[depth]))
+        copies[-1].start()
+    for copy in copies:
+        copy.wait()
 
 
 def in_grad_square_kernel(og, chans, count, w_ref, *refs):
@@ -460,14 +480,14 @@
     out_ref[...] = value.astype(BF16).reshape(out_ref.shape)
 
 
-def local_call(kernel, out_shape, scratch, flops, *operands):
+def local_call(kernel, out_shape, scratch, flops, *operands, out_space=pltpu.VMEM):
     total = sum(value.size * value.dtype.itemsize for value in operands)
     total += sum(math.prod(o.shape) * o.dtype.itemsize for o in jax.tree.leaves(out_shape))
     return pl.pallas_call(
         kernel,
         out_shape=out_shape,
         in_specs=[pl.BlockSpec(memory_space=pltpu.VMEM)] * len(operands),
-        out_specs=jax.tree.map(lambda _: pl.BlockSpec(memory_space=pltpu.VMEM), out_shape),
+        out_specs=jax.tree.map(lambda _: pl.BlockSpec(memory_space=out_space), out_shape),
         scratch_shapes=scratch,
         cost_estimate=pl.CostEstimate(flops=flops, bytes_accessed=total, transcendentals=0),
         compiler_params=pltpu.CompilerParams(vmem_limit_bytes=50 * 1024 * 1024),
@@ -688,14 +708,17 @@
         pieces.append(lax.ppermute(pair, both, pairs))
     filter_two = local_call(
         lambda *r: filter_two_square_kernel(og, chans, count, scale_two, *r),
-        shape((3 * block, all_out), F32),
+        shape((3, block, all_out), F32),
         [
             pltpu.VMEM((count, block, width), BF16),
             pltpu.VMEM((count, block, width), BF16),
+            pltpu.VMEM((3, block, all_out), F32),
+            pltpu.SemaphoreType.DMA((3,)),
         ],
         2 * 3 * count * block * all_out * width,
         grads,
         act,
+        out_space=pl.ANY,
     )
     near_p = [p_local] + [
         lax.ppermute(p_local, "chan", [(i, i ^ mask) for i in range(count)]) for mask in range(1, count)
@@ -710,11 +733,16 @@
     )
     filter_one = local_call(
         lambda *r: join_kernel(chans, count, *r),
-        shape((3 * block, all_chans), F32),
-        [pltpu.VMEM((count // 2, 2 * rows, all_chans), BF16)],
+        shape((3, block, all_chans), F32),
+        [
+            pltpu.VMEM((count // 2, 2 * rows, all_chans), BF16),
+            pltpu.VMEM((3, block, all_chans), F32),
+            pltpu.SemaphoreType.DMA((3,)),
+        ],
         2 * rows * 16 * all_chans * all_chans,
         jnp.asarray(join_matrix(chans, count), BF16),
         *pieces,
+        out_space=pl.ANY,
     )
     return (
         in_grad.reshape(samples, chans, planes, cells),

time: 45 us -> 45.1 us (level)
  no operation moved by 1% of the time
where the time goes in v6:
time: 45.1 us; the launch traced here: 44.5 us
  starting transfers between devices  24.2 us (54%)
  waiting for transfers between devices  10.5 us (23%)
  Pallas kernels  8.17 us (18%)
  local copies, waits for them, and re-layouts  0.92 us (2%)
  between operations  0.74 us (2%)
    pallas_call x8, Pallas kernels, local_call(): pl.pallas_call(kernel, out_shape=out_shape, in_specs=[pl.BlockSpec(memory...  8.17 us
    ppermute x9, starting transfers between devices, spread(): lax.ppermute(item, axis, pairs)  6.45 us
    ppermute x1, starting transfers between devices, square_shards(): x_turned = lax.ppermute(inputs.reshape(chans, planes, cells), both, turn)  5.76 us
    ppermute x9, waiting for transfers between devices, spread(): lax.ppermute(item, axis, pairs)  5.43 us
    ppermute x2, starting transfers between devices, square_shards(): pieces.append(lax.ppermute(pair, both, pairs))  4.85 us
    ppermute x3, starting transfers between devices, paired(): lax.ppermute(value, 'space', [(i, i ^ mask) for i in range(lax.axis_size(...  3.61 us
    ppermute x3, waiting for transfers between devices, square_shards(): lax.ppermute(p_local, 'chan', [(i, i ^ mask) for i in range(count)])  3.22 us
    ppermute x3, starting transfers between devices, square_shards(): lax.ppermute(p_local, 'chan', [(i, i ^ mask) for i in range(count)])  2.99 us
  transfers between devices with their start and end apart: 19, of which 6 were waited for; matrix products, arithmetic and copies ran while one was open for 0% of the time, Pallas kernels for 16%

profile of v6, /device:TPU:3, one launch (start us, length us, event | category | flops | bytes accessed | tf_op | source)
XLA Modules:
  0.0 44.5 jit_solution(17490986454546795877)
XLA Ops:
  0.6 5.8 %collective-permute-start.12 = (bf16[32,2,1024]{2,1,0:T(2,128)(2,1)}, bf16[32,2,1024]{2,1,0:T(2,128)(2,1)S(1)}, u32[]{:S(2)}, u32[]{:S(2)}) collective-permute-start(bf16[32,2,1024]{2,1,0:T(2,128)(2,1)} %bitcast.17), channel_id=1, source_target_pairs={{0,0},{8,1},{4,2},{12,3},{2,4},{10,5},{6,6},{14,7},{1,8},{9,9},{5,... | collective-permute-start | bytes 393224 | tf_op jit(solution)/shard_map/ppermute | solution.py:657
  6.8 3.2 %collective-permute-start.2 = (bf16[64,256]{1,0:T(8,128)(2,1)}, bf16[64,256]{1,0:T(8,128)(2,1)S(1)}, u32[]{:S(2)}, u32[]{:S(2)}) collective-permute-start(bf16[64,256]{1,0:T(8,128)(2,1)} %bitcast.11), channel_id=1, source_target_pairs={{0,12},{4,8},{8,4},{12,0},{1,13},{5,9},{9,5},{13,1},{2,14},{6,10},... | collective-permute-start | bytes 98312 | tf_op jit(solution)/shard_map/ppermute | solution.py:635
  10.0 0.9 %copy-done.1 = bf16[1,32,2,1024]{3,2,1,0:T(2,128)(2,1)S(1)} copy-done((bf16[1,32,2,1024]{3,2,1,0:T(2,128)(2,1)S(1)}, bf16[1,32,2,1024]{3,2,1,0:T(2,128)(2,1)}, u32[]{:S(2)}) %copy-start.1) | copy-done | bytes 131096
  10.9 0.4 shard_map.86.r_5_
  11.4 0.9 %collective-permute-done.1.refs_2_ = bf16[64,256]{1,0:T(8,128)(2,1)S(1)} collective-permute-done((bf16[64,256]{1,0:T(8,128)(2,1)}, bf16[64,256]{1,0:T(8,128)(2,1)S(1)}, u32[]{:S(2)}, u32[]{:S(2)}) %collective-permute-start.1) | collective-permute-done | bytes 32800 | tf_op jit(solution)/shard_map/ppermute | solution.py:635
  12.3 0.8 %collective-permute-start.4 = (bf16[256,256]{1,0:T(8,128)(2,1)S(1)}, bf16[256,256]{1,0:T(8,128)(2,1)S(1)}, u32[]{:S(2)}, u32[]{:S(2)}) collective-permute-start(bf16[256,256]{1,0:T(8,128)(2,1)S(1)} %shard_map.85.r_1_), channel_id=1, source_target_pairs={{0,2},{1,3},{2,0},{3,1},{4,6},{5,7},{6,4},{7,5},{8,10},{9,11},{10,... | collective-permute-start | bytes 393224 | tf_op jit(solution)/shard_map/ppermute | solution.py:629
  13.2 3.6 %collective-permute-start.6 = (bf16[256,256]{1,0:T(8,128)(2,1)S(1)}, bf16[256,256]{1,0:T(8,128)(2,1)S(1)}, u32[]{:S(2)}, u32[]{:S(2)}) collective-permute-start(bf16[256,256]{1,0:T(8,128)(2,1)S(1)} %shard_map.86.r_5_), channel_id=1, source_target_pairs={{0,4},{4,0},{8,12},{12,8},{1,5},{5,1},{9,13},{13,9},{2,6},{6,2},{1... | collective-permute-start | bytes 393224 | tf_op jit(solution)/shard_map/ppermute | solution.py:629
  16.8 0.9 %collective-permute-start.14 = (bf16[32,2,1024]{2,1,0:T(2,128)(2,1)S(1)}, bf16[32,2,1024]{2,1,0:T(2,128)(2,1)S(1)}, u32[]{:S(2)}, u32[]{:S(2)}) collective-permute-start(bf16[32,2,1024]{2,1,0:T(2,128)(2,1)S(1)} %collective-permute-done.12.r_1_), channel_id=1, source_target_pairs={{0,2},{1,3},{2,0},{3,1},{4,6},{5,7},{6,4},{7,5},{8,10},{9,11},{10,... | collective-permute-start | bytes 393224 | tf_op jit(solution)/shard_map/ppermute | solution.py:629
  17.7 1.7 %collective-permute-done.7.r_7_ = bf16[256,256]{1,0:T(8,128)(2,1)S(1)} collective-permute-done((bf16[256,256]{1,0:T(8,128)(2,1)S(1)}, bf16[256,256]{1,0:T(8,128)(2,1)S(1)}, u32[]{:S(2)}, u32[]{:S(2)}) %collective-permute-start.7) | collective-permute-done | bytes 131104 | tf_op jit(solution)/shard_map/ppermute | solution.py:629
  19.4 0.5 %collective-permute-start.5 = (bf16[256,256]{1,0:T(8,128)(2,1)S(1)}, bf16[256,256]{1,0:T(8,128)(2,1)S(1)}, u32[]{:S(2)}, u32[]{:S(2)}) collective-permute-start(bf16[256,256]{1,0:T(8,128)(2,1)S(1)} %collective-permute-done.4.r_3_), channel_id=1, source_target_pairs={{0,1},{1,0},{2,3},{3,2},{4,5},{5,4},{6,7},{7,6},{8,9},{9,8},{10,11... | collective-permute-start | bytes 393224 | tf_op jit(solution)/shard_map/ppermute | solution.py:629
  19.9 2.3 %collective-permute-done.6.r_6_ = bf16[256,256]{1,0:T(8,128)(2,1)S(1)} collective-permute-done((bf16[256,256]{1,0:T(8,128)(2,1)S(1)}, bf16[256,256]{1,0:T(8,128)(2,1)S(1)}, u32[]{:S(2)}, u32[]{:S(2)}) %collective-permute-start.6) | collective-permute-done | bytes 131104 | tf_op jit(solution)/shard_map/ppermute | solution.py:629
  22.2 0.4 collective-permute-start.13
  22.7 1.4 %collective-permute-done.8.r_8_ = bf16[256,256]{1,0:T(8,128)(2,1)S(1)} collective-permute-done((bf16[256,256]{1,0:T(8,128)(2,1)S(1)}, bf16[256,256]{1,0:T(8,128)(2,1)S(1)}, u32[]{:S(2)}, u32[]{:S(2)}) %collective-permute-start.8) | collective-permute-done | bytes 131104 | tf_op jit(solution)/shard_map/ppermute | solution.py:629
  24.2 0.9 %shard_map.87 = (bf16[128,1024]{1,0:T(8,128)(2,1)S(1)}, bf16[352,1024]{1,0:T(8,128)(2,1)S(1)}, bf16[4,256,256]{2,1,0:T(8,128)(2,1)S(1)}, bf16[4,256,256]{2,1,0:T(8,128)(2,1)S(1)}) custom-call(bf16[864,256]{1,0:T(8,128)(2,1)S(1)} %bitcast.13, bf16[256,256]{1,0:T(8,128)(2,1)S(1)} %shard_map.85.r_1_, bf16[256,256]{1,0:T(8,128)(2,1)S(1)} %collective-permute-done.3.r_2_, ...), custom_call_target="tpu_custom_call" | custom-call | flops 452984832 | bytes 3522560 | tf_op jit(solution)/shard_map/pallas_call | solution.py:486
  25.1 0.5 %collective-permute-start.10 = (bf16[128,1024]{1,0:T(8,128)(2,1)S(1)}, bf16[128,1024]{1,0:T(8,128)(2,1)S(1)}, u32[]{:S(2)}, u32[]{:S(2)}) collective-permute-start(bf16[128,1024]{1,0:T(8,128)(2,1)S(1)} %get-tuple-element.7.r_1_), channel_id=1, source_target_pairs={{0,2},{1,3},{2,0},{3,1},{4,6},{5,7},{6,4},{7,5},{8,10},{9,11},{10,... | collective-permute-start | bytes 786440 | tf_op jit(solution)/shard_map/ppermute | solution.py:724
  25.6 2.5 %collective-permute-start.11 = (bf16[128,1024]{1,0:T(8,128)(2,1)S(1)}, bf16[128,1024]{1,0:T(8,128)(2,1)S(1)}, u32[]{:S(2)}, u32[]{:S(2)}) collective-permute-start(bf16[128,1024]{1,0:T(8,128)(2,1)S(1)} %get-tuple-element.7.r_1_), channel_id=1, source_target_pairs={{0,3},{1,2},{2,1},{3,0},{4,7},{5,6},{6,5},{7,4},{8,11},{9,10},{10,... | collective-permute-start | bytes 786440 | tf_op jit(solution)/shard_map/ppermute | solution.py:724
  28.1 2.3 %shard_map.89.r_0_ = bf16[224,128]{1,0:T(8,128)(2,1)S(1)} custom-call(bf16[352,1024]{1,0:T(8,128)(2,1)S(1)} %get-tuple-element.8.r_0_, bf16[32,2,1024]{2,1,0:T(2,128)(2,1)S(1)} %collective-permute-done.12.r_1_, bf16[32,2,1024]{2,1,0:T(2,128)(2,1)S(1)} %collective-permute-done.13.r_2_, bf16[32,2,1024]{2,1,0:T(2,128)(2,1)S(1)} %collective-permute-done.14.r_3_, ...), custom_call_target="tpu_custom_call" | custom-call | flops 905969664 | bytes 1302528 | tf_op jit(solution)/shard_map/pallas_call | solution.py:486
  30.4 0.6 %collective-permute-start.16 = (bf16[224,128]{1,0:T(8,128)(2,1)S(1)}, bf16[224,128]{1,0:T(8,128)(2,1)S(1)}, u32[]{:S(2)}, u32[]{:S(2)}) collective-permute-start(bf16[224,128]{1,0:T(8,128)(2,1)S(1)} %shard_map.89.r_0_), channel_id=1, source_target_pairs={{0,1},{1,0},{2,3},{3,2},{4,5},{5,4},{6,7},{7,6},{8,9},{9,8},{10,11... | collective-permute-start | bytes 172040 | tf_op jit(solution)/shard_map/ppermute | solution.py:692
  30.9 0.9 %collective-permute-done.16.r_1_ = bf16[224,128]{1,0:T(8,128)(2,1)S(1)} collective-permute-done((bf16[224,128]{1,0:T(8,128)(2,1)S(1)}, bf16[224,128]{1,0:T(8,128)(2,1)S(1)}, u32[]{:S(2)}, u32[]{:S(2)}) %collective-permute-start.16) | collective-permute-done | bytes 57376 | tf_op jit(solution)/shard_map/ppermute | solution.py:692
  31.8 4.7 %collective-permute-start.17 = (bf16[448,128]{1,0:T(8,128)(2,1)S(1)}, bf16[448,128]{1,0:T(8,128)(2,1)S(1)}, u32[]{:S(2)}, u32[]{:S(2)}) collective-permute-start(bf16[448,128]{1,0:T(8,128)(2,1)S(1)} %shard_map.90), channel_id=1, source_target_pairs={{0,0},{1,4},{2,8},{3,12},{4,2},{5,6},{6,10},{7,14},{8,1},{9,5},{10... | collective-permute-start | bytes 344072 | tf_op jit(solution)/shard_map/ppermute | solution.py:708
  36.7 1.4 %shard_map.92 = f32[3,288,256]{2,1,0:T(8,128)} custom-call(bf16[4,256,256]{2,1,0:T(8,128)(2,1)S(1)} %get-tuple-element.9.r_0_, bf16[4,256,256]{2,1,0:T(8,128)(2,1)S(1)} %get-tuple-element.10.r_1_), custom_call_target="tpu_custom_call" | custom-call | flops 452984832 | bytes 1933312 | tf_op jit(solution)/shard_map/pallas_call | solution.py:486
  38.1 3.2 %collective-permute-done.11.r_4_ = bf16[128,1024]{1,0:T(8,128)(2,1)S(1)} collective-permute-done((bf16[128,1024]{1,0:T(8,128)(2,1)S(1)}, bf16[128,1024]{1,0:T(8,128)(2,1)S(1)}, u32[]{:S(2)}, u32[]{:S(2)}) %collective-permute-start.11) | collective-permute-done | bytes 262176 | tf_op jit(solution)/shard_map/ppermute | solution.py:724
  41.4 2.0 %shard_map.88 = bf16[32,2,1024]{2,1,0:T(2,128)(2,1)} custom-call(bf16[864,128]{1,0:T(8,128)(2,1)S(1)} %bitcast.14, bf16[128,1024]{1,0:T(8,128)(2,1)S(1)} %get-tuple-element.7.r_1_, bf16[128,1024]{1,0:T(8,128)(2,1)S(1)} %collective-permute-done.9.r_2_, bf16[128,1024]{1,0:T(8,128)(2,1)S(1)} %collective-permute-done.10.r_3_, ...), custom_call_target="tpu_custom_call" | custom-call | flops 452984832 | bytes 1400832 | tf_op jit(solution)/shard_map/pallas_call | solution.py:486
  43.4 1.1 %shard_map.91 = f32[3,288,128]{2,1,0:T(8,128)} custom-call(bf16[512,512]{1,0:T(8,128)(2,1)S(1)} %copy-done, bf16[448,128]{1,0:T(8,128)(2,1)S(1)} %collective-permute-done.17.r_1_, bf16[448,128]{1,0:T(8,128)(2,1)S(1)} %collective-permute-done.18.r_2_), custom_call_target="tpu_custom_call" | custom-call | flops 117440512 | bytes 1196032 | tf_op jit(solution)/shard_map/pallas_call | solution.py:486
  (32 shorter events, 0.8 us)
Async XLA Ops:
  0.6 16.2 %collective-permute-start.12 = (bf16[32,2,1024]{2,1,0:T(2,128)(2,1)}, bf16[32,2,1024]{2,1,0:T(2,128)(2,1)S(1)}, u32[]{:S(2)}, u32[]{:S(2)}) collective-permute-start(bf16[32,2,1024]{2,1,0:T(2,128)(2,1)} %bitcast.17), channel_id=1, source_target_pairs={{0,0},{8,1},{4,2},{12,3},{2,4},{10,5},{6,6},{14,7},{1,8},{9,9},{5,... | collective-permute-start | bytes 393224 | tf_op jit(solution)/shard_map/ppermute | solution.py:657
  6.4 5.0 %collective-permute-start = (bf16[64,256]{1,0:T(8,128)(2,1)}, bf16[64,256]{1,0:T(8,128)(2,1)S(1)}, u32[]{:S(2)}, u32[]{:S(2)}) collective-permute-start(bf16[64,256]{1,0:T(8,128)(2,1)} %bitcast.9), channel_id=1, source_target_pairs={{0,4},{4,0},{8,12},{12,8},{1,5},{5,1},{9,13},{13,9},{2,6},{6,2},{1... | collective-permute-start | bytes 98312 | tf_op jit(solution)/shard_map/ppermute | solution.py:635
  6.8 5.5 %collective-permute-start.1 = (bf16[64,256]{1,0:T(8,128)(2,1)}, bf16[64,256]{1,0:T(8,128)(2,1)S(1)}, u32[]{:S(2)}, u32[]{:S(2)}) collective-permute-start(bf16[64,256]{1,0:T(8,128)(2,1)} %bitcast.10), channel_id=1, source_target_pairs={{0,8},{4,12},{8,0},{12,4},{1,9},{5,13},{9,1},{13,5},{2,10},{6,14},... | collective-permute-start | bytes 98312 | tf_op jit(solution)/shard_map/ppermute | solution.py:635
  6.8 5.5 %collective-permute-start.2 = (bf16[64,256]{1,0:T(8,128)(2,1)}, bf16[64,256]{1,0:T(8,128)(2,1)S(1)}, u32[]{:S(2)}, u32[]{:S(2)}) collective-permute-start(bf16[64,256]{1,0:T(8,128)(2,1)} %bitcast.11), channel_id=1, source_target_pairs={{0,12},{4,8},{8,4},{12,0},{1,13},{5,9},{9,5},{13,1},{2,14},{6,10},... | collective-permute-start | bytes 98312 | tf_op jit(solution)/shard_map/ppermute | solution.py:635
  10.0 0.9 %copy-start.1 = (bf16[1,32,2,1024]{3,2,1,0:T(2,128)(2,1)S(1)}, bf16[1,32,2,1024]{3,2,1,0:T(2,128)(2,1)}, u32[]{:S(2)}) copy-start(bf16[1,32,2,1024]{3,2,1,0:T(2,128)(2,1)} %param.7) | copy-start | bytes 393220
  10.9 1.4 %copy-start.2 = (bf16[1,64,1,256]{3,1,2,0:T(8,128)(2,1)S(1)}, bf16[1,64,1,256]{3,1,2,0:T(8,128)(2,1)}, u32[]{:S(2)}) copy-start(bf16[1,64,1,256]{3,1,2,0:T(8,128)(2,1)} %param.8) | copy-start | bytes 98308
  10.9 13.2 %copy-start.3 = (bf16[3,3,3,32,256]{4,3,2,1,0:T(8,128)(2,1)S(1)}, bf16[3,3,3,32,256]{4,3,2,1,0:T(8,128)(2,1)}, u32[]{:S(2)}) copy-start(bf16[3,3,3,32,256]{4,3,2,1,0:T(8,128)(2,1)} %param.10) | copy-start | bytes 1327108
  11.3 8.1 %collective-permute-start.7 = (bf16[256,256]{1,0:T(8,128)(2,1)S(1)}, bf16[256,256]{1,0:T(8,128)(2,1)S(1)}, u32[]{:S(2)}, u32[]{:S(2)}) collective-permute-start(bf16[256,256]{1,0:T(8,128)(2,1)S(1)} %shard_map.86.r_5_), channel_id=1, source_target_pairs={{0,8},{4,12},{8,0},{12,4},{1,9},{5,13},{9,1},{13,5},{2,10},{6,14},... | collective-permute-start | bytes 393224 | tf_op jit(solution)/shard_map/ppermute | solution.py:629
  12.3 7.1 %collective-permute-start.4 = (bf16[256,256]{1,0:T(8,128)(2,1)S(1)}, bf16[256,256]{1,0:T(8,128)(2,1)S(1)}, u32[]{:S(2)}, u32[]{:S(2)}) collective-permute-start(bf16[256,256]{1,0:T(8,128)(2,1)S(1)} %shard_map.85.r_1_), channel_id=1, source_target_pairs={{0,2},{1,3},{2,0},{3,1},{4,6},{5,7},{6,4},{7,5},{8,10},{9,11},{10,... | collective-permute-start | bytes 393224 | tf_op jit(solution)/shard_map/ppermute | solution.py:629
  13.2 9.0 %collective-permute-start.6 = (bf16[256,256]{1,0:T(8,128)(2,1)S(1)}, bf16[256,256]{1,0:T(8,128)(2,1)S(1)}, u32[]{:S(2)}, u32[]{:S(2)}) collective-permute-start(bf16[256,256]{1,0:T(8,128)(2,1)S(1)} %shard_map.86.r_5_), channel_id=1, source_target_pairs={{0,4},{4,0},{8,12},{12,8},{1,5},{5,1},{9,13},{13,9},{2,6},{6,2},{1... | collective-permute-start | bytes 393224 | tf_op jit(solution)/shard_map/ppermute | solution.py:629
  16.8 5.8 %collective-permute-start.14 = (bf16[32,2,1024]{2,1,0:T(2,128)(2,1)S(1)}, bf16[32,2,1024]{2,1,0:T(2,128)(2,1)S(1)}, u32[]{:S(2)}, u32[]{:S(2)}) collective-permute-start(bf16[32,2,1024]{2,1,0:T(2,128)(2,1)S(1)} %collective-permute-done.12.r_1_), channel_id=1, source_target_pairs={{0,2},{1,3},{2,0},{3,1},{4,6},{5,7},{6,4},{7,5},{8,10},{9,11},{10,... | collective-permute-start | bytes 393224 | tf_op jit(solution)/shard_map/ppermute | solution.py:629
  17.7 5.0 %collective-permute-start.3 = (bf16[256,256]{1,0:T(8,128)(2,1)S(1)}, bf16[256,256]{1,0:T(8,128)(2,1)S(1)}, u32[]{:S(2)}, u32[]{:S(2)}) collective-permute-start(bf16[256,256]{1,0:T(8,128)(2,1)S(1)} %shard_map.85.r_1_), channel_id=1, source_target_pairs={{0,1},{1,0},{2,3},{3,2},{4,5},{5,4},{6,7},{7,6},{8,9},{9,8},{10,11... | collective-permute-start | bytes 393224 | tf_op jit(solution)/shard_map/ppermute | solution.py:629
  19.4 4.7 %collective-permute-start.8 = (bf16[256,256]{1,0:T(8,128)(2,1)S(1)}, bf16[256,256]{1,0:T(8,128)(2,1)S(1)}, u32[]{:S(2)}, u32[]{:S(2)}) collective-permute-start(bf16[256,256]{1,0:T(8,128)(2,1)S(1)} %collective-permute-done.7.r_7_), channel_id=1, source_target_pairs={{0,4},{4,0},{8,12},{12,8},{1,5},{5,1},{9,13},{13,9},{2,6},{6,2},{1... | collective-permute-start | bytes 393224 | tf_op jit(solution)/shard_map/ppermute | solution.py:629
  19.4 4.7 %collective-permute-start.5 = (bf16[256,256]{1,0:T(8,128)(2,1)S(1)}, bf16[256,256]{1,0:T(8,128)(2,1)S(1)}, u32[]{:S(2)}, u32[]{:S(2)}) collective-permute-start(bf16[256,256]{1,0:T(8,128)(2,1)S(1)} %collective-permute-done.4.r_3_), channel_id=1, source_target_pairs={{0,1},{1,0},{2,3},{3,2},{4,5},{5,4},{6,7},{7,6},{8,9},{9,8},{10,11... | collective-permute-start | bytes 393224 | tf_op jit(solution)/shard_map/ppermute | solution.py:629
  22.2 5.9 %collective-permute-start.13 = (bf16[32,2,1024]{2,1,0:T(2,128)(2,1)S(1)}, bf16[32,2,1024]{2,1,0:T(2,128)(2,1)S(1)}, u32[]{:S(2)}, u32[]{:S(2)}) collective-permute-start(bf16[32,2,1024]{2,1,0:T(2,128)(2,1)S(1)} %collective-permute-done.12.r_1_), channel_id=1, source_target_pairs={{0,1},{1,0},{2,3},{3,2},{4,5},{5,4},{6,7},{7,6},{8,9},{9,8},{10,11... | collective-permute-start | bytes 393224 | tf_op jit(solution)/shard_map/ppermute | solution.py:629
  22.6 5.5 %collective-permute-start.15 = (bf16[32,2,1024]{2,1,0:T(2,128)(2,1)S(1)}, bf16[32,2,1024]{2,1,0:T(2,128)(2,1)S(1)}, u32[]{:S(2)}, u32[]{:S(2)}) collective-permute-start(bf16[32,2,1024]{2,1,0:T(2,128)(2,1)S(1)} %collective-permute-done.14.r_3_), channel_id=1, source_target_pairs={{0,1},{1,0},{2,3},{3,2},{4,5},{5,4},{6,7},{7,6},{8,9},{9,8},{10,11... | collective-permute-start | bytes 393224 | tf_op jit(solution)/shard_map/ppermute | solution.py:629
  25.1 13.1 %collective-permute-start.10 = (bf16[128,1024]{1,0:T(8,128)(2,1)S(1)}, bf16[128,1024]{1,0:T(8,128)(2,1)S(1)}, u32[]{:S(2)}, u32[]{:S(2)}) collective-permute-start(bf16[128,1024]{1,0:T(8,128)(2,1)S(1)} %get-tuple-element.7.r_1_), channel_id=1, source_target_pairs={{0,2},{1,3},{2,0},{3,1},{4,6},{5,7},{6,4},{7,5},{8,10},{9,11},{10,... | collective-permute-start | bytes 786440 | tf_op jit(solution)/shard_map/ppermute | solution.py:724
  25.6 15.8 %collective-permute-start.11 = (bf16[128,1024]{1,0:T(8,128)(2,1)S(1)}, bf16[128,1024]{1,0:T(8,128)(2,1)S(1)}, u32[]{:S(2)}, u32[]{:S(2)}) collective-permute-start(bf16[128,1024]{1,0:T(8,128)(2,1)S(1)} %get-tuple-element.7.r_1_), channel_id=1, source_target_pairs={{0,3},{1,2},{2,1},{3,0},{4,7},{5,6},{6,5},{7,4},{8,11},{9,10},{10,... | collective-permute-start | bytes 786440 | tf_op jit(solution)/shard_map/ppermute | solution.py:724
  28.1 13.3 %collective-permute-start.9 = (bf16[128,1024]{1,0:T(8,128)(2,1)S(1)}, bf16[128,1024]{1,0:T(8,128)(2,1)S(1)}, u32[]{:S(2)}, u32[]{:S(2)}) collective-permute-start(bf16[128,1024]{1,0:T(8,128)(2,1)S(1)} %get-tuple-element.7.r_1_), channel_id=1, source_target_pairs={{0,1},{1,0},{2,3},{3,2},{4,5},{5,4},{6,7},{7,6},{8,9},{9,8},{10,11... | collective-permute-start | bytes 786440 | tf_op jit(solution)/shard_map/ppermute | solution.py:724
  30.4 1.5 %collective-permute-start.16 = (bf16[224,128]{1,0:T(8,128)(2,1)S(1)}, bf16[224,128]{1,0:T(8,128)(2,1)S(1)}, u32[]{:S(2)}, u32[]{:S(2)}) collective-permute-start(bf16[224,128]{1,0:T(8,128)(2,1)S(1)} %shard_map.89.r_0_), channel_id=1, source_target_pairs={{0,1},{1,0},{2,3},{3,2},{4,5},{5,4},{6,7},{7,6},{8,9},{9,8},{10,11... | collective-permute-start | bytes 172040 | tf_op jit(solution)/shard_map/ppermute | solution.py:692
  31.8 11.6 %collective-permute-start.17 = (bf16[448,128]{1,0:T(8,128)(2,1)S(1)}, bf16[448,128]{1,0:T(8,128)(2,1)S(1)}, u32[]{:S(2)}, u32[]{:S(2)}) collective-permute-start(bf16[448,128]{1,0:T(8,128)(2,1)S(1)} %shard_map.90), channel_id=1, source_target_pairs={{0,0},{1,4},{2,8},{3,12},{4,2},{5,6},{6,10},{7,14},{8,1},{9,5},{10... | collective-permute-start | bytes 344072 | tf_op jit(solution)/shard_map/ppermute | solution.py:708
  36.6 6.8 %collective-permute-start.18 = (bf16[448,128]{1,0:T(8,128)(2,1)S(1)}, bf16[448,128]{1,0:T(8,128)(2,1)S(1)}, u32[]{:S(2)}, u32[]{:S(2)}) collective-permute-start(bf16[448,128]{1,0:T(8,128)(2,1)S(1)} %shard_map.90), channel_id=1, source_target_pairs={{0,8},{1,12},{2,0},{3,4},{4,10},{5,14},{6,2},{7,6},{8,9},{9,13},{1... | collective-permute-start | bytes 344072 | tf_op jit(solution)/shard_map/ppermute | solution.py:708
  36.7 4.7 %copy-start.4 = (bf16[3,3,3,32,128]{4,3,2,1,0:T(8,128)(2,1)S(1)}, bf16[3,3,3,32,128]{4,3,2,1,0:T(8,128)(2,1)}, u32[]{:S(2)}) copy-start(bf16[3,3,3,32,128]{4,3,2,1,0:T(8,128)(2,1)} %param.9) | copy-start | bytes 663556
  41.4 2.1 %copy-start = (bf16[512,512]{1,0:T(8,128)(2,1)S(1)}, bf16[512,512]{1,0:T(8,128)(2,1)}, u32[]{:S(2)}) copy-start(bf16[512,512]{1,0:T(8,128)(2,1)} %constant.2.clone.r_0_) | copy-start | bytes 1572868

commit v7 on v5

--- a/solution.py
+++ b/solution.py
@@ -469,7 +469,7 @@
         in_specs=[pl.BlockSpec(memory_space=pltpu.VMEM)] * len(operands),
         out_specs=jax.tree.map(lambda _: pl.BlockSpec(memory_space=pltpu.VMEM), out_shape),
         scratch_shapes=scratch,
-        cost_estimate=pl.CostEstimate(flops=flops, bytes_accessed=total, transcendentals=0),
+        cost_estimate=pl.CostEstimate(flops=flops, bytes_accessed=4 * total, transcendentals=0),
         compiler_params=pltpu.CompilerParams(vmem_limit_bytes=50 * 1024 * 1024),
     )(*operands)
 
@@ -632,7 +632,8 @@
     scale_two = 1.0 / math.sqrt(samples * out_grad.shape[2] * count * width)
 
     near = out_grad.reshape(-1, width)
-    around = [near] + [paired(near, step) for step in range(1, count)]
+    far = {step: paired(near, step) for step in reversed(range(1, count))}
+    around = [near] + [far[step] for step in range(1, count)]
     turn = [(mixed(j, count) * count + mixed(a, count), a * count + j) for a in range(count) for j in range(count)]
     x_turned = lax.ppermute(inputs.reshape(chans, planes, cells), both, turn)
     packed = local_call(pack_kernel, shape((count * near.shape[0], width), BF16), [], 0, *around)

time: 45 us -> 45 us (level)
  no operation moved by 1% of the time
where the time goes in v7:
time: 45 us; the launch traced here: 44.5 us
  starting transfers between devices  24.2 us (54%)
  waiting for transfers between devices  10.3 us (23%)
  Pallas kernels  8.28 us (18%)
  local copies, waits for them, and re-layouts  0.92 us (2%)
  between operations  0.72 us (2%)
    pallas_call x8, Pallas kernels, local_call(): pl.pallas_call(kernel, out_shape=out_shape, in_specs=[pl.BlockSpec(memory...  8.28 us
    ppermute x9, starting transfers between devices, spread(): lax.ppermute(item, axis, pairs)  6.45 us
    ppermute x1, starting transfers between devices, square_shards(): x_turned = lax.ppermute(inputs.reshape(chans, planes, cells), both, turn)  5.76 us
    ppermute x9, waiting for transfers between devices, spread(): lax.ppermute(item, axis, pairs)  5.43 us
    ppermute x2, starting transfers between devices, square_shards(): pieces.append(lax.ppermute(pair, both, pairs))  4.85 us
    ppermute x3, starting transfers between devices, paired(): lax.ppermute(value, 'space', [(i, i ^ mask) for i in range(lax.axis_size(...  3.61 us
    ppermute x3, waiting for transfers between devices, square_shards(): lax.ppermute(p_local, 'chan', [(i, i ^ mask) for i in range(count)])  3.08 us
    ppermute x3, starting transfers between devices, square_shards(): lax.ppermute(p_local, 'chan', [(i, i ^ mask) for i in range(count)])  2.99 us
  transfers between devices with their start and end apart: 19, of which 6 were waited for; matrix products, arithmetic and copies ran while one was open for 0% of the time, Pallas kernels for 16%

profile of v7, /device:TPU:3, one launch (start us, length us, event | category | flops | bytes accessed | tf_op | source)
XLA Modules:
  0.0 44.5 jit_solution(9487893929869338797)
XLA Ops:
  0.6 5.8 %collective-permute-start.12 = (bf16[32,2,1024]{2,1,0:T(2,128)(2,1)}, bf16[32,2,1024]{2,1,0:T(2,128)(2,1)S(1)}, u32[]{:S(2)}, u32[]{:S(2)}) collective-permute-start(bf16[32,2,1024]{2,1,0:T(2,128)(2,1)} %bitcast.17), channel_id=1, source_target_pairs={{0,0},{8,1},{4,2},{12,3},{2,4},{10,5},{6,6},{14,7},{1,8},{9,9},{5,... | collective-permute-start | bytes 393224 | tf_op jit(solution)/shard_map/ppermute | solution.py:638
  6.8 3.2 %collective-permute-start.2 = (bf16[64,256]{1,0:T(8,128)(2,1)}, bf16[64,256]{1,0:T(8,128)(2,1)S(1)}, u32[]{:S(2)}, u32[]{:S(2)}) collective-permute-start(bf16[64,256]{1,0:T(8,128)(2,1)} %bitcast.11), channel_id=1, source_target_pairs={{0,12},{4,8},{8,4},{12,0},{1,13},{5,9},{9,5},{13,1},{2,14},{6,10},... | collective-permute-start | bytes 98312 | tf_op jit(solution)/shard_map/ppermute | solution.py:615
  10.0 0.9 %copy-done.1 = bf16[1,32,2,1024]{3,2,1,0:T(2,128)(2,1)S(1)} copy-done((bf16[1,32,2,1024]{3,2,1,0:T(2,128)(2,1)S(1)}, bf16[1,32,2,1024]{3,2,1,0:T(2,128)(2,1)}, u32[]{:S(2)}) %copy-start.1) | copy-done | bytes 131096
  10.9 0.4 shard_map.86.r_5_
  11.4 0.9 %collective-permute-done.1.refs_2_ = bf16[64,256]{1,0:T(8,128)(2,1)S(1)} collective-permute-done((bf16[64,256]{1,0:T(8,128)(2,1)}, bf16[64,256]{1,0:T(8,128)(2,1)S(1)}, u32[]{:S(2)}, u32[]{:S(2)}) %collective-permute-start.1) | collective-permute-done | bytes 32800 | tf_op jit(solution)/shard_map/ppermute | solution.py:615
  12.3 0.8 %collective-permute-start.4 = (bf16[256,256]{1,0:T(8,128)(2,1)S(1)}, bf16[256,256]{1,0:T(8,128)(2,1)S(1)}, u32[]{:S(2)}, u32[]{:S(2)}) collective-permute-start(bf16[256,256]{1,0:T(8,128)(2,1)S(1)} %shard_map.85.r_1_), channel_id=1, source_target_pairs={{0,2},{1,3},{2,0},{3,1},{4,6},{5,7},{6,4},{7,5},{8,10},{9,11},{10,... | collective-permute-start | bytes 393224 | tf_op jit(solution)/shard_map/ppermute | solution.py:609
  13.2 3.6 %collective-permute-start.6 = (bf16[256,256]{1,0:T(8,128)(2,1)S(1)}, bf16[256,256]{1,0:T(8,128)(2,1)S(1)}, u32[]{:S(2)}, u32[]{:S(2)}) collective-permute-start(bf16[256,256]{1,0:T(8,128)(2,1)S(1)} %shard_map.86.r_5_), channel_id=1, source_target_pairs={{0,4},{4,0},{8,12},{12,8},{1,5},{5,1},{9,13},{13,9},{2,6},{6,2},{1... | collective-permute-start | bytes 393224 | tf_op jit(solution)/shard_map/ppermute | solution.py:609
  16.8 0.9 %collective-permute-start.14 = (bf16[32,2,1024]{2,1,0:T(2,128)(2,1)S(1)}, bf16[32,2,1024]{2,1,0:T(2,128)(2,1)S(1)}, u32[]{:S(2)}, u32[]{:S(2)}) collective-permute-start(bf16[32,2,1024]{2,1,0:T(2,128)(2,1)S(1)} %collective-permute-done.12.r_1_), channel_id=1, source_target_pairs={{0,2},{1,3},{2,0},{3,1},{4,6},{5,7},{6,4},{7,5},{8,10},{9,11},{10,... | collective-permute-start | bytes 393224 | tf_op jit(solution)/shard_map/ppermute | solution.py:609
  17.7 1.7 %collective-permute-done.7.r_7_ = bf16[256,256]{1,0:T(8,128)(2,1)S(1)} collective-permute-done((bf16[256,256]{1,0:T(8,128)(2,1)S(1)}, bf16[256,256]{1,0:T(8,128)(2,1)S(1)}, u32[]{:S(2)}, u32[]{:S(2)}) %collective-permute-start.7) | collective-permute-done | bytes 131104 | tf_op jit(solution)/shard_map/ppermute | solution.py:609
  19.4 0.5 %collective-permute-start.5 = (bf16[256,256]{1,0:T(8,128)(2,1)S(1)}, bf16[256,256]{1,0:T(8,128)(2,1)S(1)}, u32[]{:S(2)}, u32[]{:S(2)}) collective-permute-start(bf16[256,256]{1,0:T(8,128)(2,1)S(1)} %collective-permute-done.4.r_3_), channel_id=1, source_target_pairs={{0,1},{1,0},{2,3},{3,2},{4,5},{5,4},{6,7},{7,6},{8,9},{9,8},{10,11... | collective-permute-start | bytes 393224 | tf_op jit(solution)/shard_map/ppermute | solution.py:609
  19.9 2.3 %collective-permute-done.6.r_6_ = bf16[256,256]{1,0:T(8,128)(2,1)S(1)} collective-permute-done((bf16[256,256]{1,0:T(8,128)(2,1)S(1)}, bf16[256,256]{1,0:T(8,128)(2,1)S(1)}, u32[]{:S(2)}, u32[]{:S(2)}) %collective-permute-start.6) | collective-permute-done | bytes 131104 | tf_op jit(solution)/shard_map/ppermute | solution.py:609
  22.2 0.4 collective-permute-start.13
  22.7 1.4 %collective-permute-done.8.r_8_ = bf16[256,256]{1,0:T(8,128)(2,1)S(1)} collective-permute-done((bf16[256,256]{1,0:T(8,128)(2,1)S(1)}, bf16[256,256]{1,0:T(8,128)(2,1)S(1)}, u32[]{:S(2)}, u32[]{:S(2)}) %collective-permute-start.8) | collective-permute-done | bytes 131104 | tf_op jit(solution)/shard_map/ppermute | solution.py:609
  24.2 0.9 %shard_map.87 = (bf16[128,1024]{1,0:T(8,128)(2,1)S(1)}, bf16[352,1024]{1,0:T(8,128)(2,1)S(1)}, bf16[4,256,256]{2,1,0:T(8,128)(2,1)S(1)}, bf16[4,256,256]{2,1,0:T(8,128)(2,1)S(1)}) custom-call(bf16[864,256]{1,0:T(8,128)(2,1)S(1)} %bitcast.13, bf16[256,256]{1,0:T(8,128)(2,1)S(1)} %shard_map.85.r_1_, bf16[256,256]{1,0:T(8,128)(2,1)S(1)} %collective-permute-done.3.r_2_, ...), custom_call_target="tpu_custom_call" | custom-call | flops 452984832 | bytes 14090240 | tf_op jit(solution)/shard_map/pallas_call | solution.py:466
  25.1 0.5 %collective-permute-start.10 = (bf16[128,1024]{1,0:T(8,128)(2,1)S(1)}, bf16[128,1024]{1,0:T(8,128)(2,1)S(1)}, u32[]{:S(2)}, u32[]{:S(2)}) collective-permute-start(bf16[128,1024]{1,0:T(8,128)(2,1)S(1)} %get-tuple-element.7.r_1_), channel_id=1, source_target_pairs={{0,2},{1,3},{2,0},{3,1},{4,6},{5,7},{6,4},{7,5},{8,10},{9,11},{10,... | collective-permute-start | bytes 786440 | tf_op jit(solution)/shard_map/ppermute | solution.py:702
  25.6 2.5 %collective-permute-start.11 = (bf16[128,1024]{1,0:T(8,128)(2,1)S(1)}, bf16[128,1024]{1,0:T(8,128)(2,1)S(1)}, u32[]{:S(2)}, u32[]{:S(2)}) collective-permute-start(bf16[128,1024]{1,0:T(8,128)(2,1)S(1)} %get-tuple-element.7.r_1_), channel_id=1, source_target_pairs={{0,3},{1,2},{2,1},{3,0},{4,7},{5,6},{6,5},{7,4},{8,11},{9,10},{10,... | collective-permute-start | bytes 786440 | tf_op jit(solution)/shard_map/ppermute | solution.py:702
  28.1 2.3 %shard_map.89.r_0_ = bf16[224,128]{1,0:T(8,128)(2,1)S(1)} custom-call(bf16[352,1024]{1,0:T(8,128)(2,1)S(1)} %get-tuple-element.8.r_0_, bf16[32,2,1024]{2,1,0:T(2,128)(2,1)S(1)} %collective-permute-done.12.r_1_, bf16[32,2,1024]{2,1,0:T(2,128)(2,1)S(1)} %collective-permute-done.13.r_2_, bf16[32,2,1024]{2,1,0:T(2,128)(2,1)S(1)} %collective-permute-done.14.r_3_, ...), custom_call_target="tpu_custom_call" | custom-call | flops 905969664 | bytes 5210112 | tf_op jit(solution)/shard_map/pallas_call | solution.py:466
  30.4 0.6 %collective-permute-start.16 = (bf16[224,128]{1,0:T(8,128)(2,1)S(1)}, bf16[224,128]{1,0:T(8,128)(2,1)S(1)}, u32[]{:S(2)}, u32[]{:S(2)}) collective-permute-start(bf16[224,128]{1,0:T(8,128)(2,1)S(1)} %shard_map.89.r_0_), channel_id=1, source_target_pairs={{0,1},{1,0},{2,3},{3,2},{4,5},{5,4},{6,7},{7,6},{8,9},{9,8},{10,11... | collective-permute-start | bytes 172040 | tf_op jit(solution)/shard_map/ppermute | solution.py:673
  30.9 0.9 %collective-permute-done.16.r_1_ = bf16[224,128]{1,0:T(8,128)(2,1)S(1)} collective-permute-done((bf16[224,128]{1,0:T(8,128)(2,1)S(1)}, bf16[224,128]{1,0:T(8,128)(2,1)S(1)}, u32[]{:S(2)}, u32[]{:S(2)}) %collective-permute-start.16) | collective-permute-done | bytes 57376 | tf_op jit(solution)/shard_map/ppermute | solution.py:673
  31.8 4.7 %collective-permute-start.17 = (bf16[448,128]{1,0:T(8,128)(2,1)S(1)}, bf16[448,128]{1,0:T(8,128)(2,1)S(1)}, u32[]{:S(2)}, u32[]{:S(2)}) collective-permute-start(bf16[448,128]{1,0:T(8,128)(2,1)S(1)} %shard_map.90), channel_id=1, source_target_pairs={{0,0},{1,4},{2,8},{3,12},{4,2},{5,6},{6,10},{7,14},{8,1},{9,5},{10... | collective-permute-start | bytes 344072 | tf_op jit(solution)/shard_map/ppermute | solution.py:689
  36.7 1.6 %shard_map.92 = f32[864,256]{1,0:T(8,128)} custom-call(bf16[4,256,256]{2,1,0:T(8,128)(2,1)S(1)} %get-tuple-element.9.r_0_, bf16[4,256,256]{2,1,0:T(8,128)(2,1)S(1)} %get-tuple-element.10.r_1_), custom_call_target="tpu_custom_call" | custom-call | flops 452984832 | bytes 7733248 | tf_op jit(solution)/shard_map/pallas_call | solution.py:466
  38.3 3.1 %collective-permute-done.11.r_4_ = bf16[128,1024]{1,0:T(8,128)(2,1)S(1)} collective-permute-done((bf16[128,1024]{1,0:T(8,128)(2,1)S(1)}, bf16[128,1024]{1,0:T(8,128)(2,1)S(1)}, u32[]{:S(2)}, u32[]{:S(2)}) %collective-permute-start.11) | collective-permute-done | bytes 262176 | tf_op jit(solution)/shard_map/ppermute | solution.py:702
  41.4 2.0 %shard_map.88 = bf16[32,2,1024]{2,1,0:T(2,128)(2,1)} custom-call(bf16[864,128]{1,0:T(8,128)(2,1)S(1)} %bitcast.14, bf16[128,1024]{1,0:T(8,128)(2,1)S(1)} %get-tuple-element.7.r_1_, bf16[128,1024]{1,0:T(8,128)(2,1)S(1)} %collective-permute-done.9.r_2_, bf16[128,1024]{1,0:T(8,128)(2,1)S(1)} %collective-permute-done.10.r_3_, ...), custom_call_target="tpu_custom_call" | custom-call | flops 452984832 | bytes 5603328 | tf_op jit(solution)/shard_map/pallas_call | solution.py:466
  43.4 1.0 %shard_map.91 = f32[864,128]{1,0:T(8,128)} custom-call(bf16[512,512]{1,0:T(8,128)(2,1)S(1)} %copy-done, bf16[448,128]{1,0:T(8,128)(2,1)S(1)} %collective-permute-done.17.r_1_, bf16[448,128]{1,0:T(8,128)(2,1)S(1)} %collective-permute-done.18.r_2_), custom_call_target="tpu_custom_call" | custom-call | flops 117440512 | bytes 4784128 | tf_op jit(solution)/shard_map/pallas_call | solution.py:466
  (32 shorter events, 0.8 us)
Async XLA Ops:
  0.6 16.2 %collective-permute-start.12 = (bf16[32,2,1024]{2,1,0:T(2,128)(2,1)}, bf16[32,2,1024]{2,1,0:T(2,128)(2,1)S(1)}, u32[]{:S(2)}, u32[]{:S(2)}) collective-permute-start(bf16[32,2,1024]{2,1,0:T(2,128)(2,1)} %bitcast.17), channel_id=1, source_target_pairs={{0,0},{8,1},{4,2},{12,3},{2,4},{10,5},{6,6},{14,7},{1,8},{9,9},{5,... | collective-permute-start | bytes 393224 | tf_op jit(solution)/shard_map/ppermute | solution.py:638
  6.4 5.0 %collective-permute-start = (bf16[64,256]{1,0:T(8,128)(2,1)}, bf16[64,256]{1,0:T(8,128)(2,1)S(1)}, u32[]{:S(2)}, u32[]{:S(2)}) collective-permute-start(bf16[64,256]{1,0:T(8,128)(2,1)} %bitcast.9), channel_id=1, source_target_pairs={{0,4},{4,0},{8,12},{12,8},{1,5},{5,1},{9,13},{13,9},{2,6},{6,2},{1... | collective-permute-start | bytes 98312 | tf_op jit(solution)/shard_map/ppermute | solution.py:615
  6.8 5.5 %collective-permute-start.1 = (bf16[64,256]{1,0:T(8,128)(2,1)}, bf16[64,256]{1,0:T(8,128)(2,1)S(1)}, u32[]{:S(2)}, u32[]{:S(2)}) collective-permute-start(bf16[64,256]{1,0:T(8,128)(2,1)} %bitcast.10), channel_id=1, source_target_pairs={{0,8},{4,12},{8,0},{12,4},{1,9},{5,13},{9,1},{13,5},{2,10},{6,14},... | collective-permute-start | bytes 98312 | tf_op jit(solution)/shard_map/ppermute | solution.py:615
  6.8 5.5 %collective-permute-start.2 = (bf16[64,256]{1,0:T(8,128)(2,1)}, bf16[64,256]{1,0:T(8,128)(2,1)S(1)}, u32[]{:S(2)}, u32[]{:S(2)}) collective-permute-start(bf16[64,256]{1,0:T(8,128)(2,1)} %bitcast.11), channel_id=1, source_target_pairs={{0,12},{4,8},{8,4},{12,0},{1,13},{5,9},{9,5},{13,1},{2,14},{6,10},... | collective-permute-start | bytes 98312 | tf_op jit(solution)/shard_map/ppermute | solution.py:615
  10.0 0.9 %copy-start.1 = (bf16[1,32,2,1024]{3,2,1,0:T(2,128)(2,1)S(1)}, bf16[1,32,2,1024]{3,2,1,0:T(2,128)(2,1)}, u32[]{:S(2)}) copy-start(bf16[1,32,2,1024]{3,2,1,0:T(2,128)(2,1)} %param.7) | copy-start | bytes 393220
  10.9 1.4 %copy-start.2 = (bf16[1,64,1,256]{3,1,2,0:T(8,128)(2,1)S(1)}, bf16[1,64,1,256]{3,1,2,0:T(8,128)(2,1)}, u32[]{:S(2)}) copy-start(bf16[1,64,1,256]{3,1,2,0:T(8,128)(2,1)} %param.8) | copy-start | bytes 98308
  10.9 13.2 %copy-start.3 = (bf16[3,3,3,32,256]{4,3,2,1,0:T(8,128)(2,1)S(1)}, bf16[3,3,3,32,256]{4,3,2,1,0:T(8,128)(2,1)}, u32[]{:S(2)}) copy-start(bf16[3,3,3,32,256]{4,3,2,1,0:T(8,128)(2,1)} %param.10) | copy-start | bytes 1327108
  11.3 8.1 %collective-permute-start.7 = (bf16[256,256]{1,0:T(8,128)(2,1)S(1)}, bf16[256,256]{1,0:T(8,128)(2,1)S(1)}, u32[]{:S(2)}, u32[]{:S(2)}) collective-permute-start(bf16[256,256]{1,0:T(8,128)(2,1)S(1)} %shard_map.86.r_5_), channel_id=1, source_target_pairs={{0,8},{4,12},{8,0},{12,4},{1,9},{5,13},{9,1},{13,5},{2,10},{6,14},... | collective-permute-start | bytes 393224 | tf_op jit(solution)/shard_map/ppermute | solution.py:609
  12.3 7.1 %collective-permute-start.4 = (bf16[256,256]{1,0:T(8,128)(2,1)S(1)}, bf16[256,256]{1,0:T(8,128)(2,1)S(1)}, u32[]{:S(2)}, u32[]{:S(2)}) collective-permute-start(bf16[256,256]{1,0:T(8,128)(2,1)S(1)} %shard_map.85.r_1_), channel_id=1, source_target_pairs={{0,2},{1,3},{2,0},{3,1},{4,6},{5,7},{6,4},{7,5},{8,10},{9,11},{10,... | collective-permute-start | bytes 393224 | tf_op jit(solution)/shard_map/ppermute | solution.py:609
  13.2 9.0 %collective-permute-start.6 = (bf16[256,256]{1,0:T(8,128)(2,1)S(1)}, bf16[256,256]{1,0:T(8,128)(2,1)S(1)}, u32[]{:S(2)}, u32[]{:S(2)}) collective-permute-start(bf16[256,256]{1,0:T(8,128)(2,1)S(1)} %shard_map.86.r_5_), channel_id=1, source_target_pairs={{0,4},{4,0},{8,12},{12,8},{1,5},{5,1},{9,13},{13,9},{2,6},{6,2},{1... | collective-permute-start | bytes 393224 | tf_op jit(solution)/shard_map/ppermute | solution.py:609
  16.8 5.8 %collective-permute-start.14 = (bf16[32,2,1024]{2,1,0:T(2,128)(2,1)S(1)}, bf16[32,2,1024]{2,1,0:T(2,128)(2,1)S(1)}, u32[]{:S(2)}, u32[]{:S(2)}) collective-permute-start(bf16[32,2,1024]{2,1,0:T(2,128)(2,1)S(1)} %collective-permute-done.12.r_1_), channel_id=1, source_target_pairs={{0,2},{1,3},{2,0},{3,1},{4,6},{5,7},{6,4},{7,5},{8,10},{9,11},{10,... | collective-permute-start | bytes 393224 | tf_op jit(solution)/shard_map/ppermute | solution.py:609
  17.7 5.0 %collective-permute-start.3 = (bf16[256,256]{1,0:T(8,128)(2,1)S(1)}, bf16[256,256]{1,0:T(8,128)(2,1)S(1)}, u32[]{:S(2)}, u32[]{:S(2)}) collective-permute-start(bf16[256,256]{1,0:T(8,128)(2,1)S(1)} %shard_map.85.r_1_), channel_id=1, source_target_pairs={{0,1},{1,0},{2,3},{3,2},{4,5},{5,4},{6,7},{7,6},{8,9},{9,8},{10,11... | collective-permute-start | bytes 393224 | tf_op jit(solution)/shard_map/ppermute | solution.py:609
  19.4 4.7 %collective-permute-start.8 = (bf16[256,256]{1,0:T(8,128)(2,1)S(1)}, bf16[256,256]{1,0:T(8,128)(2,1)S(1)}, u32[]{:S(2)}, u32[]{:S(2)}) collective-permute-start(bf16[256,256]{1,0:T(8,128)(2,1)S(1)} %collective-permute-done.7.r_7_), channel_id=1, source_target_pairs={{0,4},{4,0},{8,12},{12,8},{1,5},{5,1},{9,13},{13,9},{2,6},{6,2},{1... | collective-permute-start | bytes 393224 | tf_op jit(solution)/shard_map/ppermute | solution.py:609
  19.4 4.7 %collective-permute-start.5 = (bf16[256,256]{1,0:T(8,128)(2,1)S(1)}, bf16[256,256]{1,0:T(8,128)(2,1)S(1)}, u32[]{:S(2)}, u32[]{:S(2)}) collective-permute-start(bf16[256,256]{1,0:T(8,128)(2,1)S(1)} %collective-permute-done.4.r_3_), channel_id=1, source_target_pairs={{0,1},{1,0},{2,3},{3,2},{4,5},{5,4},{6,7},{7,6},{8,9},{9,8},{10,11... | collective-permute-start | bytes 393224 | tf_op jit(solution)/shard_map/ppermute | solution.py:609
  22.2 5.9 %collective-permute-start.13 = (bf16[32,2,1024]{2,1,0:T(2,128)(2,1)S(1)}, bf16[32,2,1024]{2,1,0:T(2,128)(2,1)S(1)}, u32[]{:S(2)}, u32[]{:S(2)}) collective-permute-start(bf16[32,2,1024]{2,1,0:T(2,128)(2,1)S(1)} %collective-permute-done.12.r_1_), channel_id=1, source_target_pairs={{0,1},{1,0},{2,3},{3,2},{4,5},{5,4},{6,7},{7,6},{8,9},{9,8},{10,11... | collective-permute-start | bytes 393224 | tf_op jit(solution)/shard_map/ppermute | solution.py:609
  22.6 5.5 %collective-permute-start.15 = (bf16[32,2,1024]{2,1,0:T(2,128)(2,1)S(1)}, bf16[32,2,1024]{2,1,0:T(2,128)(2,1)S(1)}, u32[]{:S(2)}, u32[]{:S(2)}) collective-permute-start(bf16[32,2,1024]{2,1,0:T(2,128)(2,1)S(1)} %collective-permute-done.14.r_3_), channel_id=1, source_target_pairs={{0,1},{1,0},{2,3},{3,2},{4,5},{5,4},{6,7},{7,6},{8,9},{9,8},{10,11... | collective-permute-start | bytes 393224 | tf_op jit(solution)/shard_map/ppermute | solution.py:609
  25.1 13.2 %collective-permute-start.10 = (bf16[128,1024]{1,0:T(8,128)(2,1)S(1)}, bf16[128,1024]{1,0:T(8,128)(2,1)S(1)}, u32[]{:S(2)}, u32[]{:S(2)}) collective-permute-start(bf16[128,1024]{1,0:T(8,128)(2,1)S(1)} %get-tuple-element.7.r_1_), channel_id=1, source_target_pairs={{0,2},{1,3},{2,0},{3,1},{4,6},{5,7},{6,4},{7,5},{8,10},{9,11},{10,... | collective-permute-start | bytes 786440 | tf_op jit(solution)/shard_map/ppermute | solution.py:702
  25.6 15.8 %collective-permute-start.11 = (bf16[128,1024]{1,0:T(8,128)(2,1)S(1)}, bf16[128,1024]{1,0:T(8,128)(2,1)S(1)}, u32[]{:S(2)}, u32[]{:S(2)}) collective-permute-start(bf16[128,1024]{1,0:T(8,128)(2,1)S(1)} %get-tuple-element.7.r_1_), channel_id=1, source_target_pairs={{0,3},{1,2},{2,1},{3,0},{4,7},{5,6},{6,5},{7,4},{8,11},{9,10},{10,... | collective-permute-start | bytes 786440 | tf_op jit(solution)/shard_map/ppermute | solution.py:702
  28.1 13.3 %collective-permute-start.9 = (bf16[128,1024]{1,0:T(8,128)(2,1)S(1)}, bf16[128,1024]{1,0:T(8,128)(2,1)S(1)}, u32[]{:S(2)}, u32[]{:S(2)}) collective-permute-start(bf16[128,1024]{1,0:T(8,128)(2,1)S(1)} %get-tuple-element.7.r_1_), channel_id=1, source_target_pairs={{0,1},{1,0},{2,3},{3,2},{4,5},{5,4},{6,7},{7,6},{8,9},{9,8},{10,11... | collective-permute-start | bytes 786440 | tf_op jit(solution)/shard_map/ppermute | solution.py:702
  30.4 1.5 %collective-permute-start.16 = (bf16[224,128]{1,0:T(8,128)(2,1)S(1)}, bf16[224,128]{1,0:T(8,128)(2,1)S(1)}, u32[]{:S(2)}, u32[]{:S(2)}) collective-permute-start(bf16[224,128]{1,0:T(8,128)(2,1)S(1)} %shard_map.89.r_0_), channel_id=1, source_target_pairs={{0,1},{1,0},{2,3},{3,2},{4,5},{5,4},{6,7},{7,6},{8,9},{9,8},{10,11... | collective-permute-start | bytes 172040 | tf_op jit(solution)/shard_map/ppermute | solution.py:673
  31.8 11.6 %collective-permute-start.17 = (bf16[448,128]{1,0:T(8,128)(2,1)S(1)}, bf16[448,128]{1,0:T(8,128)(2,1)S(1)}, u32[]{:S(2)}, u32[]{:S(2)}) collective-permute-start(bf16[448,128]{1,0:T(8,128)(2,1)S(1)} %shard_map.90), channel_id=1, source_target_pairs={{0,0},{1,4},{2,8},{3,12},{4,2},{5,6},{6,10},{7,14},{8,1},{9,5},{10... | collective-permute-start | bytes 344072 | tf_op jit(solution)/shard_map/ppermute | solution.py:689
  36.6 6.8 %collective-permute-start.18 = (bf16[448,128]{1,0:T(8,128)(2,1)S(1)}, bf16[448,128]{1,0:T(8,128)(2,1)S(1)}, u32[]{:S(2)}, u32[]{:S(2)}) collective-permute-start(bf16[448,128]{1,0:T(8,128)(2,1)S(1)} %shard_map.90), channel_id=1, source_target_pairs={{0,8},{1,12},{2,0},{3,4},{4,10},{5,14},{6,2},{7,6},{8,9},{9,13},{1... | collective-permute-start | bytes 344072 | tf_op jit(solution)/shard_map/ppermute | solution.py:689
  36.7 4.7 %copy-start.4 = (bf16[3,3,3,32,128]{4,3,2,1,0:T(8,128)(2,1)S(1)}, bf16[3,3,3,32,128]{4,3,2,1,0:T(8,128)(2,1)}, u32[]{:S(2)}) copy-start(bf16[3,3,3,32,128]{4,3,2,1,0:T(8,128)(2,1)} %param.9) | copy-start | bytes 663556
  41.4 2.1 %copy-start = (bf16[512,512]{1,0:T(8,128)(2,1)S(1)}, bf16[512,512]{1,0:T(8,128)(2,1)}, u32[]{:S(2)}) copy-start(bf16[512,512]{1,0:T(8,128)(2,1)} %constant.2.clone.r_0_) | copy-start | bytes 1572868
